TPU v7x, 32 devices: a whole 2x2x4 slice. The times are simulated.
32 devices in a mesh: dp: 4 (over y, x), seq: 8 (over z, core).
Axes of the slice: x: 2, y: 2, z: 4, core: 2. Of those that a mesh axis runs over, the one named last changes fastest.
Arguments:
- query: bfloat16 [4, 6144, 1536], P('dp', 'seq'), may hold values from -6 to 6
- key_states: bfloat16 [4, 6144, 1536], P('dp', 'seq'), may hold values from -6 to 6
- value_states: bfloat16 [4, 6144, 1536], P('dp', 'seq'), may hold values from -6 to 6
- attn_out: bfloat16 [4, 6144, 1536], P('dp', 'seq'), may hold values from -0.59765625 to 0.59765625
- log_norm: float32 [4, 12, 6144], P('dp', None, 'seq'), may hold values from 6 to 7
- out_grad: bfloat16 [4, 6144, 3072], P('dp', 'seq'), may hold values from -24 to 24
- out_weight: bfloat16 [1536, 3072], P('dp'), may hold values from -0.15625 to 0.15625
- tile_lists: int32 [4, 16, 3], P('dp'), may hold values from 0 to 15, as said below
Outputs:
- query_grad: bfloat16 [4, 6144, 1536], P('dp', 'seq')
- key_grad: bfloat16 [4, 6144, 1536], P('dp', 'seq')
- value_grad: bfloat16 [4, 6144, 1536], P('dp', 'seq')
- weight_grad: float32 [1536, 3072], P('dp')
Inputs may be any that keep to these rules, and one draw needn't show every extreme that they name: `tile_lists`: row i of a clip's list names 3 different tiles: tile i itself and tiles j with (i // 2) * 2 - 1 <= j <= (i // 2) * 2 + 2.
All inputs are finite; a program needn't handle non-finite values.
Results may differ from a plain program's by a relative error of at most 0.0095.
Values may be sent and summed in bfloat16 or wider, within the bound.
A program may use at most 256 MiB of HBM per device.

v0:
```python
import functools
import math

import jax
import jax.numpy as jnp
from jax import lax
from jax.experimental import pallas as pl
from jax.experimental.pallas import tpu as pltpu
from jax.sharding import PartitionSpec as P

TILE = 384
HD = 128
VMEM = 56 * 1024 * 1024
NT = (((1,), (1,)), ((), ()))
TN = (((0,), (0,)), ((), ()))


def mm(a, b, dims=(((1,), (0,)), ((), ()))):
    return lax.dot_general(a, b, dims, preferred_element_type=jnp.float32)


def weight_kernel(places, out_ref, grad_ref, part_ref):
    part_ref[0, 0] = mm(out_ref[...], grad_ref[...], TN).astype(part_ref.dtype)


def weight_part(places, rows, grads, send):
    tokens, width = rows.shape
    high = width // 4
    wide = grads.shape[1] // 4

    def out_at(n, p, at):
        swapped = (p % 2) * 2 + p // 2
        return (0, at[0] ^ jnp.where(n == 0, swapped, p))

    def grad_at(n, p, at):
        half = 1 - at[1] if send else at[1]
        return (0, half * 2 + n)

    return pl.pallas_call(
        weight_kernel,
        grid_spec=pltpu.PrefetchScalarGridSpec(
            num_scalar_prefetch=1,
            grid=(2, 4),
            in_specs=[
                pl.BlockSpec((tokens, high), out_at),
                pl.BlockSpec((tokens, wide), grad_at),
            ],
            out_specs=pl.BlockSpec((1, 1, high, wide), lambda n, p, at: (n, p, 0, 0)),
        ),
        out_shape=jax.ShapeDtypeStruct((2, 4, high, wide), jnp.bfloat16),
        compiler_params=pltpu.CompilerParams(vmem_limit_bytes=VMEM),
        cost_estimate=pl.CostEstimate(
            flops=tokens * width * grads.shape[1],
            bytes_accessed=tokens * width * 2 + tokens * grads.shape[1] + width * grads.shape[1],
            transcendentals=0,
        ),
    )(places, rows, grads)


def attend_kernel(scale, halves, chained, places, *refs):
    weights = refs[: 2 if halves else 1]
    refs = refs[len(weights) :]
    (grad_ref, q_ref, o_ref, norm_ref, k_ref, v_ref, kb_ref, vb_ref, ka_ref, va_ref) = refs[:10]
    refs = refs[11:] if chained else refs[10:]
    (dq_ref, dk_ref, dv_ref, low_ref, high_ref) = refs[:5]
    (full, attn_grad, kwin, vwin, kflip, dk, dv) = refs[5:]
    head = pl.program_id(0)
    tokens = q_ref.shape[0]
    tiles = tokens // TILE

    @pl.when(head == 0)
    def _():
        if halves:
            rows = weights[0].shape[0]
            mine = pl.multiple_of(places[1] * rows, rows)
            other = pl.multiple_of((1 - places[1]) * rows, rows)
            full[pl.ds(mine, rows)] = weights[0][...]
            full[pl.ds(other, rows)] = weights[1][...]
            block = full[...]
        else:
            block = weights[0][...]
        got = mm(grad_ref[...], block, NT).astype(jnp.bfloat16)
        for i in range(attn_grad.shape[0]):
            attn_grad[i] = got[:, i * HD : (i + 1) * HD]

    kwin[0] = kb_ref[...]
    vwin[0] = vb_ref[...]
    for t in range(tiles):
        kwin[t + 1] = k_ref[t * TILE : (t + 1) * TILE]
        vwin[t + 1] = v_ref[t * TILE : (t + 1) * TILE]
    kwin[tiles + 1] = ka_ref[...]
    vwin[tiles + 1] = va_ref[...]
    for w in range(tiles + 2):
        kflip[w] = kwin[w].T
    dk[...] = jnp.zeros_like(dk)
    dv[...] = jnp.zeros_like(dv)
    for t in range(tiles):
        rows = slice(t * TILE, (t + 1) * TILE)
        q = q_ref[rows]
        do = attn_grad[head, rows]
        norm = norm_ref[0, :, rows]
        delta = (do.astype(jnp.float32) * o_ref[rows].astype(jnp.float32)).T.sum(0, keepdims=True)
        dq = jnp.zeros((HD, TILE), jnp.float32)
        for n in range(3):
            w = places[2 + t * 3 + n]
            p = jnp.exp(mm(kwin[w], q, NT) * scale - norm)
            ds = (p * (mm(vwin[w], do, NT) - delta)).astype(jnp.bfloat16)
            dv[w] += mm(p.astype(jnp.bfloat16), do)
            dk[w] += mm(ds, q)
            dq += mm(kflip[w], ds)
        dq_ref[rows] = (dq * scale).T.astype(jnp.bfloat16)
    for t in range(tiles):
        rows = slice(t * TILE, (t + 1) * TILE)
        dk_ref[rows] = dk[t + 1]
        dv_ref[rows] = dv[t + 1]
    low_ref[0] = dk[0].astype(jnp.bfloat16)
    low_ref[1] = dv[0].astype(jnp.bfloat16)
    high_ref[0] = dk[tiles + 1].astype(jnp.bfloat16)
    high_ref[1] = dv[tiles + 1].astype(jnp.bfloat16)


def attend(places, step, heads, weights, grads, query, attn_out, norm, keys, values, halos, before):
    tokens, width = query.shape
    tiles = tokens // TILE
    group = heads * HD
    depth = grads.shape[1]

    def at_head(h, at):
        return (0, (at[0] ^ step) * heads + h)

    def column(rows):
        return pl.BlockSpec((rows, HD), at_head)

    whole = [pl.BlockSpec(w.shape, lambda h, at: (0, 0)) for w in (*weights, grads)]
    in_specs = [
        *whole,
        column(tokens),
        column(tokens),
        pl.BlockSpec((1, 1, tokens), lambda h, at: ((at[0] ^ step) * heads + h, 0, 0)),
        column(tokens),
        column(tokens),
        *[column(TILE)] * 4,
    ]
    operands = [*weights, grads, query, attn_out, norm, keys, values, *halos]
    chained = before is not None
    if chained:
        in_specs.append(pl.BlockSpec(memory_space=pl.ANY))
        operands.append(before)
    rim = pl.BlockSpec((2, TILE, HD), lambda h, at: (0, 0, h))
    local = pl.BlockSpec((tokens, HD), lambda h, at: (0, h))
    kept = 3
    return pl.pallas_call(
        functools.partial(attend_kernel, 1.0 / math.sqrt(HD), len(weights) == 2, chained),
        grid_spec=pltpu.PrefetchScalarGridSpec(
            num_scalar_prefetch=1,
            grid=(heads,),
            in_specs=in_specs,
            out_specs=[column(tokens), local, local, rim, rim],
            scratch_shapes=[
                pltpu.VMEM((group, depth), jnp.bfloat16),
                pltpu.VMEM((heads, tokens, HD), jnp.bfloat16),
                pltpu.VMEM((tiles + 2, TILE, HD), jnp.bfloat16),
                pltpu.VMEM((tiles + 2, TILE, HD), jnp.bfloat16),
                pltpu.VMEM((tiles + 2, HD, TILE), jnp.bfloat16),
                pltpu.VMEM((tiles + 2, TILE, HD), jnp.float32),
                pltpu.VMEM((tiles + 2, TILE, HD), jnp.float32),
            ],
        ),
        out_shape=[
            jax.ShapeDtypeStruct((tokens, width), jnp.bfloat16),
            jax.ShapeDtypeStruct((tokens, group), jnp.float32),
            jax.ShapeDtypeStruct((tokens, group), jnp.float32),
            jax.ShapeDtypeStruct((2, TILE, group), jnp.bfloat16),
            jax.ShapeDtypeStruct((2, TILE, group), jnp.bfloat16),
        ],
        input_output_aliases={len(operands): 0} if chained else {},
        compiler_params=pltpu.CompilerParams(vmem_limit_bytes=VMEM),
        cost_estimate=pl.CostEstimate(
            flops=2 * tokens * depth * group + 20 * tokens * kept * TILE * group,
            bytes_accessed=2 * tokens * depth + 2 * depth * group + 24 * tokens * group,
            transcendentals=heads * tokens * kept * TILE,
        ),
    )(places, *operands)


def finish_kernel(scale, chained, places, dk_ref, dv_ref, below_ref, above_ref, *refs):
    key_ref, value_ref = refs[2:] if chained else refs
    tokens = dk_ref.shape[0]
    tiles = tokens // TILE
    for t in range(tiles):
        rows = slice(t * TILE, (t + 1) * TILE)
        key, value = dk_ref[rows], dv_ref[rows]
        if t == 0:
            key = key + below_ref[0].astype(jnp.float32)
            value = value + below_ref[1].astype(jnp.float32)
        if t == tiles - 1:
            key = key + above_ref[0].astype(jnp.float32)
            value = value + above_ref[1].astype(jnp.float32)
        key_ref[rows] = (key * scale).astype(jnp.bfloat16)
        value_ref[rows] = value.astype(jnp.bfloat16)


def finish(places, step, width, dk, dv, below, above, before):
    tokens, group = dk.shape
    chained = before is not None
    parts = group // HD
    local = pl.BlockSpec((tokens, HD), lambda h, at: (0, h))
    rim = pl.BlockSpec((2, TILE, HD), lambda h, at: (0, 0, h))
    placed = pl.BlockSpec((tokens, HD), lambda h, at: (0, (at[0] ^ step) * parts + h))
    in_specs = [local, local, rim, rim]
    operands = [dk, dv, below, above]
    if chained:
        in_specs += [pl.BlockSpec(memory_space=pl.ANY)] * 2
        operands += before
    return pl.pallas_call(
        functools.partial(finish_kernel, 1.0 / math.sqrt(HD), chained),
        grid_spec=pltpu.PrefetchScalarGridSpec(
            num_scalar_prefetch=1, grid=(parts,), in_specs=in_specs, out_specs=[placed, placed]
        ),
        out_shape=[jax.ShapeDtypeStruct((tokens, width), jnp.bfloat16)] * 2,
        input_output_aliases={5: 0, 6: 1} if chained else {},
        compiler_params=pltpu.CompilerParams(vmem_limit_bytes=VMEM),
        cost_estimate=pl.CostEstimate(
            flops=4 * tokens * group, bytes_accessed=16 * tokens * group, transcendentals=0
        ),
    )(places, *operands)


def body(query, key_states, value_states, attn_out, log_norm, out_grad, out_weight, tile_lists):
    dp_size, seq_size = lax.axis_size("dp"), lax.axis_size("seq")
    cube = dp_size == 4 and seq_size == 8
    query, keys, values, rows = query[0], key_states[0], value_states[0], attn_out[0]
    grads = out_grad[0]
    norm = log_norm[0][:, None, :]
    tokens, width = query.shape
    tiles = tokens // TILE
    head_count = norm.shape[0]
    steps = 4
    heads = head_count // steps
    high = width // steps
    dp, seq = lax.axis_index("dp"), lax.axis_index("seq")
    core = seq % 2
    own = lax.dynamic_slice_in_dim(tile_lists[0], seq * tiles, tiles, 0)
    kept = (own - (seq * tiles - 1)).reshape(-1).astype(jnp.int32)
    first = dp if cube else jnp.int32(0)
    places = jnp.concatenate([jnp.stack([first, core]).astype(jnp.int32), kept])

    def swap(value, dp_bit, seq_bit):
        pairs = [
            (a * seq_size + b, (a ^ dp_bit) * seq_size + (b ^ seq_bit))
            for a in range(dp_size)
            for b in range(seq_size)
        ]
        return lax.ppermute(value, ("dp", "seq"), pairs)

    def along(value, by):
        pairs = [(i, i + by) for i in range(seq_size) if 0 <= i + by < seq_size]
        return lax.ppermute(value, "seq", pairs)

    if cube:
        half = lax.dynamic_slice_in_dim(out_weight, core * (high // 2), high // 2, 0)
        by_x, by_y = swap(half, 1, 0), swap(half, 2, 0)
        quarter = high // 4
        by_both = jnp.concatenate([swap(by_x[:quarter], 2, 0), swap(by_y[quarter:], 1, 0)], axis=0)
        blocks = [[out_weight]] + [[b, swap(b, 0, 1)] for b in (by_x, by_y, by_both)]
    else:
        gathered = lax.all_gather(out_weight, "dp", axis=0, tiled=True)
        blocks = [[gathered[i * high : (i + 1) * high]] for i in range(steps)]

    halos = [
        along(keys[tokens - TILE :], 1),
        along(values[tokens - TILE :], 1),
        along(keys[:TILE], -1),
        along(values[:TILE], -1),
    ]

    if cube:
        f32 = jnp.float32
        sent = swap(weight_part(places, rows, grads, True), 0, 1)
        mine = weight_part(places, rows, grads, False)
        total = mine.astype(f32) + sent.astype(f32)
        half = total.astype(jnp.bfloat16)
        over_x = half[0, :2].astype(f32) + swap(half[0, 2:], 1, 0).astype(f32)
        left = over_x[0] + swap(over_x[1].astype(jnp.bfloat16), 2, 0).astype(f32)
        over_y = half[1, :2].astype(f32) + swap(half[1, 2:], 2, 0).astype(f32)
        right = over_y[0] + swap(over_y[1].astype(jnp.bfloat16), 1, 0).astype(f32)
        plane = jnp.concatenate([left, right], axis=1).astype(jnp.bfloat16)

        def cut(value, bit):
            size = value.shape[0] // 2
            mine = lax.dynamic_slice_in_dim(value, bit * size, size, 0)
            other = lax.dynamic_slice_in_dim(value, (1 - bit) * size, size, 0)
            return mine, other

        def join(value, got, bit):
            return jnp.where(
                bit == 0, jnp.concatenate([value, got], 0), jnp.concatenate([got, value], 0)
            )

        low, up = (seq // 2) % 2, seq // 4
        mine, other = cut(plane, low)
        pair = (mine.astype(f32) + swap(other, 0, 2).astype(f32)).astype(jnp.bfloat16)
        mine, other = cut(pair, up)
        line = (mine.astype(f32) + swap(other, 0, 4).astype(f32)).astype(jnp.bfloat16)
        line = join(line, swap(line, 0, 4), up)
        line = join(line, swap(line, 0, 2), low)
        mate = swap(line, 0, 1)
        weight_grad = jnp.where(
            core == 0, jnp.concatenate([line, mate], 1), jnp.concatenate([mate, line], 1)
        ).astype(f32)
    else:
        summed = lax.psum_scatter(
            jnp.einsum("th,td->hd", rows, grads, preferred_element_type=jnp.float32),
            ("dp", "seq"),
            scatter_dimension=0,
            tiled=True,
        )
        weight_grad = lax.all_gather(summed, "seq", axis=0, tiled=True)

    query_grad, done = None, None
    for step in range(steps):
        query_grad, dk, dv, low_rim, high_rim = attend(
            places, step, heads, blocks[step], grads, query, rows, norm, keys, values, halos, query_grad
        )
        below, above = along(high_rim, 1), along(low_rim, -1)
        done = finish(places, step, width, dk, dv, below, above, done)
    return (query_grad[None], done[0][None], done[1][None], weight_grad)


def solution(mesh):
    token = P("dp", "seq", None)
    return jax.shard_map(
        body,
        mesh=mesh,
        in_specs=(token,) * 4
        + (P("dp", None, "seq"), token, P("dp", None), P("dp", None, None)),
        out_specs=(token, token, token, P("dp", None)),
        check_vma=False,
    )
```

profile of v0, /device:TPU:1, one launch (start us, length us, event | category | flops | bytes accessed | tf_op | source)
XLA Modules:
  0.0 264.2 jit_solution(7535553138787766949)
XLA Ops:
  2.1 10.7 %shard_map.120 = bf16[2,4,384,768]{3,2,1,0:T(8,128)(2,1)} custom-call(s32[8]{0:T(128)} %pad_add_fusion.places, bf16[768,1536]{1,0:T(8,128)(2,1)} %bitcast.69, bf16[768,3072]{1,0:T(8,128)(2,1)} %bitcast.59), custom_call_target="tpu_custom_call" | custom-call | flops 3623878656 | bytes 9437184 | tf_op jit(solution)/shard_map/pallas_call | solution.py:39
  12.9 10.7 %shard_map.119 = bf16[2,4,384,768]{3,2,1,0:T(8,128)(2,1)} custom-call(s32[8]{0:T(128)} %pad_add_fusion.places, bf16[768,1536]{1,0:T(8,128)(2,1)} %bitcast.70, bf16[768,3072]{1,0:T(8,128)(2,1)} %bitcast.60), custom_call_target="tpu_custom_call" | custom-call | flops 3623878656 | bytes 9437184 | tf_op jit(solution)/shard_map/pallas_call | solution.py:39
  23.6 3.6 %add_convert_fusion = bf16[2,4,384,768]{3,2,1,0:T(8,128)(2,1)S(1)} fusion(bf16[2,4,384,768]{3,2,1,0:T(8,128)(2,1)S(1)} %collective-permute-done.19, bf16[2,4,384,768]{3,2,1,0:T(8,128)(2,1)} %shard_map.119), kind=kLoop, calls=%fused_computation | loop fusion | flops 9437184 | bytes 14155776 | tf_op jit(solution)/shard_map/convert_element_type | solution.py:282
  27.4 2.0 copy-done.2
  29.4 2.7 %collective-permute-start.22 = (bf16[2,384,768]{2,1,0:T(8,128)(2,1)S(1)}, bf16[2,384,768]{2,1,0:T(8,128)(2,1)S(1)}, u32[]{:S(2)}, u32[]{:S(2)}) collective-permute-start(bf16[2,384,768]{2,1,0:T(8,128)(2,1)S(1)} %get-tuple-element.62), channel_id=1, source_target_pairs={{0,16},{1,17},{2,18},{3,19},{4,20},{5,21},{6,22},{7,23},{8,24},{9,... | collective-permute-start | bytes 3538952 | tf_op jit(solution)/shard_map/ppermute | solution.py:254
  32.1 1.2 collective-permute-start.20
  33.3 1.5 constant_dynamic-slice_fusion.1
  35.3 1.6 slice_bitcast_fusion.7
  36.9 4.4 %collective-permute-start.5 = (bf16[384,1536]{1,0:T(8,128)(2,1)}, bf16[384,1536]{1,0:T(8,128)(2,1)}, u32[]{:S(2)}, u32[]{:S(2)}) collective-permute-start(bf16[384,1536]{1,0:T(8,128)(2,1)} %get-tuple-element.67), channel_id=1, source_target_pairs={{0,1},{1,2},{2,3},{3,4},{4,5},{5,6},{6,7},{8,9},{9,10},{10,11},{11... | collective-permute-start | bytes 3538952 | tf_op jit(solution)/shard_map/ppermute | solution.py:258
  41.3 17.3 %collective-permute-done.22 = bf16[2,384,768]{2,1,0:T(8,128)(2,1)S(1)} collective-permute-done((bf16[2,384,768]{2,1,0:T(8,128)(2,1)S(1)}, bf16[2,384,768]{2,1,0:T(8,128)(2,1)S(1)}, u32[]{:S(2)}, u32[]{:S(2)}) %collective-permute-start.22) | collective-permute-done | bytes 1179680 | tf_op jit(solution)/shard_map/ppermute | solution.py:254
  58.5 0.9 collective-permute-done.20
  59.5 1.9 convert_add_fusion
  61.8 1.3 slice_bitcast_fusion.6
  63.2 4.9 %collective-permute-start.6 = (bf16[384,1536]{1,0:T(8,128)(2,1)}, bf16[384,1536]{1,0:T(8,128)(2,1)}, u32[]{:S(2)}, u32[]{:S(2)}) collective-permute-start(bf16[384,1536]{1,0:T(8,128)(2,1)} %get-tuple-element.65), channel_id=1, source_target_pairs={{0,1},{1,2},{2,3},{3,4},{4,5},{5,6},{6,7},{8,9},{9,10},{10,11},{11... | collective-permute-start | bytes 3538952 | tf_op jit(solution)/shard_map/ppermute | solution.py:258
  68.1 16.7 %collective-permute-done.refs_0_ = bf16[192,3072]{1,0:T(8,128)(2,1)} collective-permute-done((bf16[192,3072]{1,0:T(8,128)(2,1)S(1)}, bf16[192,3072]{1,0:T(8,128)(2,1)}, u32[]{:S(2)}, u32[]{:S(2)}) %collective-permute-start) | collective-permute-done | bytes 1179680 | tf_op jit(solution)/shard_map/ppermute | solution.py:254
  84.8 3.0 %collective-permute-start.7 = (bf16[384,1536]{1,0:T(8,128)(2,1)}, bf16[384,1536]{1,0:T(8,128)(2,1)}, u32[]{:S(2)}, u32[]{:S(2)}) collective-permute-start(bf16[384,1536]{1,0:T(8,128)(2,1)} %get-tuple-element.66), channel_id=1, source_target_pairs={{1,0},{2,1},{3,2},{4,3},{5,4},{6,5},{7,6},{9,8},{10,9},{11,10},{12... | collective-permute-start | bytes 3538952 | tf_op jit(solution)/shard_map/ppermute | solution.py:258
  87.8 1.9 collective-permute-start.8
  90.6 5.7 %collective-permute-done.21 = bf16[384,768]{1,0:T(8,128)(2,1)S(1)} collective-permute-done((bf16[384,768]{1,0:T(8,128)(2,1)S(1)}, bf16[384,768]{1,0:T(8,128)(2,1)S(1)}, u32[]{:S(2)}, u32[]{:S(2)}) %collective-permute-start.21) | collective-permute-done | bytes 589856 | tf_op jit(solution)/shard_map/ppermute | solution.py:254
  97.2 1.2 collective-permute-start.23
  98.4 1.2 slice.74
  99.6 1.1 slice.75
  100.7 1.4 fusion.4
  102.1 9.7 %collective-permute-done.23 = bf16[384,768]{1,0:T(8,128)(2,1)} collective-permute-done((bf16[384,768]{1,0:T(8,128)(2,1)}, bf16[384,768]{1,0:T(8,128)(2,1)}, u32[]{:S(2)}, u32[]{:S(2)}) %collective-permute-start.23) | collective-permute-done | bytes 589856 | tf_op jit(solution)/shard_map/ppermute | solution.py:254
  111.8 1.0 collective-permute-start.1
  112.8 1.2 fusion.2
  114.1 1.3 collective-permute-start.3
  115.4 1.3 collective-permute-start.24
  116.7 16.9 %shard_map.111 = (bf16[768,1536]{1,0:T(8,128)(2,1)}, f32[768,384]{1,0:T(8,128)}, f32[768,384]{1,0:T(8,128)}, bf16[2,384,384]{2,1,0:T(8,128)(2,1)}, bf16[2,384,384]{2,1,0:T(8,128)(2,1)}) custom-call(s32[8]{0:T(128)} %pad_add_fusion.places, bf16[384,3072]{1,0:T(8,128)(2,1)} %refs_0_.1, bf16[768,3072]{1,0:T(8,128)(2,1)} %bitcast.61, ...), custom_call_target="tpu_custom_call" | custom-call | flops 8606711808 | bytes 14155776 | tf_op jit(solution)/shard_map/pallas_call | solution.py:152
  133.6 4.5 %collective-permute-start.17 = (bf16[2,384,384]{2,1,0:T(8,128)(2,1)}, bf16[2,384,384]{2,1,0:T(8,128)(2,1)S(1)}, u32[]{:S(2)}, u32[]{:S(2)}) collective-permute-start(bf16[2,384,384]{2,1,0:T(8,128)(2,1)} %get-tuple-element.50), channel_id=1, source_target_pairs={{0,1},{1,2},{2,3},{3,4},{4,5},{5,6},{6,7},{8,9},{9,10},{10,11},{11... | collective-permute-start | bytes 1769480 | tf_op jit(solution)/shard_map/ppermute | solution.py:258
  138.1 2.1 collective-permute-start.18
  141.9 3.6 %collective-permute-start.25 = (bf16[96,1536]{1,0:T(8,128)(2,1)S(1)}, bf16[96,1536]{1,0:T(8,128)(2,1)S(1)}, u32[]{:S(2)}, u32[]{:S(2)}) collective-permute-start(bf16[96,1536]{1,0:T(8,128)(2,1)S(1)} %constant_dynamic-slice_fusion), channel_id=1, source_target_pairs={{0,4},{1,5},{2,6},{3,7},{4,0},{5,1},{6,2},{7,3},{8,12},{9,13},{10,... | collective-permute-start | bytes 884744 | tf_op jit(solution)/shard_map/ppermute | solution.py:254
  146.3 12.7 %collective-permute-done.25 = bf16[96,1536]{1,0:T(8,128)(2,1)S(1)} collective-permute-done((bf16[96,1536]{1,0:T(8,128)(2,1)S(1)}, bf16[96,1536]{1,0:T(8,128)(2,1)S(1)}, u32[]{:S(2)}, u32[]{:S(2)}) %collective-permute-start.25) | collective-permute-done | bytes 294944 | tf_op jit(solution)/shard_map/ppermute | solution.py:254
  159.0 12.3 %collective-permute-start.4 = (bf16[192,3072]{1,0:T(8,128)(2,1)}, bf16[192,3072]{1,0:T(8,128)(2,1)S(1)}, u32[]{:S(2)}, u32[]{:S(2)}) collective-permute-start(bf16[192,3072]{1,0:T(8,128)(2,1)} %constant_dynamic-update-slice_fusion.refs_0_), channel_id=1, source_target_pairs={{0,1},{1,0},{2,3},{3,2},{4,5},{5,4},{6,7},{7,6},{8,9},{9,8},{10,11... | collective-permute-start | bytes 3538952 | tf_op jit(solution)/shard_map/ppermute | solution.py:254
  172.4 16.8 %shard_map.112 = (bf16[768,1536]{1,0:T(8,128)(2,1)}, f32[768,384]{1,0:T(8,128)}, f32[768,384]{1,0:T(8,128)}, bf16[2,384,384]{2,1,0:T(8,128)(2,1)}, bf16[2,384,384]{2,1,0:T(8,128)(2,1)}) custom-call(s32[8]{0:T(128)} %pad_add_fusion.places, bf16[192,3072]{1,0:T(8,128)(2,1)} %collective-permute-done.refs_0_, ...), custom_call_target="tpu_custom_call", output_to_operand_aliasing={{0}: (13, {})} | custom-call | flops 8606711808 | bytes 14155776 | tf_op jit(solution)/shard_map/pallas_call | solution.py:152
  189.5 1.0 copy-done.15
  190.5 16.9 %shard_map.113 = (bf16[768,1536]{1,0:T(8,128)(2,1)}, f32[768,384]{1,0:T(8,128)}, f32[768,384]{1,0:T(8,128)}, bf16[2,384,384]{2,1,0:T(8,128)(2,1)}, bf16[2,384,384]{2,1,0:T(8,128)(2,1)}) custom-call(s32[8]{0:T(128)} %pad_add_fusion.places, bf16[192,3072]{1,0:T(8,128)(2,1)} %copy-done.12, ...), custom_call_target="tpu_custom_call", output_to_operand_aliasing={{0}: (13, {})} | custom-call | flops 8606711808 | bytes 14155776 | tf_op jit(solution)/shard_map/pallas_call | solution.py:152
  207.3 3.5 %collective-permute-start.13 = (bf16[2,384,384]{2,1,0:T(8,128)(2,1)}, bf16[2,384,384]{2,1,0:T(8,128)(2,1)S(1)}, u32[]{:S(2)}, u32[]{:S(2)}) collective-permute-start(bf16[2,384,384]{2,1,0:T(8,128)(2,1)} %get-tuple-element.42), channel_id=1, source_target_pairs={{0,1},{1,2},{2,3},{3,4},{4,5},{5,6},{6,7},{8,9},{9,10},{10,11},{11... | collective-permute-start | bytes 1769480 | tf_op jit(solution)/shard_map/ppermute | solution.py:258
  210.9 2.1 collective-permute-start.14
  213.3 3.6 %collective-permute-start.15 = (bf16[2,384,384]{2,1,0:T(8,128)(2,1)S(1)}, bf16[2,384,384]{2,1,0:T(8,128)(2,1)}, u32[]{:S(2)}, u32[]{:S(2)}) collective-permute-start(bf16[2,384,384]{2,1,0:T(8,128)(2,1)S(1)} %copy-done.18), channel_id=1, source_target_pairs={{0,1},{1,2},{2,3},{3,4},{4,5},{5,6},{6,7},{8,9},{9,10},{10,11},{11... | collective-permute-start | bytes 1769480 | tf_op jit(solution)/shard_map/ppermute | solution.py:258
  217.0 2.1 collective-permute-start.16
  220.2 16.8 %shard_map.114 = (bf16[768,1536]{1,0:T(8,128)(2,1)}, f32[768,384]{1,0:T(8,128)}, f32[768,384]{1,0:T(8,128)}, bf16[2,384,384]{2,1,0:T(8,128)(2,1)}, bf16[2,384,384]{2,1,0:T(8,128)(2,1)}) custom-call(s32[8]{0:T(128)} %pad_add_fusion.places, bf16[192,3072]{1,0:T(8,128)(2,1)} %constant_dynamic-update-slice_fusion.refs_0_, ...), custom_call_target="tpu_custom_call", output_to_operand_aliasing={{0}: (13, {})} | custom-call | flops 8606711808 | bytes 14155776 | tf_op jit(solution)/shard_map/pallas_call | solution.py:152
  237.1 3.6 %collective-permute-start.11 = (bf16[2,384,384]{2,1,0:T(8,128)(2,1)}, bf16[2,384,384]{2,1,0:T(8,128)(2,1)}, u32[]{:S(2)}, u32[]{:S(2)}) collective-permute-start(bf16[2,384,384]{2,1,0:T(8,128)(2,1)} %get-tuple-element.38), channel_id=1, source_target_pairs={{0,1},{1,2},{2,3},{3,4},{4,5},{5,6},{6,7},{8,9},{9,10},{10,11},{11... | collective-permute-start | bytes 1769480 | tf_op jit(solution)/shard_map/ppermute | solution.py:258
  240.7 1.9 collective-permute-start.12
  242.7 4.4 %shard_map.115 = (bf16[768,1536]{1,0:T(8,128)(2,1)}, bf16[768,1536]{1,0:T(8,128)(2,1)}) custom-call(s32[8]{0:T(128)} %pad_add_fusion.places, f32[768,384]{1,0:T(8,128)} %get-tuple-element.48.dk_ref, f32[768,384]{1,0:T(8,128)} %get-tuple-element.49.dv_ref, bf16[2,384,384]{2,1,0:T(8,128)(2,1)} %copy-done.11, bf16[2,384,384]{2,1,0:T(8,128)(2,1)} %collective-permute-done.18.above_ref), custom_call_target="tpu_custom_call" | custom-call | flops 1179648 | bytes 4718592 | tf_op jit(solution)/shard_map/pallas_call | solution.py:215
  247.1 4.4 %shard_map.116 = (bf16[768,1536]{1,0:T(8,128)(2,1)}, bf16[768,1536]{1,0:T(8,128)(2,1)}) custom-call(s32[8]{0:T(128)} %pad_add_fusion.places, f32[768,384]{1,0:T(8,128)} %get-tuple-element.44.dk_ref, f32[768,384]{1,0:T(8,128)} %get-tuple-element.45.dv_ref, ...), custom_call_target="tpu_custom_call", output_to_operand_aliasing={{0}: (5, {}), {1}: (6, {})} | custom-call | flops 1179648 | bytes 4718592 | tf_op jit(solution)/shard_map/pallas_call | solution.py:215
  252.5 4.4 %shard_map.117 = (bf16[768,1536]{1,0:T(8,128)(2,1)}, bf16[768,1536]{1,0:T(8,128)(2,1)}) custom-call(s32[8]{0:T(128)} %pad_add_fusion.places, f32[768,384]{1,0:T(8,128)} %get-tuple-element.40.dk_ref, f32[768,384]{1,0:T(8,128)} %get-tuple-element.41.dv_ref, bf16[2,384,384]{2,1,0:T(8,128)(2,1)} %copy-done.7, ...), custom_call_target="tpu_custom_call", output_to_operand_aliasing={{0}: (5, {}), {1}: (6, {})} | custom-call | flops 1179648 | bytes 4718592 | tf_op jit(solution)/shard_map/pallas_call | solution.py:215
  256.9 4.4 %shard_map.118 = (bf16[768,1536]{1,0:T(8,128)(2,1)}, bf16[768,1536]{1,0:T(8,128)(2,1)}) custom-call(s32[8]{0:T(128)} %pad_add_fusion.places, f32[768,384]{1,0:T(8,128)} %get-tuple-element.36.dk_ref, f32[768,384]{1,0:T(8,128)} %get-tuple-element.37.dv_ref, ...), custom_call_target="tpu_custom_call", output_to_operand_aliasing={{0}: (5, {}), {1}: (6, {})} | custom-call | flops 1179648 | bytes 4718592 | tf_op jit(solution)/shard_map/pallas_call | solution.py:215
  261.3 2.9 %fusion = f32[384,3072]{1,0:T(8,128)} fusion(bf16[384,1536]{1,0:T(8,128)(2,1)S(1)} %collective-permute-done.28, bf16[384,1536]{1,0:T(8,128)(2,1)S(1)} %maximum_select_fusion.1, pred[]{:T(512)S(6)} %eq.12), kind=kLoop, calls=%fused_computation.2 | loop fusion | flops 11796480 | bytes 7077889 | tf_op jit(solution)/shard_map/convert_element_type | solution.py:310
  (84 shorter events, 10.7 us)
Async XLA Ops:
  0.6 0.7 copy-start
  12.8 10.8 %collective-permute-start.19 = (bf16[2,4,384,768]{3,2,1,0:T(8,128)(2,1)}, bf16[2,4,384,768]{3,2,1,0:T(8,128)(2,1)S(1)}, u32[]{:S(2)}, u32[]{:S(2)}) collective-permute-start(bf16[2,4,384,768]{3,2,1,0:T(8,128)(2,1)} %shard_map.120), channel_id=1, source_target_pairs={{0,1},{1,0},{2,3},{3,2},{4,5},{5,4},{6,7},{7,6},{8,9},{9,8},{10,11... | collective-permute-start | bytes 14155784 | tf_op jit(solution)/shard_map/ppermute | solution.py:254
  27.2 2.2 copy-start.2
  29.4 29.1 %collective-permute-start.22 = (bf16[2,384,768]{2,1,0:T(8,128)(2,1)S(1)}, bf16[2,384,768]{2,1,0:T(8,128)(2,1)S(1)}, u32[]{:S(2)}, u32[]{:S(2)}) collective-permute-start(bf16[2,384,768]{2,1,0:T(8,128)(2,1)S(1)} %get-tuple-element.62), channel_id=1, source_target_pairs={{0,16},{1,17},{2,18},{3,19},{4,20},{5,21},{6,22},{7,23},{8,24},{9,... | collective-permute-start | bytes 3538952 | tf_op jit(solution)/shard_map/ppermute | solution.py:254
  32.1 27.4 %collective-permute-start.20 = (bf16[2,384,768]{2,1,0:T(8,128)(2,1)S(1)}, bf16[2,384,768]{2,1,0:T(8,128)(2,1)}, u32[]{:S(2)}, u32[]{:S(2)}) collective-permute-start(bf16[2,384,768]{2,1,0:T(8,128)(2,1)S(1)} %get-tuple-element.63), channel_id=1, source_target_pairs={{0,8},{1,9},{2,10},{3,11},{4,12},{5,13},{6,14},{7,15},{8,0},{9,1},... | collective-permute-start | bytes 3538952 | tf_op jit(solution)/shard_map/ppermute | solution.py:254
  33.3 2.0 copy-start.5
  34.8 50.0 %collective-permute-start = (bf16[192,3072]{1,0:T(8,128)(2,1)S(1)}, bf16[192,3072]{1,0:T(8,128)(2,1)}, u32[]{:S(2)}, u32[]{:S(2)}) collective-permute-start(bf16[192,3072]{1,0:T(8,128)(2,1)S(1)} %constant_dynamic-slice_fusion.1), channel_id=1, source_target_pairs={{0,8},{1,9},{2,10},{3,11},{4,12},{5,13},{6,14},{7,15},{8,0},{9,1},... | collective-permute-start | bytes 3538952 | tf_op jit(solution)/shard_map/ppermute | solution.py:254
  35.1 52.6 %collective-permute-start.2 = (bf16[192,3072]{1,0:T(8,128)(2,1)S(1)}, bf16[192,3072]{1,0:T(8,128)(2,1)S(1)}, u32[]{:S(2)}, u32[]{:S(2)}) collective-permute-start(bf16[192,3072]{1,0:T(8,128)(2,1)S(1)} %constant_dynamic-slice_fusion.1), channel_id=1, source_target_pairs={{0,16},{1,17},{2,18},{3,19},{4,20},{5,21},{6,22},{7,23},{8,24},{9,... | collective-permute-start | bytes 3538952 | tf_op jit(solution)/shard_map/ppermute | solution.py:254
  35.3 24.2 %copy-start.3 = (bf16[2,4,384,768]{3,2,1,0:T(8,128)(2,1)S(1)}, bf16[2,4,384,768]{3,2,1,0:T(8,128)(2,1)}, u32[]{:S(2)}) copy-start(bf16[2,4,384,768]{3,2,1,0:T(8,128)(2,1)} %copy-done.2) | copy-start | bytes 14155780
  36.9 77.2 %collective-permute-start.5 = (bf16[384,1536]{1,0:T(8,128)(2,1)}, bf16[384,1536]{1,0:T(8,128)(2,1)}, u32[]{:S(2)}, u32[]{:S(2)}) collective-permute-start(bf16[384,1536]{1,0:T(8,128)(2,1)} %get-tuple-element.67), channel_id=1, source_target_pairs={{0,1},{1,2},{2,3},{3,4},{4,5},{5,6},{6,7},{8,9},{9,10},{10,11},{11... | collective-permute-start | bytes 3538952 | tf_op jit(solution)/shard_map/ppermute | solution.py:258
  59.5 2.4 copy-start.6
  61.4 1.8 copy-start.4
  61.4 34.9 %collective-permute-start.21 = (bf16[384,768]{1,0:T(8,128)(2,1)S(1)}, bf16[384,768]{1,0:T(8,128)(2,1)S(1)}, u32[]{:S(2)}, u32[]{:S(2)}) collective-permute-start(bf16[384,768]{1,0:T(8,128)(2,1)S(1)} %fusion.5), channel_id=1, source_target_pairs={{0,16},{1,17},{2,18},{3,19},{4,20},{5,21},{6,22},{7,23},{8,24},{9,... | collective-permute-start | bytes 1769480 | tf_op jit(solution)/shard_map/ppermute | solution.py:254
  63.2 52.2 %collective-permute-start.6 = (bf16[384,1536]{1,0:T(8,128)(2,1)}, bf16[384,1536]{1,0:T(8,128)(2,1)}, u32[]{:S(2)}, u32[]{:S(2)}) collective-permute-start(bf16[384,1536]{1,0:T(8,128)(2,1)} %get-tuple-element.65), channel_id=1, source_target_pairs={{0,1},{1,2},{2,3},{3,4},{4,5},{5,6},{6,7},{8,9},{9,10},{10,11},{11... | collective-permute-start | bytes 3538952 | tf_op jit(solution)/shard_map/ppermute | solution.py:258
  84.8 31.9 %collective-permute-start.7 = (bf16[384,1536]{1,0:T(8,128)(2,1)}, bf16[384,1536]{1,0:T(8,128)(2,1)}, u32[]{:S(2)}, u32[]{:S(2)}) collective-permute-start(bf16[384,1536]{1,0:T(8,128)(2,1)} %get-tuple-element.66), channel_id=1, source_target_pairs={{1,0},{2,1},{3,2},{4,3},{5,4},{6,5},{7,6},{9,8},{10,9},{11,10},{12... | collective-permute-start | bytes 3538952 | tf_op jit(solution)/shard_map/ppermute | solution.py:258
  87.8 8.6 %copy-start.12 = (bf16[192,3072]{1,0:T(8,128)(2,1)}, bf16[192,3072]{1,0:T(8,128)(2,1)S(1)}, u32[]{:S(2)}) copy-start(bf16[192,3072]{1,0:T(8,128)(2,1)S(1)} %collective-permute-done.2.refs_0_) | copy-start | bytes 3538948
  87.8 28.9 %collective-permute-start.8 = (bf16[384,1536]{1,0:T(8,128)(2,1)S(1)}, bf16[384,1536]{1,0:T(8,128)(2,1)}, u32[]{:S(2)}, u32[]{:S(2)}) collective-permute-start(bf16[384,1536]{1,0:T(8,128)(2,1)S(1)} %get-tuple-element.64), channel_id=1, source_target_pairs={{1,0},{2,1},{3,2},{4,3},{5,4},{6,5},{7,6},{9,8},{10,9},{11,10},{12... | collective-permute-start | bytes 3538952 | tf_op jit(solution)/shard_map/ppermute | solution.py:258
  96.3 0.8 copy-start.9
  97.2 14.6 %collective-permute-start.23 = (bf16[384,768]{1,0:T(8,128)(2,1)}, bf16[384,768]{1,0:T(8,128)(2,1)}, u32[]{:S(2)}, u32[]{:S(2)}) collective-permute-start(bf16[384,768]{1,0:T(8,128)(2,1)} %fusion.6), channel_id=1, source_target_pairs={{0,8},{1,9},{2,10},{3,11},{4,12},{5,13},{6,14},{7,15},{8,0},{9,1},... | collective-permute-start | bytes 1769480 | tf_op jit(solution)/shard_map/ppermute | solution.py:254
  98.4 2.3 copy-start.10
  111.8 28.4 %collective-permute-start.1 = (bf16[96,3072]{1,0:T(8,128)(2,1)S(1)}, bf16[96,3072]{1,0:T(8,128)(2,1)S(1)}, u32[]{:S(2)}, u32[]{:S(2)}) collective-permute-start(bf16[96,3072]{1,0:T(8,128)(2,1)S(1)} %slice.74), channel_id=1, source_target_pairs={{0,16},{1,17},{2,18},{3,19},{4,20},{5,21},{6,22},{7,23},{8,24},{9,... | collective-permute-start | bytes 1769480 | tf_op jit(solution)/shard_map/ppermute | solution.py:254
  114.1 27.7 %collective-permute-start.3 = (bf16[96,3072]{1,0:T(8,128)(2,1)S(1)}, bf16[96,3072]{1,0:T(8,128)(2,1)S(1)}, u32[]{:S(2)}, u32[]{:S(2)}) collective-permute-start(bf16[96,3072]{1,0:T(8,128)(2,1)S(1)} %slice.75), channel_id=1, source_target_pairs={{0,8},{1,9},{2,10},{3,11},{4,12},{5,13},{6,14},{7,15},{8,0},{9,1},... | collective-permute-start | bytes 1769480 | tf_op jit(solution)/shard_map/ppermute | solution.py:254
  115.4 25.8 %collective-permute-start.24 = (bf16[192,1536]{1,0:T(8,128)(2,1)S(1)}, bf16[192,1536]{1,0:T(8,128)(2,1)S(1)}, u32[]{:S(2)}, u32[]{:S(2)}) collective-permute-start(bf16[192,1536]{1,0:T(8,128)(2,1)S(1)} %fusion.7), channel_id=1, source_target_pairs={{0,2},{1,3},{2,0},{3,1},{4,6},{5,7},{6,4},{7,5},{8,10},{9,11},{10,... | collective-permute-start | bytes 1769480 | tf_op jit(solution)/shard_map/ppermute | solution.py:254
  116.7 23.5 %copy-start.13 = (bf16[192,3072]{1,0:T(8,128)(2,1)S(1)}, bf16[192,3072]{1,0:T(8,128)(2,1)}, u32[]{:S(2)}) copy-start(bf16[192,3072]{1,0:T(8,128)(2,1)} %copy-done.12) | copy-start | bytes 3538948
  133.6 79.7 %collective-permute-start.17 = (bf16[2,384,384]{2,1,0:T(8,128)(2,1)}, bf16[2,384,384]{2,1,0:T(8,128)(2,1)S(1)}, u32[]{:S(2)}, u32[]{:S(2)}) collective-permute-start(bf16[2,384,384]{2,1,0:T(8,128)(2,1)} %get-tuple-element.50), channel_id=1, source_target_pairs={{0,1},{1,2},{2,3},{3,4},{4,5},{5,6},{6,7},{8,9},{9,10},{10,11},{11... | collective-permute-start | bytes 1769480 | tf_op jit(solution)/shard_map/ppermute | solution.py:258
  138.1 78.9 %collective-permute-start.18 = (bf16[2,384,384]{2,1,0:T(8,128)(2,1)}, bf16[2,384,384]{2,1,0:T(8,128)(2,1)}, u32[]{:S(2)}, u32[]{:S(2)}) collective-permute-start(bf16[2,384,384]{2,1,0:T(8,128)(2,1)} %get-tuple-element.51), channel_id=1, source_target_pairs={{1,0},{2,1},{3,2},{4,3},{5,4},{6,5},{7,6},{9,8},{10,9},{11,10},{12... | collective-permute-start | bytes 1769480 | tf_op jit(solution)/shard_map/ppermute | solution.py:258
  140.2 49.2 %collective-permute-start.9 = (bf16[192,3072]{1,0:T(8,128)(2,1)S(1)}, bf16[192,3072]{1,0:T(8,128)(2,1)S(1)}, u32[]{:S(2)}, u32[]{:S(2)}) collective-permute-start(bf16[192,3072]{1,0:T(8,128)(2,1)S(1)} %copy-done.13), channel_id=1, source_target_pairs={{0,1},{1,0},{2,3},{3,2},{4,5},{5,4},{6,7},{7,6},{8,9},{9,8},{10,11... | collective-permute-start | bytes 3538952 | tf_op jit(solution)/shard_map/ppermute | solution.py:254
  141.2 30.2 %collective-permute-start.10 = (bf16[192,3072]{1,0:T(8,128)(2,1)}, bf16[192,3072]{1,0:T(8,128)(2,1)S(1)}, u32[]{:S(2)}, u32[]{:S(2)}) collective-permute-start(bf16[192,3072]{1,0:T(8,128)(2,1)} %collective-permute-done.refs_0_), channel_id=1, source_target_pairs={{0,1},{1,0},{2,3},{3,2},{4,5},{5,4},{6,7},{7,6},{8,9},{9,8},{10,11... | collective-permute-start | bytes 3538952 | tf_op jit(solution)/shard_map/ppermute | solution.py:254
  141.9 17.2 %collective-permute-start.25 = (bf16[96,1536]{1,0:T(8,128)(2,1)S(1)}, bf16[96,1536]{1,0:T(8,128)(2,1)S(1)}, u32[]{:S(2)}, u32[]{:S(2)}) collective-permute-start(bf16[96,1536]{1,0:T(8,128)(2,1)S(1)} %constant_dynamic-slice_fusion), channel_id=1, source_target_pairs={{0,4},{1,5},{2,6},{3,7},{4,0},{5,1},{6,2},{7,3},{8,12},{9,13},{10,... | collective-permute-start | bytes 884744 | tf_op jit(solution)/shard_map/ppermute | solution.py:254
  159.0 60.2 %collective-permute-start.4 = (bf16[192,3072]{1,0:T(8,128)(2,1)}, bf16[192,3072]{1,0:T(8,128)(2,1)S(1)}, u32[]{:S(2)}, u32[]{:S(2)}) collective-permute-start(bf16[192,3072]{1,0:T(8,128)(2,1)} %constant_dynamic-update-slice_fusion.refs_0_), channel_id=1, source_target_pairs={{0,1},{1,0},{2,3},{3,2},{4,5},{5,4},{6,7},{7,6},{8,9},{9,8},{10,11... | collective-permute-start | bytes 3538952 | tf_op jit(solution)/shard_map/ppermute | solution.py:254
  171.4 1.0 copy-start.16
  171.4 17.9 %collective-permute-start.26 = (bf16[96,1536]{1,0:T(8,128)(2,1)S(1)}, bf16[96,1536]{1,0:T(8,128)(2,1)S(1)}, u32[]{:S(2)}, u32[]{:S(2)}) collective-permute-start(bf16[96,1536]{1,0:T(8,128)(2,1)S(1)} %add_convert_fusion.2), channel_id=1, source_target_pairs={{0,4},{1,5},{2,6},{3,7},{4,0},{5,1},{6,2},{7,3},{8,12},{9,13},{10,... | collective-permute-start | bytes 884744 | tf_op jit(solution)/shard_map/ppermute | solution.py:254
  189.4 21.5 %collective-permute-start.27 = (bf16[192,1536]{1,0:T(8,128)(2,1)S(1)}, bf16[192,1536]{1,0:T(8,128)(2,1)S(1)}, u32[]{:S(2)}, u32[]{:S(2)}) collective-permute-start(bf16[192,1536]{1,0:T(8,128)(2,1)S(1)} %maximum_select_fusion.2), channel_id=1, source_target_pairs={{0,2},{1,3},{2,0},{3,1},{4,6},{5,7},{6,4},{7,5},{8,10},{9,11},{10,... | collective-permute-start | bytes 1769480 | tf_op jit(solution)/shard_map/ppermute | solution.py:254
  189.4 1.0 copy-start.15
  207.3 44.1 %collective-permute-start.13 = (bf16[2,384,384]{2,1,0:T(8,128)(2,1)}, bf16[2,384,384]{2,1,0:T(8,128)(2,1)S(1)}, u32[]{:S(2)}, u32[]{:S(2)}) collective-permute-start(bf16[2,384,384]{2,1,0:T(8,128)(2,1)} %get-tuple-element.42), channel_id=1, source_target_pairs={{0,1},{1,2},{2,3},{3,4},{4,5},{5,6},{6,7},{8,9},{9,10},{10,11},{11... | collective-permute-start | bytes 1769480 | tf_op jit(solution)/shard_map/ppermute | solution.py:258
  210.9 2.5 copy-start.18
  210.9 6.1 %copy-start.17 = (bf16[2,384,384]{2,1,0:T(8,128)(2,1)S(1)}, bf16[2,384,384]{2,1,0:T(8,128)(2,1)}, u32[]{:S(2)}) copy-start(bf16[2,384,384]{2,1,0:T(8,128)(2,1)} %get-tuple-element.47) | copy-start | bytes 1769476
  210.9 40.6 %collective-permute-start.14 = (bf16[2,384,384]{2,1,0:T(8,128)(2,1)}, bf16[2,384,384]{2,1,0:T(8,128)(2,1)S(1)}, u32[]{:S(2)}, u32[]{:S(2)}) collective-permute-start(bf16[2,384,384]{2,1,0:T(8,128)(2,1)} %get-tuple-element.43), channel_id=1, source_target_pairs={{1,0},{2,1},{3,2},{4,3},{5,4},{6,5},{7,6},{9,8},{10,9},{11,10},{12... | collective-permute-start | bytes 1769480 | tf_op jit(solution)/shard_map/ppermute | solution.py:258
  213.3 5.8 %copy-start.11 = (bf16[2,384,384]{2,1,0:T(8,128)(2,1)}, bf16[2,384,384]{2,1,0:T(8,128)(2,1)S(1)}, u32[]{:S(2)}) copy-start(bf16[2,384,384]{2,1,0:T(8,128)(2,1)S(1)} %collective-permute-done.17.below_ref) | copy-start | bytes 1769476
  213.3 23.7 %collective-permute-start.15 = (bf16[2,384,384]{2,1,0:T(8,128)(2,1)S(1)}, bf16[2,384,384]{2,1,0:T(8,128)(2,1)}, u32[]{:S(2)}, u32[]{:S(2)}) collective-permute-start(bf16[2,384,384]{2,1,0:T(8,128)(2,1)S(1)} %copy-done.18), channel_id=1, source_target_pairs={{0,1},{1,2},{2,3},{3,4},{4,5},{5,6},{6,7},{8,9},{9,10},{10,11},{11... | collective-permute-start | bytes 1769480 | tf_op jit(solution)/shard_map/ppermute | solution.py:258
  217.0 23.7 %collective-permute-start.16 = (bf16[2,384,384]{2,1,0:T(8,128)(2,1)S(1)}, bf16[2,384,384]{2,1,0:T(8,128)(2,1)}, u32[]{:S(2)}, u32[]{:S(2)}) collective-permute-start(bf16[2,384,384]{2,1,0:T(8,128)(2,1)S(1)} %copy-done.17), channel_id=1, source_target_pairs={{1,0},{2,1},{3,2},{4,3},{5,4},{6,5},{7,6},{9,8},{10,9},{11,10},{12... | collective-permute-start | bytes 1769480 | tf_op jit(solution)/shard_map/ppermute | solution.py:258
  219.2 1.0 copy-start.14
  219.2 42.1 %collective-permute-start.28 = (bf16[384,1536]{1,0:T(8,128)(2,1)S(1)}, bf16[384,1536]{1,0:T(8,128)(2,1)S(1)}, u32[]{:S(2)}, u32[]{:S(2)}) collective-permute-start(bf16[384,1536]{1,0:T(8,128)(2,1)S(1)} %maximum_select_fusion.1), channel_id=1, source_target_pairs={{0,1},{1,0},{2,3},{3,2},{4,5},{5,4},{6,7},{7,6},{8,9},{9,8},{10,11... | collective-permute-start | bytes 3538952 | tf_op jit(solution)/shard_map/ppermute | solution.py:254
  237.1 19.8 %collective-permute-start.11 = (bf16[2,384,384]{2,1,0:T(8,128)(2,1)}, bf16[2,384,384]{2,1,0:T(8,128)(2,1)}, u32[]{:S(2)}, u32[]{:S(2)}) collective-permute-start(bf16[2,384,384]{2,1,0:T(8,128)(2,1)} %get-tuple-element.38), channel_id=1, source_target_pairs={{0,1},{1,2},{2,3},{3,4},{4,5},{5,6},{6,7},{8,9},{9,10},{10,11},{11... | collective-permute-start | bytes 1769480 | tf_op jit(solution)/shard_map/ppermute | solution.py:258
  240.7 16.1 %collective-permute-start.12 = (bf16[2,384,384]{2,1,0:T(8,128)(2,1)}, bf16[2,384,384]{2,1,0:T(8,128)(2,1)}, u32[]{:S(2)}, u32[]{:S(2)}) collective-permute-start(bf16[2,384,384]{2,1,0:T(8,128)(2,1)} %get-tuple-element.39), channel_id=1, source_target_pairs={{1,0},{2,1},{3,2},{4,3},{5,4},{6,5},{7,6},{9,8},{10,9},{11,10},{12... | collective-permute-start | bytes 1769480 | tf_op jit(solution)/shard_map/ppermute | solution.py:258
  251.4 0.8 copy-start.7
  251.5 1.0 copy-start.8
  261.3 2.9 %copy-start.1 = (s32[1,16,3]{1,0,2:T(1,128)S(1)}, s32[1,16,3]{1,0,2:T(1,128)}, u32[]{:S(2)}) copy-start(s32[1,16,3]{1,0,2:T(1,128)} %param.15) | copy-start | bytes 580
where the time goes:
time: 265 us; the launch traced here: 264 us
  Pallas kernels  106 us (40%)
  starting transfers between devices  63.9 us (24%)
  waiting for transfers between devices  63.1 us (24%)
  local copies, waits for them, and re-layouts  17.4 us (7%)
  other arithmetic  12.3 us (5%)
    pallas_call x4, Pallas kernels, attend(): pl.pallas_call(functools.partial(attend_kernel, 1.0 / math.sqrt(HD), len(...  67.4 us
    ppermute x17, waiting for transfers between devices, swap(): return lax.ppermute(value, ('dp', 'seq'), pairs)  63 us
    ppermute x12, starting transfers between devices, along(): return lax.ppermute(value, 'seq', pairs)  37.7 us
    ppermute x17, starting transfers between devices, swap(): return lax.ppermute(value, ('dp', 'seq'), pairs)  26.2 us
    pallas_call x2, Pallas kernels, weight_part(): pl.pallas_call(weight_kernel, grid_spec=pltpu.PrefetchScalarGridSpec(num_...  21.4 us
    pallas_call x4, Pallas kernels, finish(): pl.pallas_call(functools.partial(finish_kernel, 1.0 / math.sqrt(HD), chai...  17.6 us
    unnamed x40, local copies, waits for them, and re-layouts  8.54 us
  transfers between devices with their start and end apart: 29, of which 6 were waited for; matrix products, arithmetic and copies ran while one was open for 6% of the time, Pallas kernels for 36%

commit v1 on v0

v1 whole, which is shorter than its diff:
```python
import functools
import math

import jax
import jax.numpy as jnp
from jax import lax
from jax.experimental import pallas as pl
from jax.experimental.pallas import tpu as pltpu
from jax.sharding import PartitionSpec as P

TILE = 384
HD = 128
VMEM = 56 * 1024 * 1024
NT = (((1,), (1,)), ((), ()))
TN = (((0,), (0,)), ((), ()))


def mm(a, b, dims=(((1,), (0,)), ((), ()))):
    return lax.dot_general(a, b, dims, preferred_element_type=jnp.float32)


def weight_kernel(places, out_ref, grad_ref, part_ref):
    part_ref[0] = mm(out_ref[...], grad_ref[...], TN).astype(part_ref.dtype)


def weight_part(places, rows, grads, send):
    tokens, width = rows.shape
    high = width // 4
    wide = grads.shape[1] // 2

    def half(at):
        return 1 - at[1] if send else at[1]

    def out_at(p, at):
        swapped = (p % 2) * 2 + p // 2
        return (0, at[0] ^ jnp.where(half(at) == 0, swapped, p))

    return pl.pallas_call(
        weight_kernel,
        grid_spec=pltpu.PrefetchScalarGridSpec(
            num_scalar_prefetch=1,
            grid=(4,),
            in_specs=[
                pl.BlockSpec((tokens, high), out_at),
                pl.BlockSpec((tokens, wide), lambda p, at: (0, half(at))),
            ],
            out_specs=pl.BlockSpec((1, high, wide), lambda p, at: (p, 0, 0)),
        ),
        out_shape=jax.ShapeDtypeStruct((4, high, wide), jnp.bfloat16),
        compiler_params=pltpu.CompilerParams(vmem_limit_bytes=VMEM),
        cost_estimate=pl.CostEstimate(
            flops=tokens * width * grads.shape[1],
            bytes_accessed=tokens * width * 2 + tokens * grads.shape[1] + width * grads.shape[1],
            transcendentals=0,
        ),
    )(places, rows, grads)


def sum_kernel(count, places, *refs):
    a0, b0, a1, b1 = refs[:4]
    keep_ref, send_ref = refs[4 + count :]
    f32 = jnp.float32
    keep_ref[...] = (a0[...].astype(f32) + b0[...].astype(f32)).astype(jnp.bfloat16)
    send_ref[...] = (a1[...].astype(f32) + b1[...].astype(f32)).astype(jnp.bfloat16)


def line_kernel(count, places, a_ref, b_ref, *refs):
    f32 = jnp.float32
    refs[count][...] = (a_ref[...].astype(f32) + b_ref[...].astype(f32)).astype(jnp.bfloat16)


def sum_whole(places, a, b, after):
    whole = pl.BlockSpec(a.shape, lambda i, at: (0, 0))
    return pl.pallas_call(
        functools.partial(line_kernel, len(after)),
        grid_spec=pltpu.PrefetchScalarGridSpec(
            num_scalar_prefetch=1,
            grid=(1,),
            in_specs=[whole, whole] + [pl.BlockSpec(memory_space=pl.ANY)] * len(after),
            out_specs=whole,
        ),
        out_shape=jax.ShapeDtypeStruct(a.shape, jnp.bfloat16),
        compiler_params=pltpu.CompilerParams(vmem_limit_bytes=VMEM),
        cost_estimate=pl.CostEstimate(
            flops=a.size, bytes_accessed=6 * a.size, transcendentals=0
        ),
    )(places, a, b, *after)


def sum_and_cut(places, bit, a, b, after=()):
    size, wide = a.shape[0] // 2, a.shape[1]
    chunk = min(size, 192)
    steps = size // chunk

    def half(at):
        return 0 if bit is None else at[bit]

    kept = pl.BlockSpec((chunk, wide), lambda i, at: (half(at) * steps + i, 0))
    sent = pl.BlockSpec((chunk, wide), lambda i, at: ((1 - half(at)) * steps + i, 0))
    out = pl.BlockSpec((chunk, wide), lambda i, at: (i, 0))
    return pl.pallas_call(
        functools.partial(sum_kernel, len(after)),
        grid_spec=pltpu.PrefetchScalarGridSpec(
            num_scalar_prefetch=1,
            grid=(steps,),
            in_specs=[kept, kept, sent, sent] + [pl.BlockSpec(memory_space=pl.ANY)] * len(after),
            out_specs=[out, out],
        ),
        out_shape=[jax.ShapeDtypeStruct((size, wide), jnp.bfloat16)] * 2,
        compiler_params=pltpu.CompilerParams(vmem_limit_bytes=VMEM),
        cost_estimate=pl.CostEstimate(
            flops=a.size, bytes_accessed=6 * a.size, transcendentals=0
        ),
    )(places, a, b, a, b, *after)


def attend_kernel(scale, halves, extra, places, *refs):
    weights = refs[: 2 if halves else 1]
    refs = refs[len(weights) :]
    (grad_ref, q_ref, o_ref, norm_ref, k_ref, v_ref, below_ref, above_ref) = refs[:8]
    refs = refs[8 + extra :]
    (dq_ref, dk_ref, dv_ref, low_ref, high_ref) = refs[:5]
    (full, attn_grad, kwin, vwin, kflip, dk, dv) = refs[5:]
    head = pl.program_id(0)
    tokens = q_ref.shape[0]
    tiles = tokens // TILE

    @pl.when(head == 0)
    def _():
        if halves:
            rows = weights[0].shape[0]
            mine = pl.multiple_of(places[1] * rows, rows)
            other = pl.multiple_of((1 - places[1]) * rows, rows)
            full[pl.ds(mine, rows)] = weights[0][...]
            full[pl.ds(other, rows)] = weights[1][...]
            block = full[...]
        else:
            block = weights[0][...]
        got = mm(grad_ref[...], block, NT).astype(jnp.bfloat16)
        for i in range(attn_grad.shape[0]):
            attn_grad[i] = got[:, i * HD : (i + 1) * HD]

    kwin[0] = below_ref[0]
    vwin[0] = below_ref[1]
    for t in range(tiles):
        kwin[t + 1] = k_ref[t * TILE : (t + 1) * TILE]
        vwin[t + 1] = v_ref[t * TILE : (t + 1) * TILE]
    kwin[tiles + 1] = above_ref[0]
    vwin[tiles + 1] = above_ref[1]
    for w in range(tiles + 2):
        kflip[w] = kwin[w].T
    dk[...] = jnp.zeros_like(dk)
    dv[...] = jnp.zeros_like(dv)
    log2e = 1.0 / math.log(2.0)

    def rows_of(t):
        return slice(t * TILE, (t + 1) * TILE)

    def products(t, n):
        w = places[4 + t * 3 + n]
        q, do = q_ref[rows_of(t)], attn_grad[head, rows_of(t)]
        return w, mm(kwin[w], q, NT), mm(vwin[w], do, NT)

    pieces = [(t, n) for t in range(tiles) for n in range(3)]
    ahead = products(*pieces[0])
    dq = None
    for at, (t, n) in enumerate(pieces):
        w, scores, prob = ahead
        if at + 1 < len(pieces):
            ahead = products(*pieces[at + 1])
        rows = rows_of(t)
        q, do = q_ref[rows], attn_grad[head, rows]
        if n == 0:
            norm = norm_ref[0, :, rows] * log2e
            both = do.astype(jnp.float32) * o_ref[rows].astype(jnp.float32)
            delta = both.T.sum(0, keepdims=True)
        p = jnp.exp2(scores * (scale * log2e) - norm)
        ds = (p * (prob - delta)).astype(jnp.bfloat16)
        dv[w] += mm(p.astype(jnp.bfloat16), do)
        dk[w] += mm(ds, q)
        part = mm(kflip[w], ds)
        dq = part if n == 0 else dq + part
        if n == 2:
            dq_ref[rows] = (dq * scale).T.astype(jnp.bfloat16)
    for t in range(tiles):
        dk_ref[rows_of(t)] = dk[t + 1].astype(jnp.bfloat16)
        dv_ref[rows_of(t)] = dv[t + 1].astype(jnp.bfloat16)
    low_ref[0] = dk[0].astype(jnp.bfloat16)
    low_ref[1] = dv[0].astype(jnp.bfloat16)
    high_ref[0] = dk[tiles + 1].astype(jnp.bfloat16)
    high_ref[1] = dv[tiles + 1].astype(jnp.bfloat16)


def attend(places, step, heads, weights, grads, query, attn_out, norm, keys, values, halos, before, after=()):
    tokens, width = query.shape
    tiles = tokens // TILE
    group = heads * HD
    depth = grads.shape[1]

    def at_head(h, at):
        return (0, (at[0] ^ step) * heads + h)

    def column(rows):
        return pl.BlockSpec((rows, HD), at_head)

    whole = [pl.BlockSpec(w.shape, lambda h, at: (0, 0)) for w in (*weights, grads)]
    in_specs = [
        *whole,
        column(tokens),
        column(tokens),
        pl.BlockSpec((1, 1, tokens), lambda h, at: ((at[0] ^ step) * heads + h, 0, 0)),
        column(tokens),
        column(tokens),
        *[pl.BlockSpec((2, TILE, HD), lambda h, at: (0, 0, (at[0] ^ step) * heads + h))] * 2,
    ]
    operands = [*weights, grads, query, attn_out, norm, keys, values, *halos]
    aliases = {}
    if before is not None:
        aliases = {len(operands) + 1 + i: i for i in range(3)}
        operands += before
    operands += after
    extra = len(operands) - len(in_specs)
    in_specs += [pl.BlockSpec(memory_space=pl.ANY)] * extra
    rim = pl.BlockSpec((2, TILE, HD), lambda h, at: (0, 0, h))
    kept = 3
    return pl.pallas_call(
        functools.partial(attend_kernel, 1.0 / math.sqrt(HD), len(weights) == 2, extra),
        grid_spec=pltpu.PrefetchScalarGridSpec(
            num_scalar_prefetch=1,
            grid=(heads,),
            in_specs=in_specs,
            out_specs=[column(tokens)] * 3 + [rim, rim],
            scratch_shapes=[
                pltpu.VMEM((group, depth), jnp.bfloat16),
                pltpu.VMEM((heads, tokens, HD), jnp.bfloat16),
                pltpu.VMEM((tiles + 2, TILE, HD), jnp.bfloat16),
                pltpu.VMEM((tiles + 2, TILE, HD), jnp.bfloat16),
                pltpu.VMEM((tiles + 2, HD, TILE), jnp.bfloat16),
                pltpu.VMEM((tiles + 2, TILE, HD), jnp.float32),
                pltpu.VMEM((tiles + 2, TILE, HD), jnp.float32),
            ],
        ),
        out_shape=[
            *[jax.ShapeDtypeStruct((tokens, width), jnp.bfloat16)] * 3,
            jax.ShapeDtypeStruct((2, TILE, group), jnp.bfloat16),
            jax.ShapeDtypeStruct((2, TILE, group), jnp.bfloat16),
        ],
        input_output_aliases=aliases,
        compiler_params=pltpu.CompilerParams(vmem_limit_bytes=VMEM),
        cost_estimate=pl.CostEstimate(
            flops=2 * tokens * depth * group + 20 * tokens * kept * TILE * group,
            bytes_accessed=2 * tokens * depth + 2 * depth * group + 24 * tokens * group,
            transcendentals=heads * tokens * kept * TILE,
        ),
    )(places, *operands)


def finish_kernel(scale, places, dk_ref, dv_ref, *refs):
    rims, (key_ref, value_ref) = refs[:-2], refs[-2:]
    tokens = dk_ref.shape[0]
    tiles = tokens // TILE
    f32 = jnp.float32
    for step in range(len(rims) // 2):

        @pl.when(pl.program_id(0) == step)
        def _(below=rims[2 * step], above=rims[2 * step + 1]):
            for t in range(tiles):
                rows = slice(t * TILE, (t + 1) * TILE)
                key, value = dk_ref[rows].astype(f32), dv_ref[rows].astype(f32)
                if t == 0:
                    key, value = key + below[0].astype(f32), value + below[1].astype(f32)
                if t == tiles - 1:
                    key, value = key + above[0].astype(f32), value + above[1].astype(f32)
                key_ref[rows] = (key * scale).astype(jnp.bfloat16)
                value_ref[rows] = value.astype(jnp.bfloat16)


def finish(places, dk, dv, rims):
    tokens, width = dk.shape
    steps = len(rims) // 2
    group = width // steps
    rim = pl.BlockSpec((2, TILE, group), lambda j, at: (0, 0, 0))
    placed = pl.BlockSpec((tokens, group), lambda j, at: (0, at[0] ^ j))
    return pl.pallas_call(
        functools.partial(finish_kernel, 1.0 / math.sqrt(HD)),
        grid_spec=pltpu.PrefetchScalarGridSpec(
            num_scalar_prefetch=1,
            grid=(steps,),
            in_specs=[placed, placed] + [rim] * len(rims),
            out_specs=[placed, placed],
        ),
        out_shape=[jax.ShapeDtypeStruct((tokens, width), jnp.bfloat16)] * 2,
        compiler_params=pltpu.CompilerParams(vmem_limit_bytes=VMEM),
        cost_estimate=pl.CostEstimate(
            flops=4 * tokens * width, bytes_accessed=12 * tokens * width, transcendentals=0
        ),
    )(places, dk, dv, *rims)


def body(query, key_states, value_states, attn_out, log_norm, out_grad, out_weight, tile_lists):
    dp_size, seq_size = lax.axis_size("dp"), lax.axis_size("seq")
    cube = dp_size == 4 and seq_size == 8
    query, keys, values, rows = query[0], key_states[0], value_states[0], attn_out[0]
    grads = out_grad[0]
    norm = log_norm[0][:, None, :]
    tokens, width = query.shape
    tiles = tokens // TILE
    head_count = norm.shape[0]
    steps = 4
    heads = head_count // steps
    high = width // steps
    dp, seq = lax.axis_index("dp"), lax.axis_index("seq")
    core = seq % 2
    own = lax.dynamic_slice_in_dim(tile_lists[0], seq * tiles, tiles, 0)
    kept = (own - (seq * tiles - 1)).reshape(-1).astype(jnp.int32)
    first = dp if cube else jnp.int32(0)
    bits = jnp.stack([first, core, (seq // 2) % 2, seq // 4]).astype(jnp.int32)
    places = jnp.concatenate([bits, kept])

    def send(value, partner):
        pairs = []
        for a in range(dp_size):
            for b in range(seq_size):
                to, at = partner(a, b)
                pairs.append((a * seq_size + b, to * seq_size + at))
        return lax.ppermute(value, ("dp", "seq"), pairs)

    def swap(value, dp_bit, seq_bit):
        return send(value, lambda a, b: (a ^ dp_bit, b ^ seq_bit))

    def swap_by_core(value, bits):
        return send(value, lambda a, b: (a ^ bits[b % 2], b))

    def along(value, by):
        pairs = [(i, i + by) for i in range(seq_size) if 0 <= i + by < seq_size]
        return lax.ppermute(value, "seq", pairs)

    if cube:
        half = lax.dynamic_slice_in_dim(out_weight, core * (high // 2), high // 2, 0)
        by_x, by_y = swap(half, 1, 0), swap(half, 2, 0)
        by_both = swap_by_core(jnp.where(core == 0, by_x, by_y), (2, 1))
        blocks = [[out_weight]] + [[b, swap(b, 0, 1)] for b in (by_x, by_y, by_both)]
    else:
        gathered = lax.all_gather(out_weight, "dp", axis=0, tiled=True)
        blocks = [[gathered[i * high : (i + 1) * high]] for i in range(steps)]

    halos = [
        along(jnp.stack([keys[tokens - TILE :], values[tokens - TILE :]]), 1),
        along(jnp.stack([keys[:TILE], values[:TILE]]), -1),
    ]

    first_after = ()
    if cube:
        wide = grads.shape[1] // 2
        sent = swap(weight_part(places, rows, grads, True), 0, 1).reshape(width, wide)
        mine = weight_part(places, rows, grads, False).reshape(width, wide)
        chip_keep, chip_send = sum_and_cut(places, None, mine, sent)
        chip_got = swap_by_core(chip_send, (1, 2))
        first_after = (chip_send,)

    results, rims, marks = None, [], []
    for step in range(steps):
        after = first_after if step == 0 else rims[2 * step - 4 : 2 * step - 2] if step > 1 else ()
        *results, low_rim, high_rim = attend(
            places, step, heads, blocks[step], grads, query, rows, norm, keys, values, halos, results, after
        )
        rims += [along(high_rim, 1), along(low_rim, -1)]
        marks.append((low_rim,))
    key_grad, value_grad = finish(places, results[1], results[2], rims)

    if cube:

        def join(value, got, bit):
            return jnp.where(
                bit == 0, jnp.concatenate([value, got], 0), jnp.concatenate([got, value], 0)
            )

        keep, other = sum_and_cut(places, None, chip_keep, chip_got)
        keep, other = sum_and_cut(places, 2, keep, swap_by_core(other, (2, 1)), marks[0])
        keep, other = sum_and_cut(places, 3, keep, swap(other, 0, 2), marks[1])
        line = sum_whole(places, keep, swap(other, 0, 4), marks[2])
        line = join(line, swap(line, 0, 4), places[3])
        line = join(line, swap(line, 0, 2), places[2])
        mate = swap(line, 0, 1)
        weight_grad = jnp.where(
            core == 0, jnp.concatenate([line, mate], 1), jnp.concatenate([mate, line], 1)
        ).astype(jnp.float32)
    else:
        summed = lax.psum_scatter(
            jnp.einsum("th,td->hd", rows, grads, preferred_element_type=jnp.float32),
            ("dp", "seq"),
            scatter_dimension=0,
            tiled=True,
        )
        weight_grad = lax.all_gather(summed, "seq", axis=0, tiled=True)
    return (results[0][None], key_grad[None], value_grad[None], weight_grad)


def solution(mesh):
    token = P("dp", "seq", None)
    return jax.shard_map(
        body,
        mesh=mesh,
        in_specs=(token,) * 4
        + (P("dp", None, "seq"), token, P("dp", None), P("dp", None, None)),
        out_specs=(token, token, token, P("dp", None)),
        check_vma=False,
    )
```

time: 265 us -> 252 us (0.951)
  starting transfers between devices: 63.9 us -> 53.8 us
  Pallas kernels: 106 us -> 111 us
  local copies, waits for them, and re-layouts: 17.4 us -> 13.6 us
  other arithmetic: 12.3 us -> 9.08 us
    ppermute x17 -> x14, waiting for transfers between devices: 63 us -> 46.9 us  [send(): return lax.ppermute(value, ('dp', 'seq'), pairs)]
    ppermute x12 -> x10, waiting for transfers between devices: 0.03 us -> 15.4 us  [along(): return lax.ppermute(value, 'seq', pairs)]
    pallas_call x4 -> x6, Pallas kernels: 17.6 us -> 27.5 us  [the longest x4 17.3 us: sum_and_cut(): pl.pallas_call(functools.partial(sum_kernel, len(after)), grid_spec=pltpu...]
    ppermute x12 -> x10, starting transfers between devices: 37.7 us -> 28.3 us  [along(): return lax.ppermute(value, 'seq', pairs)]
    pallas_call x2, Pallas kernels: 21.4 us -> 17 us  [weight_part(): pl.pallas_call(weight_kernel, grid_spec=pltpu.PrefetchScalarGridSpec(num_...]
    convert_element_type x3 -> x0, other arithmetic: 3.8 us -> none  [the longest x1 3.58 us: body(): half = total.astype(jnp.bfloat16)]
    slice x3 -> x0, local copies, waits for them, and re-layouts: 3.59 us -> none  [the longest x1 1.32 us: body(): values[:TILE]]
    ppermute x17 -> x14, starting transfers between devices: 26.2 us -> 25.5 us  [send(): return lax.ppermute(value, ('dp', 'seq'), pairs)]
  transfers between devices with their start and end apart: 29 -> 24, of which waited for: 6 -> 8; matrix products, arithmetic and copies ran while one was open for 6% -> 4% of each run, Pallas kernels for 36% -> 38%
where the time goes in v1:
time: 252 us; the launch traced here: 251 us
  Pallas kernels  111 us (44%)
  waiting for transfers between devices  62.3 us (25%)
  starting transfers between devices  53.8 us (21%)
  local copies, waits for them, and re-layouts  13.6 us (5%)
  other arithmetic  9.08 us (4%)
    pallas_call x4, Pallas kernels, attend(): pl.pallas_call(functools.partial(attend_kernel, 1.0 / math.sqrt(HD), len(...  66.6 us
    ppermute x14, waiting for transfers between devices, send(): return lax.ppermute(value, ('dp', 'seq'), pairs)  46.9 us
    ppermute x10, starting transfers between devices, along(): return lax.ppermute(value, 'seq', pairs)  28.3 us
    ppermute x14, starting transfers between devices, send(): return lax.ppermute(value, ('dp', 'seq'), pairs)  25.5 us
    pallas_call x4, Pallas kernels, sum_and_cut(): pl.pallas_call(functools.partial(sum_kernel, len(after)), grid_spec=pltpu...  17.3 us
    pallas_call x2, Pallas kernels, weight_part(): pl.pallas_call(weight_kernel, grid_spec=pltpu.PrefetchScalarGridSpec(num_...  17 us
    ppermute x10, waiting for transfers between devices, along(): return lax.ppermute(value, 'seq', pairs)  15.4 us
    unnamed x41, local copies, waits for them, and re-layouts  8.85 us
  transfers between devices with their start and end apart: 24, of which 8 were waited for; matrix products, arithmetic and copies ran while one was open for 4% of the time, Pallas kernels for 38%

profile of v1, /device:TPU:1, one launch (start us, length us, event | category | flops | bytes accessed | tf_op | source)
XLA Modules:
  0.0 251.0 jit_solution(7053951843778186705)
XLA Ops:
  2.2 8.5 %shard_map.112 = bf16[4,384,1536]{2,1,0:T(8,128)(2,1)} custom-call(s32[10]{0:T(128)} %concatenate.21.places, bf16[768,1536]{1,0:T(8,128)(2,1)} %bitcast.37, bf16[768,3072]{1,0:T(8,128)(2,1)} %bitcast.27), custom_call_target="tpu_custom_call" | custom-call | flops 3623878656 | bytes 9437184 | tf_op jit(solution)/shard_map/pallas_call | solution.py:38
  10.7 8.5 %shard_map.111 = bf16[4,384,1536]{2,1,0:T(8,128)(2,1)} custom-call(s32[10]{0:T(128)} %concatenate.21.places, bf16[768,1536]{1,0:T(8,128)(2,1)} %bitcast.38, bf16[768,3072]{1,0:T(8,128)(2,1)} %bitcast.28), custom_call_target="tpu_custom_call" | custom-call | flops 3623878656 | bytes 9437184 | tf_op jit(solution)/shard_map/pallas_call | solution.py:38
  19.2 2.2 copy-done.2
  21.4 6.9 %shard_map.113 = (bf16[768,1536]{1,0:T(8,128)(2,1)}, bf16[768,1536]{1,0:T(8,128)(2,1)}) custom-call(s32[10]{0:T(128)} %concatenate.21.places, bf16[1536,1536]{1,0:T(8,128)(2,1)} %bitcast.17, bf16[1536,1536]{1,0:T(8,128)(2,1)} %bitcast.15, bf16[1536,1536]{1,0:T(8,128)(2,1)} %bitcast.18, bf16[1536,1536]{1,0:T(8,128)(2,1)} %bitcast.16), custom_call_target="tpu_custom_call" | custom-call | flops 2359296 | bytes 14155776 | tf_op jit(solution)/shard_map/pallas_call | solution.py:101
  28.3 2.7 %collective-permute-start.17 = (bf16[768,1536]{1,0:T(8,128)(2,1)}, bf16[768,1536]{1,0:T(8,128)(2,1)S(1)}, u32[]{:S(2)}, u32[]{:S(2)}) collective-permute-start(bf16[768,1536]{1,0:T(8,128)(2,1)} %get-tuple-element.34.refs_9_), channel_id=1, source_target_pairs={{0,8},{1,17},{2,10},{3,19},{4,12},{5,21},{6,14},{7,23},{8,0},{9,25... | collective-permute-start | bytes 7077896 | tf_op jit(solution)/shard_map/ppermute | solution.py:326
  31.0 2.6 %fusion.1 = (bf16[1,384,1536]{2,1,0:T(8,128)(2,1)S(1)}, bf16[1,384,1536]{2,1,0:T(8,128)(2,1)S(1)}, bf16[1,384,1536]{2,1,0:T(8,128)(2,1)S(1)}, bf16[1,384,1536]{2,1,0:T(8,128)(2,1)S(1)}) fusion(bf16[1,768,1536]{2,1,0:T(8,128)(2,1)} %param.9, bf16[1,768,1536]{2,1,0:T(8,128)(2,1)} %param.10), kind=kLoop, calls=%fused_computation.10 | loop fusion | bytes 9437184 | tf_op jit(solution)/shard_map/slice | solution.py:349
  33.6 1.6 pad_maximum_fusion
  35.2 3.3 %collective-permute-start.4 = (bf16[2,384,1536]{2,1,0:T(8,128)(2,1)}, bf16[2,384,1536]{2,1,0:T(8,128)(2,1)}, u32[]{:S(2)}, u32[]{:S(2)}) collective-permute-start(bf16[2,384,1536]{2,1,0:T(8,128)(2,1)} %pad_maximum_fusion), channel_id=1, source_target_pairs={{0,1},{1,2},{2,3},{3,4},{4,5},{5,6},{6,7},{8,9},{9,10},{10,11},{11... | collective-permute-start | bytes 7077896 | tf_op jit(solution)/shard_map/ppermute | solution.py:336
  38.6 1.6 pad_maximum_fusion.1
  40.2 2.4 collective-permute-start.5
  42.6 1.4 constant_dynamic-slice_fusion
  44.0 1.3 collective-permute-start
  45.5 26.7 %collective-permute-done.refs_0_ = bf16[192,3072]{1,0:T(8,128)(2,1)} collective-permute-done((bf16[192,3072]{1,0:T(8,128)(2,1)S(1)}, bf16[192,3072]{1,0:T(8,128)(2,1)}, u32[]{:S(2)}, u32[]{:S(2)}) %collective-permute-start) | collective-permute-done | bytes 1179680 | tf_op jit(solution)/shard_map/ppermute | solution.py:326
  72.2 11.5 %collective-permute-start.7 = (bf16[192,3072]{1,0:T(8,128)(2,1)}, bf16[192,3072]{1,0:T(8,128)(2,1)}, u32[]{:S(2)}, u32[]{:S(2)}) collective-permute-start(bf16[192,3072]{1,0:T(8,128)(2,1)} %collective-permute-done.refs_0_), channel_id=1, source_target_pairs={{0,1},{1,0},{2,3},{3,2},{4,5},{5,4},{6,7},{7,6},{8,9},{9,8},{10,11... | collective-permute-start | bytes 3538952 | tf_op jit(solution)/shard_map/ppermute | solution.py:326
  83.7 1.4 copy-done.3
  85.1 4.2 %shard_map.119 = (bf16[384,1536]{1,0:T(8,128)(2,1)}, bf16[384,1536]{1,0:T(8,128)(2,1)}) custom-call(s32[10]{0:T(128)} %concatenate.21.places, bf16[768,1536]{1,0:T(8,128)(2,1)} %get-tuple-element.57.refs_0_.refs_2_, bf16[768,1536]{1,0:T(8,128)(2,1)} %copy-done.3, bf16[768,1536]{1,0:T(8,128)(2,1)} %get-tuple-element.57.refs_0_.refs_2_, ...), custom_call_target="tpu_custom_call" | custom-call | flops 1179648 | bytes 7077888 | tf_op jit(solution)/shard_map/pallas_call | solution.py:101
  89.3 1.7 collective-permute-start.18
  91.0 1.4 broadcast_select_fusion
  92.9 16.5 %shard_map.114 = (bf16[768,1536]{1,0:T(8,128)(2,1)}, bf16[768,1536]{1,0:T(8,128)(2,1)}, bf16[768,1536]{1,0:T(8,128)(2,1)}, bf16[2,384,384]{2,1,0:T(8,128)(2,1)}, bf16[2,384,384]{2,1,0:T(8,128)(2,1)}) custom-call(s32[10]{0:T(128)} %concatenate.21.places, bf16[384,3072]{1,0:T(8,128)(2,1)} %refs_0_.1, bf16[768,3072]{1,0:T(8,128)(2,1)} %bitcast.29, ...), custom_call_target="tpu_custom_call" | custom-call | flops 8606711808 | bytes 14155776 | tf_op jit(solution)/shard_map/pallas_call | solution.py:226
  109.4 3.5 %collective-permute-start.9 = (bf16[2,384,384]{2,1,0:T(8,128)(2,1)}, bf16[2,384,384]{2,1,0:T(8,128)(2,1)S(1)}, u32[]{:S(2)}, u32[]{:S(2)}) collective-permute-start(bf16[2,384,384]{2,1,0:T(8,128)(2,1)} %get-tuple-element.41), channel_id=1, source_target_pairs={{0,1},{1,2},{2,3},{3,4},{4,5},{5,6},{6,7},{8,9},{9,10},{10,11},{11... | collective-permute-start | bytes 1769480 | tf_op jit(solution)/shard_map/ppermute | solution.py:336
  113.0 2.1 collective-permute-start.10
  115.1 3.4 %shard_map.120 = (bf16[192,1536]{1,0:T(8,128)(2,1)}, bf16[192,1536]{1,0:T(8,128)(2,1)}) custom-call(s32[10]{0:T(128)} %concatenate.21.places, bf16[384,1536]{1,0:T(8,128)(2,1)} %get-tuple-element.58.refs_0_.refs_2_, bf16[384,1536]{1,0:T(8,128)(2,1)} %copy-done.4, bf16[384,1536]{1,0:T(8,128)(2,1)} %get-tuple-element.58.refs_0_.refs_2_, ...), custom_call_target="tpu_custom_call" | custom-call | flops 589824 | bytes 3538944 | tf_op jit(solution)/shard_map/pallas_call | solution.py:101
  118.5 1.3 collective-permute-start.19
  119.8 16.7 %shard_map.115 = (bf16[768,1536]{1,0:T(8,128)(2,1)}, bf16[768,1536]{1,0:T(8,128)(2,1)}, bf16[768,1536]{1,0:T(8,128)(2,1)}, bf16[2,384,384]{2,1,0:T(8,128)(2,1)}, bf16[2,384,384]{2,1,0:T(8,128)(2,1)}) custom-call(s32[10]{0:T(128)} %concatenate.21.places, ...), custom_call_target="tpu_custom_call", output_to_operand_aliasing={{0}: (11, {}), {1}: (12, {}), {2}: (13, {})} | custom-call | flops 8606711808 | bytes 14155776 | tf_op jit(solution)/shard_map/pallas_call | solution.py:226
  137.3 2.8 %shard_map.121 = (bf16[96,1536]{1,0:T(8,128)(2,1)}, bf16[96,1536]{1,0:T(8,128)(2,1)}) custom-call(s32[10]{0:T(128)} %concatenate.21.places, bf16[192,1536]{1,0:T(8,128)(2,1)} %get-tuple-element.60.refs_0_.refs_2_, bf16[192,1536]{1,0:T(8,128)(2,1)} %copy-done.5, bf16[192,1536]{1,0:T(8,128)(2,1)} %get-tuple-element.60.refs_0_.refs_2_, ...), custom_call_target="tpu_custom_call" | custom-call | flops 294912 | bytes 1769472 | tf_op jit(solution)/shard_map/pallas_call | solution.py:101
  140.1 1.7 collective-permute-start.20
  141.8 1.0 copy-done.17
  143.1 16.7 %shard_map.116 = (bf16[768,1536]{1,0:T(8,128)(2,1)}, bf16[768,1536]{1,0:T(8,128)(2,1)}, bf16[768,1536]{1,0:T(8,128)(2,1)}, bf16[2,384,384]{2,1,0:T(8,128)(2,1)}, bf16[2,384,384]{2,1,0:T(8,128)(2,1)}) custom-call(s32[10]{0:T(128)} %concatenate.21.places, ...), custom_call_target="tpu_custom_call", output_to_operand_aliasing={{0}: (11, {}), {1}: (12, {}), {2}: (13, {})} | custom-call | flops 8606711808 | bytes 14155776 | tf_op jit(solution)/shard_map/pallas_call | solution.py:226
  160.5 2.5 shard_map.122
  163.8 1.8 collective-permute-start.3
  165.5 13.3 %collective-permute-done.21 = bf16[96,1536]{1,0:T(8,128)(2,1)S(1)} collective-permute-done((bf16[96,1536]{1,0:T(8,128)(2,1)}, bf16[96,1536]{1,0:T(8,128)(2,1)S(1)}, u32[]{:S(2)}, u32[]{:S(2)}) %collective-permute-start.21) | collective-permute-done | bytes 294944 | tf_op jit(solution)/shard_map/ppermute | solution.py:326
  178.8 1.2 maximum_select_fusion.2
  180.1 4.6 %collective-permute-start.11 = (bf16[2,384,384]{2,1,0:T(8,128)(2,1)S(1)}, bf16[2,384,384]{2,1,0:T(8,128)(2,1)S(1)}, u32[]{:S(2)}, u32[]{:S(2)}) collective-permute-start(bf16[2,384,384]{2,1,0:T(8,128)(2,1)S(1)} %copy-done.19), channel_id=1, source_target_pairs={{0,1},{1,2},{2,3},{3,4},{4,5},{5,6},{6,7},{8,9},{9,10},{10,11},{11... | collective-permute-start | bytes 1769480 | tf_op jit(solution)/shard_map/ppermute | solution.py:336
  184.7 2.1 collective-permute-start.12
  186.9 6.9 %collective-permute-done.22 = bf16[192,1536]{1,0:T(8,128)(2,1)S(1)} collective-permute-done((bf16[192,1536]{1,0:T(8,128)(2,1)S(1)}, bf16[192,1536]{1,0:T(8,128)(2,1)S(1)}, u32[]{:S(2)}, u32[]{:S(2)}) %collective-permute-start.22) | collective-permute-done | bytes 589856 | tf_op jit(solution)/shard_map/ppermute | solution.py:326
  194.1 2.1 collective-permute-start.23
  196.2 3.3 %collective-permute-done.11.refs_13_.refs_2_ = bf16[2,384,384]{2,1,0:T(8,128)(2,1)S(1)} collective-permute-done((bf16[2,384,384]{2,1,0:T(8,128)(2,1)S(1)}, bf16[2,384,384]{2,1,0:T(8,128)(2,1)S(1)}, u32[]{:S(2)}, u32[]{:S(2)}) %collective-permute-start.11) | collective-permute-done | bytes 589856 | tf_op jit(solution)/shard_map/ppermute | solution.py:336
  199.5 1.9 collective-permute-done.12.refs_14_.refs_3_
  202.3 16.8 %shard_map.117 = (bf16[768,1536]{1,0:T(8,128)(2,1)}, bf16[768,1536]{1,0:T(8,128)(2,1)}, bf16[768,1536]{1,0:T(8,128)(2,1)}, bf16[2,384,384]{2,1,0:T(8,128)(2,1)}, bf16[2,384,384]{2,1,0:T(8,128)(2,1)}) custom-call(s32[10]{0:T(128)} %concatenate.21.places, ...), custom_call_target="tpu_custom_call", output_to_operand_aliasing={{0}: (11, {}), {1}: (12, {}), {2}: (13, {})} | custom-call | flops 8606711808 | bytes 14155776 | tf_op jit(solution)/shard_map/pallas_call | solution.py:226
  219.1 2.7 %collective-permute-start.15 = (bf16[2,384,384]{2,1,0:T(8,128)(2,1)}, bf16[2,384,384]{2,1,0:T(8,128)(2,1)S(1)}, u32[]{:S(2)}, u32[]{:S(2)}) collective-permute-start(bf16[2,384,384]{2,1,0:T(8,128)(2,1)} %get-tuple-element.53), channel_id=1, source_target_pairs={{0,1},{1,2},{2,3},{3,4},{4,5},{5,6},{6,7},{8,9},{9,10},{10,11},{11... | collective-permute-start | bytes 1769480 | tf_op jit(solution)/shard_map/ppermute | solution.py:336
  221.8 1.9 collective-permute-start.16
  223.7 3.6 %collective-permute-start.13 = (bf16[2,384,384]{2,1,0:T(8,128)(2,1)S(1)}, bf16[2,384,384]{2,1,0:T(8,128)(2,1)S(1)}, u32[]{:S(2)}, u32[]{:S(2)}) collective-permute-start(bf16[2,384,384]{2,1,0:T(8,128)(2,1)S(1)} %copy-done.18), channel_id=1, source_target_pairs={{0,1},{1,2},{2,3},{3,4},{4,5},{5,6},{6,7},{8,9},{9,10},{10,11},{11... | collective-permute-start | bytes 1769480 | tf_op jit(solution)/shard_map/ppermute | solution.py:336
  227.4 1.9 collective-permute-start.14
  229.3 3.9 %collective-permute-done.16.refs_7_ = bf16[2,384,384]{2,1,0:T(8,128)(2,1)S(1)} collective-permute-done((bf16[2,384,384]{2,1,0:T(8,128)(2,1)}, bf16[2,384,384]{2,1,0:T(8,128)(2,1)S(1)}, u32[]{:S(2)}, u32[]{:S(2)}) %collective-permute-start.16) | collective-permute-done | bytes 589856 | tf_op jit(solution)/shard_map/ppermute | solution.py:336
  233.2 1.9 collective-permute-done.13.refs_4_
  235.1 4.4 %collective-permute-done.14.refs_5_ = bf16[2,384,384]{2,1,0:T(8,128)(2,1)S(1)} collective-permute-done((bf16[2,384,384]{2,1,0:T(8,128)(2,1)S(1)}, bf16[2,384,384]{2,1,0:T(8,128)(2,1)S(1)}, u32[]{:S(2)}, u32[]{:S(2)}) %collective-permute-start.14) | collective-permute-done | bytes 589856 | tf_op jit(solution)/shard_map/ppermute | solution.py:336
  240.3 7.7 %shard_map.118 = (bf16[768,1536]{1,0:T(8,128)(2,1)}, bf16[768,1536]{1,0:T(8,128)(2,1)}) custom-call(s32[10]{0:T(128)} %concatenate.21.places, bf16[768,1536]{1,0:T(8,128)(2,1)} %get-tuple-element.49.dk_ref, bf16[768,1536]{1,0:T(8,128)(2,1)} %get-tuple-element.50.dv_ref, bf16[2,384,384]{2,1,0:T(8,128)(2,1)} %copy-done.6, bf16[2,384,384]{2,1,0:T(8,128)(2,1)} %copy-done.7, ...), custom_call_target="tpu_custom_call" | custom-call | flops 4718592 | bytes 14155776 | tf_op jit(solution)/shard_map/pallas_call | solution.py:284
  248.1 2.9 %fusion = f32[384,3072]{1,0:T(8,128)} fusion(bf16[384,1536]{1,0:T(8,128)(2,1)S(1)} %collective-permute-done.23, bf16[384,1536]{1,0:T(8,128)(2,1)S(1)} %maximum_select_fusion.1, pred[]{:T(512)S(6)} %eq.13), kind=kLoop, calls=%fused_computation.3 | loop fusion | flops 11796480 | bytes 7077889 | tf_op jit(solution)/shard_map/convert_element_type | solution.py:387
  (65 shorter events, 7.0 us)
Async XLA Ops:
  0.6 0.7 copy-start
  10.7 8.6 %collective-permute-start.8 = (bf16[4,384,1536]{2,1,0:T(8,128)(2,1)}, bf16[4,384,1536]{2,1,0:T(8,128)(2,1)S(1)}, u32[]{:S(2)}, u32[]{:S(2)}) collective-permute-start(bf16[4,384,1536]{2,1,0:T(8,128)(2,1)} %shard_map.112), channel_id=1, source_target_pairs={{0,1},{1,0},{2,3},{3,2},{4,5},{5,4},{6,7},{7,6},{8,9},{9,8},{10,11... | collective-permute-start | bytes 14155784 | tf_op jit(solution)/shard_map/ppermute | solution.py:326
  19.2 2.2 copy-start.2
  28.3 55.4 %collective-permute-start.17 = (bf16[768,1536]{1,0:T(8,128)(2,1)}, bf16[768,1536]{1,0:T(8,128)(2,1)S(1)}, u32[]{:S(2)}, u32[]{:S(2)}) collective-permute-start(bf16[768,1536]{1,0:T(8,128)(2,1)} %get-tuple-element.34.refs_9_), channel_id=1, source_target_pairs={{0,8},{1,17},{2,10},{3,19},{4,12},{5,21},{6,14},{7,23},{8,0},{9,25... | collective-permute-start | bytes 7077896 | tf_op jit(solution)/shard_map/ppermute | solution.py:326
  35.2 57.3 %collective-permute-start.4 = (bf16[2,384,1536]{2,1,0:T(8,128)(2,1)}, bf16[2,384,1536]{2,1,0:T(8,128)(2,1)}, u32[]{:S(2)}, u32[]{:S(2)}) collective-permute-start(bf16[2,384,1536]{2,1,0:T(8,128)(2,1)} %pad_maximum_fusion), channel_id=1, source_target_pairs={{0,1},{1,2},{2,3},{3,4},{4,5},{5,6},{6,7},{8,9},{9,10},{10,11},{11... | collective-permute-start | bytes 7077896 | tf_op jit(solution)/shard_map/ppermute | solution.py:336
  40.2 52.7 %collective-permute-start.5 = (bf16[2,384,1536]{2,1,0:T(8,128)(2,1)}, bf16[2,384,1536]{2,1,0:T(8,128)(2,1)}, u32[]{:S(2)}, u32[]{:S(2)}) collective-permute-start(bf16[2,384,1536]{2,1,0:T(8,128)(2,1)} %pad_maximum_fusion.1), channel_id=1, source_target_pairs={{1,0},{2,1},{3,2},{4,3},{5,4},{6,5},{7,6},{9,8},{10,9},{11,10},{12... | collective-permute-start | bytes 7077896 | tf_op jit(solution)/shard_map/ppermute | solution.py:336
  44.0 28.2 %collective-permute-start = (bf16[192,3072]{1,0:T(8,128)(2,1)S(1)}, bf16[192,3072]{1,0:T(8,128)(2,1)}, u32[]{:S(2)}, u32[]{:S(2)}) collective-permute-start(bf16[192,3072]{1,0:T(8,128)(2,1)S(1)} %constant_dynamic-slice_fusion), channel_id=1, source_target_pairs={{0,8},{1,9},{2,10},{3,11},{4,12},{5,13},{6,14},{7,15},{8,0},{9,1},... | collective-permute-start | bytes 3538952 | tf_op jit(solution)/shard_map/ppermute | solution.py:326
  45.2 45.8 %collective-permute-start.1 = (bf16[192,3072]{1,0:T(8,128)(2,1)S(1)}, bf16[192,3072]{1,0:T(8,128)(2,1)}, u32[]{:S(2)}, u32[]{:S(2)}) collective-permute-start(bf16[192,3072]{1,0:T(8,128)(2,1)S(1)} %constant_dynamic-slice_fusion), channel_id=1, source_target_pairs={{0,16},{1,17},{2,18},{3,19},{4,20},{5,21},{6,22},{7,23},{8,24},{9,... | collective-permute-start | bytes 3538952 | tf_op jit(solution)/shard_map/ppermute | solution.py:326
  72.2 46.3 %collective-permute-start.7 = (bf16[192,3072]{1,0:T(8,128)(2,1)}, bf16[192,3072]{1,0:T(8,128)(2,1)}, u32[]{:S(2)}, u32[]{:S(2)}) collective-permute-start(bf16[192,3072]{1,0:T(8,128)(2,1)} %collective-permute-done.refs_0_), channel_id=1, source_target_pairs={{0,1},{1,0},{2,3},{3,2},{4,5},{5,4},{6,7},{7,6},{8,9},{9,8},{10,11... | collective-permute-start | bytes 3538952 | tf_op jit(solution)/shard_map/ppermute | solution.py:326
  83.7 1.4 copy-start.3
  89.3 23.7 %collective-permute-start.18 = (bf16[384,1536]{1,0:T(8,128)(2,1)}, bf16[384,1536]{1,0:T(8,128)(2,1)S(1)}, u32[]{:S(2)}, u32[]{:S(2)}) collective-permute-start(bf16[384,1536]{1,0:T(8,128)(2,1)} %get-tuple-element.59), channel_id=1, source_target_pairs={{0,16},{1,9},{2,18},{3,11},{4,20},{5,13},{6,22},{7,15},{8,24},{9,1... | collective-permute-start | bytes 3538952 | tf_op jit(solution)/shard_map/ppermute | solution.py:326
  92.4 71.3 %collective-permute-start.2 = (bf16[192,3072]{1,0:T(8,128)(2,1)S(1)}, bf16[192,3072]{1,0:T(8,128)(2,1)}, u32[]{:S(2)}, u32[]{:S(2)}) collective-permute-start(bf16[192,3072]{1,0:T(8,128)(2,1)S(1)} %broadcast_select_fusion), channel_id=1, source_target_pairs={{0,16},{1,9},{2,18},{3,11},{4,20},{5,13},{6,22},{7,15},{8,24},{9,1... | collective-permute-start | bytes 3538952 | tf_op jit(solution)/shard_map/ppermute | solution.py:326
  92.5 49.2 %collective-permute-start.6 = (bf16[192,3072]{1,0:T(8,128)(2,1)}, bf16[192,3072]{1,0:T(8,128)(2,1)S(1)}, u32[]{:S(2)}, u32[]{:S(2)}) collective-permute-start(bf16[192,3072]{1,0:T(8,128)(2,1)} %collective-permute-done.1.refs_0_), channel_id=1, source_target_pairs={{0,1},{1,0},{2,3},{3,2},{4,5},{5,4},{6,7},{7,6},{8,9},{9,8},{10,11... | collective-permute-start | bytes 3538952 | tf_op jit(solution)/shard_map/ppermute | solution.py:326
  109.4 32.4 %collective-permute-start.9 = (bf16[2,384,384]{2,1,0:T(8,128)(2,1)}, bf16[2,384,384]{2,1,0:T(8,128)(2,1)S(1)}, u32[]{:S(2)}, u32[]{:S(2)}) collective-permute-start(bf16[2,384,384]{2,1,0:T(8,128)(2,1)} %get-tuple-element.41), channel_id=1, source_target_pairs={{0,1},{1,2},{2,3},{3,4},{4,5},{5,6},{6,7},{8,9},{9,10},{10,11},{11... | collective-permute-start | bytes 1769480 | tf_op jit(solution)/shard_map/ppermute | solution.py:336
  113.0 2.1 copy-start.4
  113.0 28.8 %collective-permute-start.10 = (bf16[2,384,384]{2,1,0:T(8,128)(2,1)}, bf16[2,384,384]{2,1,0:T(8,128)(2,1)S(1)}, u32[]{:S(2)}, u32[]{:S(2)}) collective-permute-start(bf16[2,384,384]{2,1,0:T(8,128)(2,1)} %get-tuple-element.42.refs_4_), channel_id=1, source_target_pairs={{1,0},{2,1},{3,2},{4,3},{5,4},{6,5},{7,6},{9,8},{10,9},{11,10},{12... | collective-permute-start | bytes 1769480 | tf_op jit(solution)/shard_map/ppermute | solution.py:336
  118.5 18.0 %collective-permute-start.19 = (bf16[192,1536]{1,0:T(8,128)(2,1)}, bf16[192,1536]{1,0:T(8,128)(2,1)S(1)}, u32[]{:S(2)}, u32[]{:S(2)}) collective-permute-start(bf16[192,1536]{1,0:T(8,128)(2,1)} %get-tuple-element.61), channel_id=1, source_target_pairs={{0,2},{1,3},{2,0},{3,1},{4,6},{5,7},{6,4},{7,5},{8,10},{9,11},{10,... | collective-permute-start | bytes 1769480 | tf_op jit(solution)/shard_map/ppermute | solution.py:326
  136.5 0.8 copy-start.5
  140.1 19.7 %collective-permute-start.20 = (bf16[96,1536]{1,0:T(8,128)(2,1)}, bf16[96,1536]{1,0:T(8,128)(2,1)S(1)}, u32[]{:S(2)}, u32[]{:S(2)}) collective-permute-start(bf16[96,1536]{1,0:T(8,128)(2,1)} %get-tuple-element.63), channel_id=1, source_target_pairs={{0,4},{1,5},{2,6},{3,7},{4,0},{5,1},{6,2},{7,3},{8,12},{9,13},{10,... | collective-permute-start | bytes 884744 | tf_op jit(solution)/shard_map/ppermute | solution.py:326
  141.7 1.0 copy-start.17
  141.8 1.2 copy-start.6
  141.8 1.3 copy-start.7
  159.8 20.3 %copy-start.19 = (bf16[2,384,384]{2,1,0:T(8,128)(2,1)S(1)}, bf16[2,384,384]{2,1,0:T(8,128)(2,1)}, u32[]{:S(2)}) copy-start(bf16[2,384,384]{2,1,0:T(8,128)(2,1)} %get-tuple-element.46) | copy-start | bytes 1769476
  159.8 24.9 %copy-start.15 = (bf16[2,384,384]{2,1,0:T(8,128)(2,1)S(1)}, bf16[2,384,384]{2,1,0:T(8,128)(2,1)}, u32[]{:S(2)}) copy-start(bf16[2,384,384]{2,1,0:T(8,128)(2,1)} %get-tuple-element.47.refs_4_) | copy-start | bytes 1769476
  159.8 0.7 copy-start.16
  163.0 15.8 %collective-permute-start.21 = (bf16[96,1536]{1,0:T(8,128)(2,1)}, bf16[96,1536]{1,0:T(8,128)(2,1)S(1)}, u32[]{:S(2)}, u32[]{:S(2)}) collective-permute-start(bf16[96,1536]{1,0:T(8,128)(2,1)} %shard_map.122), channel_id=1, source_target_pairs={{0,4},{1,5},{2,6},{3,7},{4,0},{5,1},{6,2},{7,3},{8,12},{9,13},{10,... | collective-permute-start | bytes 884744 | tf_op jit(solution)/shard_map/ppermute | solution.py:326
  163.8 32.5 %collective-permute-start.3 = (bf16[192,3072]{1,0:T(8,128)(2,1)}, bf16[192,3072]{1,0:T(8,128)(2,1)}, u32[]{:S(2)}, u32[]{:S(2)}) collective-permute-start(bf16[192,3072]{1,0:T(8,128)(2,1)} %collective-permute-done.2.refs_0_), channel_id=1, source_target_pairs={{0,1},{1,0},{2,3},{3,2},{4,5},{5,4},{6,7},{7,6},{8,9},{9,8},{10,11... | collective-permute-start | bytes 3538952 | tf_op jit(solution)/shard_map/ppermute | solution.py:326
  180.0 13.8 %collective-permute-start.22 = (bf16[192,1536]{1,0:T(8,128)(2,1)S(1)}, bf16[192,1536]{1,0:T(8,128)(2,1)S(1)}, u32[]{:S(2)}, u32[]{:S(2)}) collective-permute-start(bf16[192,1536]{1,0:T(8,128)(2,1)S(1)} %maximum_select_fusion.2), channel_id=1, source_target_pairs={{0,2},{1,3},{2,0},{3,1},{4,6},{5,7},{6,4},{7,5},{8,10},{9,11},{10,... | collective-permute-start | bytes 1769480 | tf_op jit(solution)/shard_map/ppermute | solution.py:326
  180.1 19.5 %collective-permute-start.11 = (bf16[2,384,384]{2,1,0:T(8,128)(2,1)S(1)}, bf16[2,384,384]{2,1,0:T(8,128)(2,1)S(1)}, u32[]{:S(2)}, u32[]{:S(2)}) collective-permute-start(bf16[2,384,384]{2,1,0:T(8,128)(2,1)S(1)} %copy-done.19), channel_id=1, source_target_pairs={{0,1},{1,2},{2,3},{3,4},{4,5},{5,6},{6,7},{8,9},{9,10},{10,11},{11... | collective-permute-start | bytes 1769480 | tf_op jit(solution)/shard_map/ppermute | solution.py:336
  184.7 16.7 %collective-permute-start.12 = (bf16[2,384,384]{2,1,0:T(8,128)(2,1)S(1)}, bf16[2,384,384]{2,1,0:T(8,128)(2,1)S(1)}, u32[]{:S(2)}, u32[]{:S(2)}) collective-permute-start(bf16[2,384,384]{2,1,0:T(8,128)(2,1)S(1)} %copy-done.15), channel_id=1, source_target_pairs={{1,0},{2,1},{3,2},{4,3},{5,4},{6,5},{7,6},{9,8},{10,9},{11,10},{12... | collective-permute-start | bytes 1769480 | tf_op jit(solution)/shard_map/ppermute | solution.py:336
  194.1 53.9 %collective-permute-start.23 = (bf16[384,1536]{1,0:T(8,128)(2,1)S(1)}, bf16[384,1536]{1,0:T(8,128)(2,1)S(1)}, u32[]{:S(2)}, u32[]{:S(2)}) collective-permute-start(bf16[384,1536]{1,0:T(8,128)(2,1)S(1)} %maximum_select_fusion.1), channel_id=1, source_target_pairs={{0,1},{1,0},{2,3},{3,2},{4,5},{5,4},{6,7},{7,6},{8,9},{9,8},{10,11... | collective-permute-start | bytes 3538952 | tf_op jit(solution)/shard_map/ppermute | solution.py:326
  199.5 1.9 copy-start.8
  201.4 0.8 copy-start.9
  202.2 21.4 %copy-start.18 = (bf16[2,384,384]{2,1,0:T(8,128)(2,1)S(1)}, bf16[2,384,384]{2,1,0:T(8,128)(2,1)}, u32[]{:S(2)}) copy-start(bf16[2,384,384]{2,1,0:T(8,128)(2,1)} %get-tuple-element.51) | copy-start | bytes 1769476
  202.2 25.1 %copy-start.14 = (bf16[2,384,384]{2,1,0:T(8,128)(2,1)S(1)}, bf16[2,384,384]{2,1,0:T(8,128)(2,1)}, u32[]{:S(2)}) copy-start(bf16[2,384,384]{2,1,0:T(8,128)(2,1)} %get-tuple-element.52.refs_0_) | copy-start | bytes 1769476
  219.1 10.2 %collective-permute-start.15 = (bf16[2,384,384]{2,1,0:T(8,128)(2,1)}, bf16[2,384,384]{2,1,0:T(8,128)(2,1)S(1)}, u32[]{:S(2)}, u32[]{:S(2)}) collective-permute-start(bf16[2,384,384]{2,1,0:T(8,128)(2,1)} %get-tuple-element.53), channel_id=1, source_target_pairs={{0,1},{1,2},{2,3},{3,4},{4,5},{5,6},{6,7},{8,9},{9,10},{10,11},{11... | collective-permute-start | bytes 1769480 | tf_op jit(solution)/shard_map/ppermute | solution.py:336
  221.8 11.4 %collective-permute-start.16 = (bf16[2,384,384]{2,1,0:T(8,128)(2,1)}, bf16[2,384,384]{2,1,0:T(8,128)(2,1)S(1)}, u32[]{:S(2)}, u32[]{:S(2)}) collective-permute-start(bf16[2,384,384]{2,1,0:T(8,128)(2,1)} %get-tuple-element.54), channel_id=1, source_target_pairs={{1,0},{2,1},{3,2},{4,3},{5,4},{6,5},{7,6},{9,8},{10,9},{11,10},{12... | collective-permute-start | bytes 1769480 | tf_op jit(solution)/shard_map/ppermute | solution.py:336
  223.7 11.4 %collective-permute-start.13 = (bf16[2,384,384]{2,1,0:T(8,128)(2,1)S(1)}, bf16[2,384,384]{2,1,0:T(8,128)(2,1)S(1)}, u32[]{:S(2)}, u32[]{:S(2)}) collective-permute-start(bf16[2,384,384]{2,1,0:T(8,128)(2,1)S(1)} %copy-done.18), channel_id=1, source_target_pairs={{0,1},{1,2},{2,3},{3,4},{4,5},{5,6},{6,7},{8,9},{9,10},{10,11},{11... | collective-permute-start | bytes 1769480 | tf_op jit(solution)/shard_map/ppermute | solution.py:336
  227.4 12.1 %collective-permute-start.14 = (bf16[2,384,384]{2,1,0:T(8,128)(2,1)S(1)}, bf16[2,384,384]{2,1,0:T(8,128)(2,1)S(1)}, u32[]{:S(2)}, u32[]{:S(2)}) collective-permute-start(bf16[2,384,384]{2,1,0:T(8,128)(2,1)S(1)} %copy-done.14), channel_id=1, source_target_pairs={{1,0},{2,1},{3,2},{4,3},{5,4},{6,5},{7,6},{9,8},{10,9},{11,10},{12... | collective-permute-start | bytes 1769480 | tf_op jit(solution)/shard_map/ppermute | solution.py:336
  229.3 10.2 %copy-start.10 = (bf16[2,384,384]{2,1,0:T(8,128)(2,1)}, bf16[2,384,384]{2,1,0:T(8,128)(2,1)S(1)}, u32[]{:S(2)}) copy-start(bf16[2,384,384]{2,1,0:T(8,128)(2,1)S(1)} %collective-permute-done.15.refs_6_) | copy-start | bytes 1769476
  233.2 6.3 %copy-start.11 = (bf16[2,384,384]{2,1,0:T(8,128)(2,1)}, bf16[2,384,384]{2,1,0:T(8,128)(2,1)S(1)}, u32[]{:S(2)}) copy-start(bf16[2,384,384]{2,1,0:T(8,128)(2,1)S(1)} %collective-permute-done.16.refs_7_) | copy-start | bytes 1769476
  235.1 4.4 %copy-start.12 = (bf16[2,384,384]{2,1,0:T(8,128)(2,1)}, bf16[2,384,384]{2,1,0:T(8,128)(2,1)S(1)}, u32[]{:S(2)}) copy-start(bf16[2,384,384]{2,1,0:T(8,128)(2,1)S(1)} %collective-permute-done.13.refs_4_) | copy-start | bytes 1769476
  239.5 0.8 copy-start.13
  240.3 10.6 %copy-start.1 = (s32[1,16,3]{1,0,2:T(1,128)S(1)}, s32[1,16,3]{1,0,2:T(1,128)}, u32[]{:S(2)}) copy-start(s32[1,16,3]{1,0,2:T(1,128)} %param.15) | copy-start | bytes 580

commit v2 on v1

--- a/solution.py
+++ b/solution.py
@@ -87,6 +87,32 @@
     )(places, a, b, *after)
 
 
+def join_kernel(bit, count, places, mine_ref, other_ref, *refs):
+    rows = mine_ref.shape[0]
+    at = places[bit]
+    refs[count][pl.ds(pl.multiple_of(at * rows, rows), rows)] = mine_ref[...]
+    refs[count][pl.ds(pl.multiple_of((1 - at) * rows, rows), rows)] = other_ref[...]
+
+
+def join(places, bit, mine, other, after):
+    rows, wide = mine.shape
+    whole = pl.BlockSpec((rows, wide), lambda i, at: (0, 0))
+    return pl.pallas_call(
+        functools.partial(join_kernel, bit, len(after)),
+        grid_spec=pltpu.PrefetchScalarGridSpec(
+            num_scalar_prefetch=1,
+            grid=(1,),
+            in_specs=[whole, whole] + [pl.BlockSpec(memory_space=pl.ANY)] * len(after),
+            out_specs=pl.BlockSpec((2 * rows, wide), lambda i, at: (0, 0)),
+        ),
+        out_shape=jax.ShapeDtypeStruct((2 * rows, wide), mine.dtype),
+        compiler_params=pltpu.CompilerParams(vmem_limit_bytes=VMEM),
+        cost_estimate=pl.CostEstimate(
+            flops=mine.size, bytes_accessed=8 * mine.size, transcendentals=0
+        ),
+    )(places, mine, other, *after)
+
+
 def sum_and_cut(places, bit, a, b, after=()):
     size, wide = a.shape[0] // 2, a.shape[1]
     chunk = min(size, 192)
@@ -120,7 +146,7 @@
     (grad_ref, q_ref, o_ref, norm_ref, k_ref, v_ref, below_ref, above_ref) = refs[:8]
     refs = refs[8 + extra :]
     (dq_ref, dk_ref, dv_ref, low_ref, high_ref) = refs[:5]
-    (full, attn_grad, kwin, vwin, kflip, dk, dv) = refs[5:]
+    (full, attn_grad, kwin, vwin, kflip, kcat, vcat, fcat, dk, dv) = refs[5:]
     head = pl.program_id(0)
     tokens = q_ref.shape[0]
     tiles = tokens // TILE
@@ -156,32 +182,35 @@
     def rows_of(t):
         return slice(t * TILE, (t + 1) * TILE)
 
-    def products(t, n):
-        w = places[4 + t * 3 + n]
+    def products(t):
+        kept = [places[4 + t * 3 + n] for n in range(3)]
+        for n, w in enumerate(kept):
+            part = slice(n * TILE, (n + 1) * TILE)
+            kcat[t, part] = kwin[w]
+            vcat[t, part] = vwin[w]
+            fcat[t, :, part] = kflip[w]
         q, do = q_ref[rows_of(t)], attn_grad[head, rows_of(t)]
-        return w, mm(kwin[w], q, NT), mm(vwin[w], do, NT)
-
-    pieces = [(t, n) for t in range(tiles) for n in range(3)]
-    ahead = products(*pieces[0])
-    dq = None
-    for at, (t, n) in enumerate(pieces):
-        w, scores, prob = ahead
-        if at + 1 < len(pieces):
-            ahead = products(*pieces[at + 1])
+        return kept, mm(kcat[t], q, NT), mm(vcat[t], do, NT)
+
+    ahead = products(0)
+    for t in range(tiles):
+        kept, scores, prob = ahead
+        if t + 1 < tiles:
+            ahead = products(t + 1)
         rows = rows_of(t)
         q, do = q_ref[rows], attn_grad[head, rows]
-        if n == 0:
-            norm = norm_ref[0, :, rows] * log2e
-            both = do.astype(jnp.float32) * o_ref[rows].astype(jnp.float32)
-            delta = both.T.sum(0, keepdims=True)
+        norm = norm_ref[0, :, rows] * log2e
+        both = do.astype(jnp.float32) * o_ref[rows].astype(jnp.float32)
+        delta = both.T.sum(0, keepdims=True)
         p = jnp.exp2(scores * (scale * log2e) - norm)
         ds = (p * (prob - delta)).astype(jnp.bfloat16)
-        dv[w] += mm(p.astype(jnp.bfloat16), do)
-        dk[w] += mm(ds, q)
-        part = mm(kflip[w], ds)
-        dq = part if n == 0 else dq + part
-        if n == 2:
-            dq_ref[rows] = (dq * scale).T.astype(jnp.bfloat16)
+        dv_all = mm(p.astype(jnp.bfloat16), do)
+        dk_all = mm(ds, q)
+        dq_ref[rows] = (mm(fcat[t], ds) * scale).T.astype(jnp.bfloat16)
+        for n, w in enumerate(kept):
+            part = slice(n * TILE, (n + 1) * TILE)
+            dv[w] += dv_all[part]
+            dk[w] += dk_all[part]
     for t in range(tiles):
         dk_ref[rows_of(t)] = dk[t + 1].astype(jnp.bfloat16)
         dv_ref[rows_of(t)] = dv[t + 1].astype(jnp.bfloat16)
@@ -236,6 +265,9 @@
                 pltpu.VMEM((tiles + 2, TILE, HD), jnp.bfloat16),
                 pltpu.VMEM((tiles + 2, TILE, HD), jnp.bfloat16),
                 pltpu.VMEM((tiles + 2, HD, TILE), jnp.bfloat16),
+                pltpu.VMEM((tiles, kept * TILE, HD), jnp.bfloat16),
+                pltpu.VMEM((tiles, kept * TILE, HD), jnp.bfloat16),
+                pltpu.VMEM((tiles, HD, kept * TILE), jnp.bfloat16),
                 pltpu.VMEM((tiles + 2, TILE, HD), jnp.float32),
                 pltpu.VMEM((tiles + 2, TILE, HD), jnp.float32),
             ],
@@ -354,7 +386,7 @@
         wide = grads.shape[1] // 2
         sent = swap(weight_part(places, rows, grads, True), 0, 1).reshape(width, wide)
         mine = weight_part(places, rows, grads, False).reshape(width, wide)
-        chip_keep, chip_send = sum_and_cut(places, None, mine, sent)
+        chip_keep, chip_send = sum_and_cut(places, None, mine, sent, (by_x, by_y, *halos))
         chip_got = swap_by_core(chip_send, (1, 2))
         first_after = (chip_send,)
 
@@ -369,18 +401,11 @@
     key_grad, value_grad = finish(places, results[1], results[2], rims)
 
     if cube:
-
-        def join(value, got, bit):
-            return jnp.where(
-                bit == 0, jnp.concatenate([value, got], 0), jnp.concatenate([got, value], 0)
-            )
-
-        keep, other = sum_and_cut(places, None, chip_keep, chip_got)
-        keep, other = sum_and_cut(places, 2, keep, swap_by_core(other, (2, 1)), marks[0])
-        keep, other = sum_and_cut(places, 3, keep, swap(other, 0, 2), marks[1])
-        line = sum_whole(places, keep, swap(other, 0, 4), marks[2])
-        line = join(line, swap(line, 0, 4), places[3])
-        line = join(line, swap(line, 0, 2), places[2])
+        keep, other = sum_and_cut(places, None, chip_keep, chip_got, marks[0])
+        keep, other = sum_and_cut(places, 2, keep, swap_by_core(other, (2, 1)), marks[1])
+        pair = sum_whole(places, keep, swap(other, 0, 2), marks[2])
+        line = sum_whole(places, pair, swap(pair, 0, 4), (*marks[3], *rims[4:6]))
+        line = join(places, 2, line, swap(line, 0, 2), (key_grad,))
         mate = swap(line, 0, 1)
         weight_grad = jnp.where(
             core == 0, jnp.concatenate([line, mate], 1), jnp.concatenate([mate, line], 1)

time: 252 us -> 232 us (0.921)
  starting transfers between devices: 53.8 us -> 40 us
  waiting for transfers between devices: 62.3 us -> 55.6 us
  Pallas kernels: 111 us -> 116 us
  local copies, waits for them, and re-layouts: 13.6 us -> 10.1 us
    ppermute x14 -> x13, starting transfers between devices: 25.5 us -> 12 us  [send(): return lax.ppermute(value, ('dp', 'seq'), pairs)]
    ppermute x10, waiting for transfers between devices: 15.4 us -> 10.9 us  [along(): return lax.ppermute(value, 'seq', pairs)]
    pallas_call x1 -> x2, Pallas kernels: 2.5 us -> 5.78 us  [sum_whole(): pl.pallas_call(functools.partial(line_kernel, len(after)), grid_spec=pltp...]
    pallas_call x0 -> x1, Pallas kernels: none -> 3.19 us  [join(): pl.pallas_call(functools.partial(join_kernel, bit, len(after)), grid_spec...]
    pallas_call x4 -> x3, Pallas kernels: 17.3 us -> 15 us  [sum_and_cut(): pl.pallas_call(functools.partial(sum_kernel, len(after)), grid_spec=pltpu...]
    ppermute x14 -> x13, waiting for transfers between devices: 46.9 us -> 44.7 us  [send(): return lax.ppermute(value, ('dp', 'seq'), pairs)]
    unnamed x41 -> x51, local copies, waits for them, and re-layouts: 8.85 us -> 7.67 us
  transfers between devices with their start and end apart: 24 -> 23, of which waited for: 8 -> 6; matrix products, arithmetic and copies ran while one was open for 4% -> 2% of each run, Pallas kernels for 38% -> 42%
where the time goes in v2:
time: 232 us; the launch traced here: 230 us
  Pallas kernels  116 us (50%)
  waiting for transfers between devices  55.6 us (24%)
  starting transfers between devices  40 us (17%)
  local copies, waits for them, and re-layouts  10.1 us (4%)
  other arithmetic  7.91 us (3%)
    pallas_call x4, Pallas kernels, attend(): pl.pallas_call(functools.partial(attend_kernel, 1.0 / math.sqrt(HD), len(...  66.5 us
    ppermute x13, waiting for transfers between devices, send(): return lax.ppermute(value, ('dp', 'seq'), pairs)  44.7 us
    ppermute x10, starting transfers between devices, along(): return lax.ppermute(value, 'seq', pairs)  28 us
    pallas_call x2, Pallas kernels, weight_part(): pl.pallas_call(weight_kernel, grid_spec=pltpu.PrefetchScalarGridSpec(num_...  17.5 us
    pallas_call x3, Pallas kernels, sum_and_cut(): pl.pallas_call(functools.partial(sum_kernel, len(after)), grid_spec=pltpu...  15 us
    ppermute x13, starting transfers between devices, send(): return lax.ppermute(value, ('dp', 'seq'), pairs)  12 us
    ppermute x10, waiting for transfers between devices, along(): return lax.ppermute(value, 'seq', pairs)  10.9 us
    unnamed x51, local copies, waits for them, and re-layouts  7.67 us
  transfers between devices with their start and end apart: 23, of which 6 were waited for; matrix products, arithmetic and copies ran while one was open for 2% of the time, Pallas kernels for 42%

profile of v2, /device:TPU:1, one launch (start us, length us, event | category | flops | bytes accessed | tf_op | source)
XLA Modules:
  0.0 230.2 jit_solution(4503715413602106951)
XLA Ops:
  0.7 0.6 copy-done
  2.2 9.0 %shard_map.112 = bf16[4,384,1536]{2,1,0:T(8,128)(2,1)} custom-call(s32[10]{0:T(128)} %concatenate.9.places, bf16[768,1536]{1,0:T(8,128)(2,1)} %bitcast.36, bf16[768,3072]{1,0:T(8,128)(2,1)} %bitcast.26), custom_call_target="tpu_custom_call" | custom-call | flops 3623878656 | bytes 9437184 | tf_op jit(solution)/shard_map/pallas_call | solution.py:38
  11.8 4.6 %collective-permute-start.4 = (bf16[2,384,1536]{2,1,0:T(8,128)(2,1)S(1)}, bf16[2,384,1536]{2,1,0:T(8,128)(2,1)}, u32[]{:S(2)}, u32[]{:S(2)}) collective-permute-start(bf16[2,384,1536]{2,1,0:T(8,128)(2,1)S(1)} %pad_maximum_fusion), channel_id=1, source_target_pairs={{0,1},{1,2},{2,3},{3,4},{4,5},{5,6},{6,7},{8,9},{9,10},{10,11},{11... | collective-permute-start | bytes 7077896 | tf_op jit(solution)/shard_map/ppermute | solution.py:368
  16.4 1.6 pad_maximum_fusion.1
  18.0 1.9 collective-permute-start.5
  19.9 1.4 constant_dynamic-slice_fusion
  21.3 2.0 collective-permute-start
  23.3 1.2 collective-permute-start.1
  24.5 8.5 %shard_map.111 = bf16[4,384,1536]{2,1,0:T(8,128)(2,1)} custom-call(s32[10]{0:T(128)} %concatenate.9.places, bf16[768,1536]{1,0:T(8,128)(2,1)} %bitcast.37, bf16[768,3072]{1,0:T(8,128)(2,1)} %bitcast.27), custom_call_target="tpu_custom_call" | custom-call | flops 3623878656 | bytes 9437184 | tf_op jit(solution)/shard_map/pallas_call | solution.py:38
  33.0 16.4 %collective-permute-done.refs_4_.refs_0_ = bf16[192,3072]{1,0:T(8,128)(2,1)S(1)} collective-permute-done((bf16[192,3072]{1,0:T(8,128)(2,1)S(1)}, bf16[192,3072]{1,0:T(8,128)(2,1)S(1)}, u32[]{:S(2)}, u32[]{:S(2)}) %collective-permute-start) | collective-permute-done | bytes 1179680 | tf_op jit(solution)/shard_map/ppermute | solution.py:358
  49.4 1.8 collective-permute-done.1.refs_5_.refs_0_
  51.2 1.0 copy-done.3
  52.2 6.9 %shard_map.113 = (bf16[768,1536]{1,0:T(8,128)(2,1)}, bf16[768,1536]{1,0:T(8,128)(2,1)}) custom-call(s32[10]{0:T(128)} %concatenate.9.places, bf16[1536,1536]{1,0:T(8,128)(2,1)} %bitcast.15, bf16[1536,1536]{1,0:T(8,128)(2,1)} %bitcast.11.refs_1_.refs_3_, bf16[1536,1536]{1,0:T(8,128)(2,1)} %bitcast.16, bf16[1536,1536]{1,0:T(8,128)(2,1)} %bitcast.11.refs_1_.refs_3_, ...), custom_call_target="tpu_custom_call" | custom-call | flops 2359296 | bytes 14155776 | tf_op jit(solution)/shard_map/pallas_call | solution.py:127
  59.1 1.2 collective-permute-start.17
  60.4 1.4 broadcast_select_fusion
  62.2 1.0 collective-permute-start.7
  63.2 16.5 %shard_map.114 = (bf16[768,1536]{1,0:T(8,128)(2,1)}, bf16[768,1536]{1,0:T(8,128)(2,1)}, bf16[768,1536]{1,0:T(8,128)(2,1)}, bf16[2,384,384]{2,1,0:T(8,128)(2,1)}, bf16[2,384,384]{2,1,0:T(8,128)(2,1)}) custom-call(s32[10]{0:T(128)} %concatenate.9.places, bf16[384,3072]{1,0:T(8,128)(2,1)} %refs_0_.1, bf16[768,3072]{1,0:T(8,128)(2,1)} %bitcast.28, ...), custom_call_target="tpu_custom_call" | custom-call | flops 8606711808 | bytes 14155776 | tf_op jit(solution)/shard_map/pallas_call | solution.py:255
  79.7 20.3 %collective-permute-done.17.refs_1_.refs_3_ = bf16[768,1536]{1,0:T(8,128)(2,1)S(1)} collective-permute-done((bf16[768,1536]{1,0:T(8,128)(2,1)}, bf16[768,1536]{1,0:T(8,128)(2,1)S(1)}, u32[]{:S(2)}, u32[]{:S(2)}) %collective-permute-start.17) | collective-permute-done | bytes 2359328 | tf_op jit(solution)/shard_map/ppermute | solution.py:358
  100.0 1.4 copy-done.2
  101.4 4.4 %shard_map.119 = (bf16[384,1536]{1,0:T(8,128)(2,1)}, bf16[384,1536]{1,0:T(8,128)(2,1)}) custom-call(s32[10]{0:T(128)} %concatenate.9.places, bf16[768,1536]{1,0:T(8,128)(2,1)} %get-tuple-element.55.refs_0_.refs_2_, bf16[768,1536]{1,0:T(8,128)(2,1)} %copy-done.2, bf16[768,1536]{1,0:T(8,128)(2,1)} %get-tuple-element.55.refs_0_.refs_2_, ...), custom_call_target="tpu_custom_call" | custom-call | flops 1179648 | bytes 7077888 | tf_op jit(solution)/shard_map/pallas_call | solution.py:127
  106.0 2.6 %collective-permute-start.6 = (bf16[192,3072]{1,0:T(8,128)(2,1)S(1)}, bf16[192,3072]{1,0:T(8,128)(2,1)S(1)}, u32[]{:S(2)}, u32[]{:S(2)}) collective-permute-start(bf16[192,3072]{1,0:T(8,128)(2,1)S(1)} %copy-done.4), channel_id=1, source_target_pairs={{0,1},{1,0},{2,3},{3,2},{4,5},{5,4},{6,7},{7,6},{8,9},{9,8},{10,11... | collective-permute-start | bytes 3538952 | tf_op jit(solution)/shard_map/ppermute | solution.py:358
  108.7 2.3 %collective-permute-start.10 = (bf16[2,384,384]{2,1,0:T(8,128)(2,1)S(1)}, bf16[2,384,384]{2,1,0:T(8,128)(2,1)S(1)}, u32[]{:S(2)}, u32[]{:S(2)}) collective-permute-start(bf16[2,384,384]{2,1,0:T(8,128)(2,1)S(1)} %copy-done.16), channel_id=1, source_target_pairs={{1,0},{2,1},{3,2},{4,3},{5,4},{6,5},{7,6},{9,8},{10,9},{11,10},{12... | collective-permute-start | bytes 1769480 | tf_op jit(solution)/shard_map/ppermute | solution.py:368
  111.1 3.4 %collective-permute-start.9 = (bf16[2,384,384]{2,1,0:T(8,128)(2,1)}, bf16[2,384,384]{2,1,0:T(8,128)(2,1)S(1)}, u32[]{:S(2)}, u32[]{:S(2)}) collective-permute-start(bf16[2,384,384]{2,1,0:T(8,128)(2,1)} %get-tuple-element.39), channel_id=1, source_target_pairs={{0,1},{1,2},{2,3},{3,4},{4,5},{5,6},{6,7},{8,9},{9,10},{10,11},{11... | collective-permute-start | bytes 1769480 | tf_op jit(solution)/shard_map/ppermute | solution.py:368
  114.5 16.7 %shard_map.115 = (bf16[768,1536]{1,0:T(8,128)(2,1)}, bf16[768,1536]{1,0:T(8,128)(2,1)}, bf16[768,1536]{1,0:T(8,128)(2,1)}, bf16[2,384,384]{2,1,0:T(8,128)(2,1)}, bf16[2,384,384]{2,1,0:T(8,128)(2,1)}) custom-call(s32[10]{0:T(128)} %concatenate.9.places, bf16[192,3072]{1,0:T(8,128)(2,1)} %copy-done.5, ...), custom_call_target="tpu_custom_call", output_to_operand_aliasing={{0}: (11, {}), {1}: (12, {}), {2}: (13, {})} | custom-call | flops 8606711808 | bytes 14155776 | tf_op jit(solution)/shard_map/pallas_call | solution.py:255
  131.2 1.9 collective-permute-start.12
  133.1 3.6 %shard_map.120 = (bf16[192,1536]{1,0:T(8,128)(2,1)}, bf16[192,1536]{1,0:T(8,128)(2,1)}) custom-call(s32[10]{0:T(128)} %concatenate.9.places, bf16[384,1536]{1,0:T(8,128)(2,1)} %get-tuple-element.56.refs_0_.refs_2_, bf16[384,1536]{1,0:T(8,128)(2,1)} %copy-done.7, bf16[384,1536]{1,0:T(8,128)(2,1)} %get-tuple-element.56.refs_0_.refs_2_, ...), custom_call_target="tpu_custom_call" | custom-call | flops 589824 | bytes 3538944 | tf_op jit(solution)/shard_map/pallas_call | solution.py:127
  136.8 3.6 %collective-permute-start.11 = (bf16[2,384,384]{2,1,0:T(8,128)(2,1)S(1)}, bf16[2,384,384]{2,1,0:T(8,128)(2,1)S(1)}, u32[]{:S(2)}, u32[]{:S(2)}) collective-permute-start(bf16[2,384,384]{2,1,0:T(8,128)(2,1)S(1)} %copy-done.24), channel_id=1, source_target_pairs={{0,1},{1,2},{2,3},{3,4},{4,5},{5,6},{6,7},{8,9},{9,10},{10,11},{11... | collective-permute-start | bytes 1769480 | tf_op jit(solution)/shard_map/ppermute | solution.py:368
  140.6 0.7 copy-done.12
  141.5 16.7 %shard_map.116 = (bf16[768,1536]{1,0:T(8,128)(2,1)}, bf16[768,1536]{1,0:T(8,128)(2,1)}, bf16[768,1536]{1,0:T(8,128)(2,1)}, bf16[2,384,384]{2,1,0:T(8,128)(2,1)}, bf16[2,384,384]{2,1,0:T(8,128)(2,1)}) custom-call(s32[10]{0:T(128)} %concatenate.9.places, bf16[192,3072]{1,0:T(8,128)(2,1)} %copy-done.3, ...), custom_call_target="tpu_custom_call", output_to_operand_aliasing={{0}: (11, {}), {1}: (12, {}), {2}: (13, {})} | custom-call | flops 8606711808 | bytes 14155776 | tf_op jit(solution)/shard_map/pallas_call | solution.py:255
  158.2 2.2 collective-permute-start.13
  160.4 2.4 %collective-permute-start.14 = (bf16[2,384,384]{2,1,0:T(8,128)(2,1)}, bf16[2,384,384]{2,1,0:T(8,128)(2,1)S(1)}, u32[]{:S(2)}, u32[]{:S(2)}) collective-permute-start(bf16[2,384,384]{2,1,0:T(8,128)(2,1)} %get-tuple-element.50.refs_0_), channel_id=1, source_target_pairs={{1,0},{2,1},{3,2},{4,3},{5,4},{6,5},{7,6},{9,8},{10,9},{11,10},{12... | collective-permute-start | bytes 1769480 | tf_op jit(solution)/shard_map/ppermute | solution.py:368
  162.8 2.9 %shard_map.121.a_ref = bf16[192,1536]{1,0:T(8,128)(2,1)} custom-call(s32[10]{0:T(128)} %concatenate.9.places, bf16[192,1536]{1,0:T(8,128)(2,1)} %get-tuple-element.58.a_ref, bf16[192,1536]{1,0:T(8,128)(2,1)} %copy-done.20, bf16[2,384,384]{2,1,0:T(8,128)(2,1)} %get-tuple-element.50.refs_0_), custom_call_target="tpu_custom_call" | custom-call | flops 294912 | bytes 1769472 | tf_op jit(solution)/shard_map/pallas_call | solution.py:74
  165.7 2.2 collective-permute-start.20
  167.9 0.8 copy-done.15
  168.9 16.7 %shard_map.117 = (bf16[768,1536]{1,0:T(8,128)(2,1)}, bf16[768,1536]{1,0:T(8,128)(2,1)}, bf16[768,1536]{1,0:T(8,128)(2,1)}, bf16[2,384,384]{2,1,0:T(8,128)(2,1)}, bf16[2,384,384]{2,1,0:T(8,128)(2,1)}) custom-call(s32[10]{0:T(128)} %concatenate.9.places, ...), custom_call_target="tpu_custom_call", output_to_operand_aliasing={{0}: (11, {}), {1}: (12, {}), {2}: (13, {})} | custom-call | flops 8606711808 | bytes 14155776 | tf_op jit(solution)/shard_map/pallas_call | solution.py:255
  185.6 3.7 %collective-permute-start.15 = (bf16[2,384,384]{2,1,0:T(8,128)(2,1)}, bf16[2,384,384]{2,1,0:T(8,128)(2,1)S(1)}, u32[]{:S(2)}, u32[]{:S(2)}) collective-permute-start(bf16[2,384,384]{2,1,0:T(8,128)(2,1)} %get-tuple-element.51), channel_id=1, source_target_pairs={{0,1},{1,2},{2,3},{3,4},{4,5},{5,6},{6,7},{8,9},{9,10},{10,11},{11... | collective-permute-start | bytes 1769480 | tf_op jit(solution)/shard_map/ppermute | solution.py:368
  189.3 1.9 collective-permute-start.16
  191.3 3.6 %collective-permute-done.20.b_ref = bf16[192,1536]{1,0:T(8,128)(2,1)S(1)} collective-permute-done((bf16[192,1536]{1,0:T(8,128)(2,1)}, bf16[192,1536]{1,0:T(8,128)(2,1)S(1)}, u32[]{:S(2)}, u32[]{:S(2)}) %collective-permute-start.20) | collective-permute-done | bytes 589856 | tf_op jit(solution)/shard_map/ppermute | solution.py:358
  194.9 0.8 copy-done.21
  195.7 2.9 %shard_map.122.mine_ref = bf16[192,1536]{1,0:T(8,128)(2,1)} custom-call(s32[10]{0:T(128)} %concatenate.9.places, bf16[192,1536]{1,0:T(8,128)(2,1)} %shard_map.121.a_ref, bf16[192,1536]{1,0:T(8,128)(2,1)} %copy-done.21, bf16[2,384,384]{2,1,0:T(8,128)(2,1)} %get-tuple-element.52.refs_0_, bf16[2,384,384]{2,1,0:T(8,128)(2,1)} %copy-done.8, ...), custom_call_target="tpu_custom_call" | custom-call | flops 294912 | bytes 1769472 | tf_op jit(solution)/shard_map/pallas_call | solution.py:74
  198.8 10.9 %collective-permute-done.16.refs_7_ = bf16[2,384,384]{2,1,0:T(8,128)(2,1)S(1)} collective-permute-done((bf16[2,384,384]{2,1,0:T(8,128)(2,1)}, bf16[2,384,384]{2,1,0:T(8,128)(2,1)S(1)}, u32[]{:S(2)}, u32[]{:S(2)}) %collective-permute-start.16) | collective-permute-done | bytes 589856 | tf_op jit(solution)/shard_map/ppermute | solution.py:368
  209.7 0.9 copy-done.18
  210.6 7.6 %shard_map.118 = (bf16[768,1536]{1,0:T(8,128)(2,1)}, bf16[768,1536]{1,0:T(8,128)(2,1)}) custom-call(s32[10]{0:T(128)} %concatenate.9.places, bf16[768,1536]{1,0:T(8,128)(2,1)} %get-tuple-element.47.dk_ref, bf16[768,1536]{1,0:T(8,128)(2,1)} %get-tuple-element.48.dv_ref, bf16[2,384,384]{2,1,0:T(8,128)(2,1)} %copy-done.13, bf16[2,384,384]{2,1,0:T(8,128)(2,1)} %copy-done.12, ...), custom_call_target="tpu_custom_call" | custom-call | flops 4718592 | bytes 14155776 | tf_op jit(solution)/shard_map/pallas_call | solution.py:316
  218.2 0.8 copy-done.19
  219.0 3.2 %shard_map.123 = bf16[384,1536]{1,0:T(8,128)(2,1)} custom-call(s32[10]{0:T(128)} %concatenate.9.places, bf16[192,1536]{1,0:T(8,128)(2,1)} %shard_map.122.mine_ref, bf16[192,1536]{1,0:T(8,128)(2,1)} %copy-done.19, bf16[768,1536]{1,0:T(8,128)(2,1)} %get-tuple-element.53.refs_0_), custom_call_target="tpu_custom_call" | custom-call | flops 294912 | bytes 2359296 | tf_op jit(solution)/shard_map/pallas_call | solution.py:100
  222.2 0.7 collective-permute-start.22
  222.8 2.7 %collective-permute-done.22 = bf16[384,1536]{1,0:T(8,128)(2,1)S(1)} collective-permute-done((bf16[384,1536]{1,0:T(8,128)(2,1)}, bf16[384,1536]{1,0:T(8,128)(2,1)S(1)}, u32[]{:S(2)}, u32[]{:S(2)}) %collective-permute-start.22) | collective-permute-done | bytes 1179680 | tf_op jit(solution)/shard_map/ppermute | solution.py:358
  225.5 4.7 %fusion = f32[384,3072]{1,0:T(8,128)} fusion(bf16[384,1536]{1,0:T(8,128)(2,1)S(1)} %collective-permute-done.22, bf16[384,1536]{1,0:T(8,128)(2,1)} %shard_map.123, pred[]{:T(512)S(6)} %eq.7), kind=kLoop, calls=%fused_computation.3 | loop fusion | flops 11796480 | bytes 7077889 | tf_op jit(solution)/shard_map/convert_element_type | solution.py:412
  (72 shorter events, 3.1 us)
Async XLA Ops:
  0.6 0.7 copy-start
  2.2 9.1 %copy-start.10 = (bf16[1,768,1536]{2,1,0:T(8,128)(2,1)S(1)}, bf16[1,768,1536]{2,1,0:T(8,128)(2,1)}, u32[]{:S(2)}) copy-start(bf16[1,768,1536]{2,1,0:T(8,128)(2,1)} %param.9) | copy-start | bytes 7077892
  2.2 9.1 %copy-start.11 = (bf16[1,768,1536]{2,1,0:T(8,128)(2,1)S(1)}, bf16[1,768,1536]{2,1,0:T(8,128)(2,1)}, u32[]{:S(2)}) copy-start(bf16[1,768,1536]{2,1,0:T(8,128)(2,1)} %param.10) | copy-start | bytes 7077892
  11.2 39.9 %collective-permute-start.8 = (bf16[4,384,1536]{2,1,0:T(8,128)(2,1)}, bf16[4,384,1536]{2,1,0:T(8,128)(2,1)}, u32[]{:S(2)}, u32[]{:S(2)}) collective-permute-start(bf16[4,384,1536]{2,1,0:T(8,128)(2,1)} %shard_map.112), channel_id=1, source_target_pairs={{0,1},{1,0},{2,3},{3,2},{4,5},{5,4},{6,7},{7,6},{8,9},{9,8},{10,11... | collective-permute-start | bytes 14155784 | tf_op jit(solution)/shard_map/ppermute | solution.py:358
  11.8 39.3 %collective-permute-start.4 = (bf16[2,384,1536]{2,1,0:T(8,128)(2,1)S(1)}, bf16[2,384,1536]{2,1,0:T(8,128)(2,1)}, u32[]{:S(2)}, u32[]{:S(2)}) collective-permute-start(bf16[2,384,1536]{2,1,0:T(8,128)(2,1)S(1)} %pad_maximum_fusion), channel_id=1, source_target_pairs={{0,1},{1,2},{2,3},{3,4},{4,5},{5,6},{6,7},{8,9},{9,10},{10,11},{11... | collective-permute-start | bytes 7077896 | tf_op jit(solution)/shard_map/ppermute | solution.py:368
  18.0 33.1 %collective-permute-start.5 = (bf16[2,384,1536]{2,1,0:T(8,128)(2,1)}, bf16[2,384,1536]{2,1,0:T(8,128)(2,1)}, u32[]{:S(2)}, u32[]{:S(2)}) collective-permute-start(bf16[2,384,1536]{2,1,0:T(8,128)(2,1)} %pad_maximum_fusion.1), channel_id=1, source_target_pairs={{1,0},{2,1},{3,2},{4,3},{5,4},{6,5},{7,6},{9,8},{10,9},{11,10},{12... | collective-permute-start | bytes 7077896 | tf_op jit(solution)/shard_map/ppermute | solution.py:368
  21.3 28.1 %collective-permute-start = (bf16[192,3072]{1,0:T(8,128)(2,1)S(1)}, bf16[192,3072]{1,0:T(8,128)(2,1)S(1)}, u32[]{:S(2)}, u32[]{:S(2)}) collective-permute-start(bf16[192,3072]{1,0:T(8,128)(2,1)S(1)} %constant_dynamic-slice_fusion), channel_id=1, source_target_pairs={{0,8},{1,9},{2,10},{3,11},{4,12},{5,13},{6,14},{7,15},{8,0},{9,1},... | collective-permute-start | bytes 3538952 | tf_op jit(solution)/shard_map/ppermute | solution.py:358
  23.3 27.9 %collective-permute-start.1 = (bf16[192,3072]{1,0:T(8,128)(2,1)S(1)}, bf16[192,3072]{1,0:T(8,128)(2,1)S(1)}, u32[]{:S(2)}, u32[]{:S(2)}) collective-permute-start(bf16[192,3072]{1,0:T(8,128)(2,1)S(1)} %constant_dynamic-slice_fusion), channel_id=1, source_target_pairs={{0,16},{1,17},{2,18},{3,19},{4,20},{5,21},{6,22},{7,23},{8,24},{9,... | collective-permute-start | bytes 3538952 | tf_op jit(solution)/shard_map/ppermute | solution.py:358
  49.4 1.8 copy-start.5
  51.1 1.0 copy-start.3
  59.1 3.0 %copy-start.6 = (bf16[192,3072]{1,0:T(8,128)(2,1)S(1)}, bf16[192,3072]{1,0:T(8,128)(2,1)}, u32[]{:S(2)}) copy-start(bf16[192,3072]{1,0:T(8,128)(2,1)} %copy-done.5) | copy-start | bytes 3538948
  59.1 40.8 %collective-permute-start.17 = (bf16[768,1536]{1,0:T(8,128)(2,1)}, bf16[768,1536]{1,0:T(8,128)(2,1)S(1)}, u32[]{:S(2)}, u32[]{:S(2)}) collective-permute-start(bf16[768,1536]{1,0:T(8,128)(2,1)} %get-tuple-element.32.refs_9_), channel_id=1, source_target_pairs={{0,8},{1,17},{2,10},{3,19},{4,12},{5,21},{6,14},{7,23},{8,0},{9,25... | collective-permute-start | bytes 7077896 | tf_op jit(solution)/shard_map/ppermute | solution.py:358
  61.8 46.9 %collective-permute-start.2 = (bf16[192,3072]{1,0:T(8,128)(2,1)S(1)}, bf16[192,3072]{1,0:T(8,128)(2,1)}, u32[]{:S(2)}, u32[]{:S(2)}) collective-permute-start(bf16[192,3072]{1,0:T(8,128)(2,1)S(1)} %broadcast_select_fusion), channel_id=1, source_target_pairs={{0,16},{1,9},{2,18},{3,11},{4,20},{5,13},{6,22},{7,15},{8,24},{9,1... | collective-permute-start | bytes 3538952 | tf_op jit(solution)/shard_map/ppermute | solution.py:358
  62.2 48.9 %collective-permute-start.7 = (bf16[192,3072]{1,0:T(8,128)(2,1)S(1)}, bf16[192,3072]{1,0:T(8,128)(2,1)}, u32[]{:S(2)}, u32[]{:S(2)}) collective-permute-start(bf16[192,3072]{1,0:T(8,128)(2,1)S(1)} %copy-done.6), channel_id=1, source_target_pairs={{0,1},{1,0},{2,3},{3,2},{4,5},{5,4},{6,7},{7,6},{8,9},{9,8},{10,11... | collective-permute-start | bytes 3538952 | tf_op jit(solution)/shard_map/ppermute | solution.py:358
  100.0 1.4 copy-start.2
  101.4 4.6 %copy-start.4 = (bf16[192,3072]{1,0:T(8,128)(2,1)S(1)}, bf16[192,3072]{1,0:T(8,128)(2,1)}, u32[]{:S(2)}) copy-start(bf16[192,3072]{1,0:T(8,128)(2,1)} %copy-done.3) | copy-start | bytes 3538948
  101.4 7.4 %copy-start.16 = (bf16[2,384,384]{2,1,0:T(8,128)(2,1)S(1)}, bf16[2,384,384]{2,1,0:T(8,128)(2,1)}, u32[]{:S(2)}) copy-start(bf16[2,384,384]{2,1,0:T(8,128)(2,1)} %get-tuple-element.40.refs_4_) | copy-start | bytes 1769476
  105.7 25.4 %collective-permute-start.18 = (bf16[384,1536]{1,0:T(8,128)(2,1)}, bf16[384,1536]{1,0:T(8,128)(2,1)S(1)}, u32[]{:S(2)}, u32[]{:S(2)}) collective-permute-start(bf16[384,1536]{1,0:T(8,128)(2,1)} %get-tuple-element.57), channel_id=1, source_target_pairs={{0,16},{1,9},{2,18},{3,11},{4,20},{5,13},{6,22},{7,15},{8,24},{9,1... | collective-permute-start | bytes 3538952 | tf_op jit(solution)/shard_map/ppermute | solution.py:358
  106.0 30.8 %collective-permute-start.6 = (bf16[192,3072]{1,0:T(8,128)(2,1)S(1)}, bf16[192,3072]{1,0:T(8,128)(2,1)S(1)}, u32[]{:S(2)}, u32[]{:S(2)}) collective-permute-start(bf16[192,3072]{1,0:T(8,128)(2,1)S(1)} %copy-done.4), channel_id=1, source_target_pairs={{0,1},{1,0},{2,3},{3,2},{4,5},{5,4},{6,7},{7,6},{8,9},{9,8},{10,11... | collective-permute-start | bytes 3538952 | tf_op jit(solution)/shard_map/ppermute | solution.py:358
  108.6 57.1 %collective-permute-start.3 = (bf16[192,3072]{1,0:T(8,128)(2,1)}, bf16[192,3072]{1,0:T(8,128)(2,1)S(1)}, u32[]{:S(2)}, u32[]{:S(2)}) collective-permute-start(bf16[192,3072]{1,0:T(8,128)(2,1)} %collective-permute-done.2.refs_0_), channel_id=1, source_target_pairs={{0,1},{1,0},{2,3},{3,2},{4,5},{5,4},{6,7},{7,6},{8,9},{9,8},{10,11... | collective-permute-start | bytes 3538952 | tf_op jit(solution)/shard_map/ppermute | solution.py:358
  108.7 31.7 %collective-permute-start.10 = (bf16[2,384,384]{2,1,0:T(8,128)(2,1)S(1)}, bf16[2,384,384]{2,1,0:T(8,128)(2,1)S(1)}, u32[]{:S(2)}, u32[]{:S(2)}) collective-permute-start(bf16[2,384,384]{2,1,0:T(8,128)(2,1)S(1)} %copy-done.16), channel_id=1, source_target_pairs={{1,0},{2,1},{3,2},{4,3},{5,4},{6,5},{7,6},{9,8},{10,9},{11,10},{12... | collective-permute-start | bytes 1769480 | tf_op jit(solution)/shard_map/ppermute | solution.py:368
  111.1 29.5 %collective-permute-start.9 = (bf16[2,384,384]{2,1,0:T(8,128)(2,1)}, bf16[2,384,384]{2,1,0:T(8,128)(2,1)S(1)}, u32[]{:S(2)}, u32[]{:S(2)}) collective-permute-start(bf16[2,384,384]{2,1,0:T(8,128)(2,1)} %get-tuple-element.39), channel_id=1, source_target_pairs={{0,1},{1,2},{2,3},{3,4},{4,5},{5,6},{6,7},{8,9},{9,10},{10,11},{11... | collective-permute-start | bytes 1769480 | tf_op jit(solution)/shard_map/ppermute | solution.py:368
  131.2 1.9 copy-start.7
  131.2 36.7 %collective-permute-start.12 = (bf16[2,384,384]{2,1,0:T(8,128)(2,1)}, bf16[2,384,384]{2,1,0:T(8,128)(2,1)S(1)}, u32[]{:S(2)}, u32[]{:S(2)}) collective-permute-start(bf16[2,384,384]{2,1,0:T(8,128)(2,1)} %get-tuple-element.45.refs_4_), channel_id=1, source_target_pairs={{1,0},{2,1},{3,2},{4,3},{5,4},{6,5},{7,6},{9,8},{10,9},{11,10},{12... | collective-permute-start | bytes 1769480 | tf_op jit(solution)/shard_map/ppermute | solution.py:368
  133.1 3.7 %copy-start.24 = (bf16[2,384,384]{2,1,0:T(8,128)(2,1)S(1)}, bf16[2,384,384]{2,1,0:T(8,128)(2,1)}, u32[]{:S(2)}) copy-start(bf16[2,384,384]{2,1,0:T(8,128)(2,1)} %get-tuple-element.44) | copy-start | bytes 1769476
  136.8 3.8 %copy-start.23 = (bf16[192,3072]{1,0:T(8,128)(2,1)}, bf16[192,3072]{1,0:T(8,128)(2,1)S(1)}, u32[]{:S(2)}) copy-start(bf16[192,3072]{1,0:T(8,128)(2,1)S(1)} %collective-permute-done.6.refs_1_) | copy-start | bytes 3538948
  136.8 31.1 %collective-permute-start.11 = (bf16[2,384,384]{2,1,0:T(8,128)(2,1)S(1)}, bf16[2,384,384]{2,1,0:T(8,128)(2,1)S(1)}, u32[]{:S(2)}, u32[]{:S(2)}) collective-permute-start(bf16[2,384,384]{2,1,0:T(8,128)(2,1)S(1)} %copy-done.24), channel_id=1, source_target_pairs={{0,1},{1,2},{2,3},{3,4},{4,5},{5,6},{6,7},{8,9},{9,10},{10,11},{11... | collective-permute-start | bytes 1769480 | tf_op jit(solution)/shard_map/ppermute | solution.py:368
  140.5 0.8 copy-start.12
  140.5 19.9 %collective-permute-start.19 = (bf16[192,1536]{1,0:T(8,128)(2,1)}, bf16[192,1536]{1,0:T(8,128)(2,1)S(1)}, u32[]{:S(2)}, u32[]{:S(2)}) collective-permute-start(bf16[192,1536]{1,0:T(8,128)(2,1)} %get-tuple-element.59), channel_id=1, source_target_pairs={{0,2},{1,3},{2,0},{3,1},{4,6},{5,7},{6,4},{7,5},{8,10},{9,11},{10,... | collective-permute-start | bytes 1769480 | tf_op jit(solution)/shard_map/ppermute | solution.py:358
  140.6 1.0 copy-start.13
  158.2 33.1 %collective-permute-start.13 = (bf16[2,384,384]{2,1,0:T(8,128)(2,1)}, bf16[2,384,384]{2,1,0:T(8,128)(2,1)S(1)}, u32[]{:S(2)}, u32[]{:S(2)}) collective-permute-start(bf16[2,384,384]{2,1,0:T(8,128)(2,1)} %get-tuple-element.49), channel_id=1, source_target_pairs={{0,1},{1,2},{2,3},{3,4},{4,5},{5,6},{6,7},{8,9},{9,10},{10,11},{11... | collective-permute-start | bytes 1769480 | tf_op jit(solution)/shard_map/ppermute | solution.py:368
  160.4 2.4 %copy-start.20 = (bf16[192,1536]{1,0:T(8,128)(2,1)}, bf16[192,1536]{1,0:T(8,128)(2,1)S(1)}, u32[]{:S(2)}) copy-start(bf16[192,1536]{1,0:T(8,128)(2,1)S(1)} %collective-permute-done.19.b_ref) | copy-start | bytes 1769476
  160.4 30.9 %collective-permute-start.14 = (bf16[2,384,384]{2,1,0:T(8,128)(2,1)}, bf16[2,384,384]{2,1,0:T(8,128)(2,1)S(1)}, u32[]{:S(2)}, u32[]{:S(2)}) collective-permute-start(bf16[2,384,384]{2,1,0:T(8,128)(2,1)} %get-tuple-element.50.refs_0_), channel_id=1, source_target_pairs={{1,0},{2,1},{3,2},{4,3},{5,4},{6,5},{7,6},{9,8},{10,9},{11,10},{12... | collective-permute-start | bytes 1769480 | tf_op jit(solution)/shard_map/ppermute | solution.py:368
  165.7 2.2 copy-start.22
  165.7 29.2 %collective-permute-start.20 = (bf16[192,1536]{1,0:T(8,128)(2,1)}, bf16[192,1536]{1,0:T(8,128)(2,1)S(1)}, u32[]{:S(2)}, u32[]{:S(2)}) collective-permute-start(bf16[192,1536]{1,0:T(8,128)(2,1)} %shard_map.121.a_ref), channel_id=1, source_target_pairs={{0,4},{1,5},{2,6},{3,7},{4,0},{5,1},{6,2},{7,3},{8,12},{9,13},{10,... | collective-permute-start | bytes 1769480 | tf_op jit(solution)/shard_map/ppermute | solution.py:358
  167.9 0.8 copy-start.15
  167.9 1.0 copy-start.14
  185.6 13.2 %collective-permute-start.15 = (bf16[2,384,384]{2,1,0:T(8,128)(2,1)}, bf16[2,384,384]{2,1,0:T(8,128)(2,1)S(1)}, u32[]{:S(2)}, u32[]{:S(2)}) collective-permute-start(bf16[2,384,384]{2,1,0:T(8,128)(2,1)} %get-tuple-element.51), channel_id=1, source_target_pairs={{0,1},{1,2},{2,3},{3,4},{4,5},{5,6},{6,7},{8,9},{9,10},{10,11},{11... | collective-permute-start | bytes 1769480 | tf_op jit(solution)/shard_map/ppermute | solution.py:368
  189.3 20.4 %collective-permute-start.16 = (bf16[2,384,384]{2,1,0:T(8,128)(2,1)}, bf16[2,384,384]{2,1,0:T(8,128)(2,1)S(1)}, u32[]{:S(2)}, u32[]{:S(2)}) collective-permute-start(bf16[2,384,384]{2,1,0:T(8,128)(2,1)} %get-tuple-element.52.refs_0_), channel_id=1, source_target_pairs={{1,0},{2,1},{3,2},{4,3},{5,4},{6,5},{7,6},{9,8},{10,9},{11,10},{12... | collective-permute-start | bytes 1769480 | tf_op jit(solution)/shard_map/ppermute | solution.py:368
  191.3 3.6 %copy-start.8 = (bf16[2,384,384]{2,1,0:T(8,128)(2,1)}, bf16[2,384,384]{2,1,0:T(8,128)(2,1)S(1)}, u32[]{:S(2)}) copy-start(bf16[2,384,384]{2,1,0:T(8,128)(2,1)S(1)} %collective-permute-done.13.refs_4_.refs_1_) | copy-start | bytes 1769476
  191.3 3.6 %copy-start.9 = (bf16[2,384,384]{2,1,0:T(8,128)(2,1)}, bf16[2,384,384]{2,1,0:T(8,128)(2,1)S(1)}, u32[]{:S(2)}) copy-start(bf16[2,384,384]{2,1,0:T(8,128)(2,1)S(1)} %collective-permute-done.14.refs_5_.refs_2_) | copy-start | bytes 1769476
  194.9 0.8 copy-start.21
  198.6 19.6 %collective-permute-start.21 = (bf16[192,1536]{1,0:T(8,128)(2,1)}, bf16[192,1536]{1,0:T(8,128)(2,1)S(1)}, u32[]{:S(2)}, u32[]{:S(2)}) collective-permute-start(bf16[192,1536]{1,0:T(8,128)(2,1)} %shard_map.122.mine_ref), channel_id=1, source_target_pairs={{0,2},{1,3},{2,0},{3,1},{4,6},{5,7},{6,4},{7,5},{8,10},{9,11},{10,... | collective-permute-start | bytes 1769480 | tf_op jit(solution)/shard_map/ppermute | solution.py:358
  198.8 10.9 %copy-start.17 = (bf16[2,384,384]{2,1,0:T(8,128)(2,1)}, bf16[2,384,384]{2,1,0:T(8,128)(2,1)S(1)}, u32[]{:S(2)}) copy-start(bf16[2,384,384]{2,1,0:T(8,128)(2,1)S(1)} %collective-permute-done.15.refs_6_) | copy-start | bytes 1769476
  209.7 0.9 copy-start.18
  218.2 0.8 copy-start.19
  219.0 11.2 %copy-start.1 = (s32[1,16,3]{1,0,2:T(1,128)S(1)}, s32[1,16,3]{1,0,2:T(1,128)}, u32[]{:S(2)}) copy-start(s32[1,16,3]{1,0,2:T(1,128)} %param.15) | copy-start | bytes 580
  222.2 3.3 %collective-permute-start.22 = (bf16[384,1536]{1,0:T(8,128)(2,1)}, bf16[384,1536]{1,0:T(8,128)(2,1)S(1)}, u32[]{:S(2)}, u32[]{:S(2)}) collective-permute-start(bf16[384,1536]{1,0:T(8,128)(2,1)} %shard_map.123), channel_id=1, source_target_pairs={{0,1},{1,0},{2,3},{3,2},{4,5},{5,4},{6,7},{7,6},{8,9},{9,8},{10,11... | collective-permute-start | bytes 3538952 | tf_op jit(solution)/shard_map/ppermute | solution.py:358

commit v3 on v2

--- a/solution.py
+++ b/solution.py
@@ -19,11 +19,11 @@
     return lax.dot_general(a, b, dims, preferred_element_type=jnp.float32)
 
 
-def weight_kernel(places, out_ref, grad_ref, part_ref):
-    part_ref[0] = mm(out_ref[...], grad_ref[...], TN).astype(part_ref.dtype)
-
-
-def weight_part(places, rows, grads, send):
+def weight_kernel(places, out_ref, grad_ref, *refs):
+    refs[-1][0] = mm(out_ref[...], grad_ref[...], TN).astype(jnp.bfloat16)
+
+
+def weight_part(places, rows, grads, send, after=()):
     tokens, width = rows.shape
     high = width // 4
     wide = grads.shape[1] // 2
@@ -43,6 +43,7 @@
             in_specs=[
                 pl.BlockSpec((tokens, high), out_at),
                 pl.BlockSpec((tokens, wide), lambda p, at: (0, half(at))),
+                *[pl.BlockSpec(memory_space=pl.ANY)] * len(after),
             ],
             out_specs=pl.BlockSpec((1, high, wide), lambda p, at: (p, 0, 0)),
         ),
@@ -53,7 +54,7 @@
             bytes_accessed=tokens * width * 2 + tokens * grads.shape[1] + width * grads.shape[1],
             transcendentals=0,
         ),
-    )(places, rows, grads)
+    )(places, rows, grads, *after)
 
 
 def sum_kernel(count, places, *refs):
@@ -111,6 +112,34 @@
             flops=mine.size, bytes_accessed=8 * mine.size, transcendentals=0
         ),
     )(places, mine, other, *after)
+
+
+def pick_kernel(count, places, x_ref, y_ref, *refs):
+    @pl.when(places[1] == 0)
+    def _():
+        refs[count][...] = x_ref[...]
+
+    @pl.when(places[1] != 0)
+    def _():
+        refs[count][...] = y_ref[...]
+
+
+def pick(places, for_first, for_second, after):
+    whole = pl.BlockSpec(for_first.shape, lambda i, at: (0, 0))
+    return pl.pallas_call(
+        functools.partial(pick_kernel, len(after)),
+        grid_spec=pltpu.PrefetchScalarGridSpec(
+            num_scalar_prefetch=1,
+            grid=(1,),
+            in_specs=[whole, whole] + [pl.BlockSpec(memory_space=pl.ANY)] * len(after),
+            out_specs=whole,
+        ),
+        out_shape=jax.ShapeDtypeStruct(for_first.shape, for_first.dtype),
+        compiler_params=pltpu.CompilerParams(vmem_limit_bytes=VMEM),
+        cost_estimate=pl.CostEstimate(
+            flops=0, bytes_accessed=6 * for_first.size, transcendentals=0
+        ),
+    )(places, for_first, for_second, *after)
 
 
 def sum_and_cut(places, bit, a, b, after=()):
@@ -370,8 +399,7 @@
     if cube:
         half = lax.dynamic_slice_in_dim(out_weight, core * (high // 2), high // 2, 0)
         by_x, by_y = swap(half, 1, 0), swap(half, 2, 0)
-        by_both = swap_by_core(jnp.where(core == 0, by_x, by_y), (2, 1))
-        blocks = [[out_weight]] + [[b, swap(b, 0, 1)] for b in (by_x, by_y, by_both)]
+        blocks = [[out_weight]] + [[b, swap(b, 0, 1)] for b in (by_x, by_y)]
     else:
         gathered = lax.all_gather(out_weight, "dp", axis=0, tiled=True)
         blocks = [[gathered[i * high : (i + 1) * high]] for i in range(steps)]
@@ -392,6 +420,11 @@
 
     results, rims, marks = None, [], []
     for step in range(steps):
+        if cube and step == 1:
+            keep, other = sum_and_cut(places, None, chip_keep, chip_got, marks[0])
+            by_both = swap_by_core(pick(places, by_x, by_y, (other,)), (2, 1))
+        if cube and step == 2:
+            blocks.append([by_both, swap(pick(places, by_both, by_both, marks[1]), 0, 1)])
         after = first_after if step == 0 else rims[2 * step - 4 : 2 * step - 2] if step > 1 else ()
         *results, low_rim, high_rim = attend(
             places, step, heads, blocks[step], grads, query, rows, norm, keys, values, halos, results, after
@@ -401,7 +434,6 @@
     key_grad, value_grad = finish(places, results[1], results[2], rims)
 
     if cube:
-        keep, other = sum_and_cut(places, None, chip_keep, chip_got, marks[0])
         keep, other = sum_and_cut(places, 2, keep, swap_by_core(other, (2, 1)), marks[1])
         pair = sum_whole(places, keep, swap(other, 0, 2), marks[2])
         line = sum_whole(places, pair, swap(pair, 0, 4), (*marks[3], *rims[4:6]))

time: 232 us -> 227 us (0.978)
  waiting for transfers between devices: 55.6 us -> 44.7 us
  Pallas kernels: 116 us -> 122 us
    ppermute x13, waiting for transfers between devices: 44.7 us -> 34.5 us  [send(): return lax.ppermute(value, ('dp', 'seq'), pairs)]
    pallas_call x0 -> x2, Pallas kernels: none -> 7.12 us  [pick(): pl.pallas_call(functools.partial(pick_kernel, len(after)), grid_spec=pltp...]
    unnamed x51 -> x55, local copies, waits for them, and re-layouts: 7.67 us -> 8.66 us
  transfers between devices with their start and end apart: 23 -> 23, of which waited for: 6 -> 6; matrix products, arithmetic and copies ran while one was open for 2% -> 2% of each run, Pallas kernels for 42% -> 46%
where the time goes in v3:
time: 227 us; the launch traced here: 226 us
  Pallas kernels  122 us (54%)
  waiting for transfers between devices  44.7 us (20%)
  starting transfers between devices  40.2 us (18%)
  local copies, waits for them, and re-layouts  11.1 us (5%)
  other arithmetic  6.51 us (3%)
    pallas_call x4, Pallas kernels, attend(): pl.pallas_call(functools.partial(attend_kernel, 1.0 / math.sqrt(HD), len(...  66.5 us
    ppermute x13, waiting for transfers between devices, send(): return lax.ppermute(value, ('dp', 'seq'), pairs)  34.5 us
    ppermute x10, starting transfers between devices, along(): return lax.ppermute(value, 'seq', pairs)  28.2 us
    pallas_call x2, Pallas kernels, weight_part(): pl.pallas_call(weight_kernel, grid_spec=pltpu.PrefetchScalarGridSpec(num_...  17.5 us
    pallas_call x3, Pallas kernels, sum_and_cut(): pl.pallas_call(functools.partial(sum_kernel, len(after)), grid_spec=pltpu...  14.7 us
    ppermute x13, starting transfers between devices, send(): return lax.ppermute(value, ('dp', 'seq'), pairs)  12.1 us
    ppermute x10, waiting for transfers between devices, along(): return lax.ppermute(value, 'seq', pairs)  10.2 us
    unnamed x55, local copies, waits for them, and re-layouts  8.66 us
  transfers between devices with their start and end apart: 23, of which 6 were waited for; matrix products, arithmetic and copies ran while one was open for 2% of the time, Pallas kernels for 46%

profile of v3, /device:TPU:1, one launch (start us, length us, event | category | flops | bytes accessed | tf_op | source)
XLA Modules:
  0.0 225.8 jit_solution(8387169686138798662)
XLA Ops:
  2.2 9.0 %shard_map.112 = bf16[4,384,1536]{2,1,0:T(8,128)(2,1)} custom-call(s32[10]{0:T(128)} %concatenate.9.places, bf16[768,1536]{1,0:T(8,128)(2,1)} %bitcast.32, bf16[768,3072]{1,0:T(8,128)(2,1)} %bitcast.26), custom_call_target="tpu_custom_call" | custom-call | flops 3623878656 | bytes 9437184 | tf_op jit(solution)/shard_map/pallas_call | solution.py:38
  11.8 4.5 %collective-permute-start.3 = (bf16[2,384,1536]{2,1,0:T(8,128)(2,1)S(1)}, bf16[2,384,1536]{2,1,0:T(8,128)(2,1)}, u32[]{:S(2)}, u32[]{:S(2)}) collective-permute-start(bf16[2,384,1536]{2,1,0:T(8,128)(2,1)S(1)} %pad_maximum_fusion), channel_id=1, source_target_pairs={{0,1},{1,2},{2,3},{3,4},{4,5},{5,6},{6,7},{8,9},{9,10},{10,11},{11... | collective-permute-start | bytes 7077896 | tf_op jit(solution)/shard_map/ppermute | solution.py:397
  16.4 1.6 pad_maximum_fusion.1
  18.0 1.9 collective-permute-start.4
  19.9 1.4 constant_dynamic-slice_fusion
  21.3 2.0 collective-permute-start.1
  23.3 1.2 collective-permute-start
  24.5 8.5 %shard_map.111 = bf16[4,384,1536]{2,1,0:T(8,128)(2,1)} custom-call(s32[10]{0:T(128)} %concatenate.9.places, bf16[768,1536]{1,0:T(8,128)(2,1)} %bitcast.33, bf16[768,3072]{1,0:T(8,128)(2,1)} %bitcast.27), custom_call_target="tpu_custom_call" | custom-call | flops 3623878656 | bytes 9437184 | tf_op jit(solution)/shard_map/pallas_call | solution.py:38
  33.0 16.4 %collective-permute-done.1.refs_5_.y_ref.refs_0_ = bf16[192,3072]{1,0:T(8,128)(2,1)S(1)} collective-permute-done((bf16[192,3072]{1,0:T(8,128)(2,1)S(1)}, bf16[192,3072]{1,0:T(8,128)(2,1)S(1)}, u32[]{:S(2)}, u32[]{:S(2)}) %collective-permute-start.1) | collective-permute-done | bytes 1179680 | tf_op jit(solution)/shard_map/ppermute | solution.py:387
  49.4 1.8 collective-permute-done.refs_4_.x_ref.refs_0_
  51.2 1.0 copy-done.5
  52.2 6.9 %shard_map.113 = (bf16[768,1536]{1,0:T(8,128)(2,1)}, bf16[768,1536]{1,0:T(8,128)(2,1)}) custom-call(s32[10]{0:T(128)} %concatenate.9.places, bf16[1536,1536]{1,0:T(8,128)(2,1)} %bitcast.15, bf16[1536,1536]{1,0:T(8,128)(2,1)} %bitcast.7.refs_1_.refs_3_, bf16[1536,1536]{1,0:T(8,128)(2,1)} %bitcast.16, bf16[1536,1536]{1,0:T(8,128)(2,1)} %bitcast.7.refs_1_.refs_3_, ...), custom_call_target="tpu_custom_call" | custom-call | flops 2359296 | bytes 14155776 | tf_op jit(solution)/shard_map/pallas_call | solution.py:156
  59.4 1.8 collective-permute-start.7
  61.1 16.5 %shard_map.114 = (bf16[768,1536]{1,0:T(8,128)(2,1)}, bf16[768,1536]{1,0:T(8,128)(2,1)}, bf16[768,1536]{1,0:T(8,128)(2,1)}, bf16[2,384,384]{2,1,0:T(8,128)(2,1)}, bf16[2,384,384]{2,1,0:T(8,128)(2,1)}) custom-call(s32[10]{0:T(128)} %concatenate.9.places, bf16[384,3072]{1,0:T(8,128)(2,1)} %refs_0_.1, bf16[768,3072]{1,0:T(8,128)(2,1)} %bitcast.28, ...), custom_call_target="tpu_custom_call" | custom-call | flops 8606711808 | bytes 14155776 | tf_op jit(solution)/shard_map/pallas_call | solution.py:284
  77.6 9.7 %collective-permute-done.5.refs_1_.refs_3_ = bf16[768,1536]{1,0:T(8,128)(2,1)S(1)} collective-permute-done((bf16[768,1536]{1,0:T(8,128)(2,1)}, bf16[768,1536]{1,0:T(8,128)(2,1)S(1)}, u32[]{:S(2)}, u32[]{:S(2)}) %collective-permute-start.5) | collective-permute-done | bytes 2359328 | tf_op jit(solution)/shard_map/ppermute | solution.py:387
  87.3 1.4 copy-done.2
  88.7 4.2 %shard_map.115 = (bf16[384,1536]{1,0:T(8,128)(2,1)}, bf16[384,1536]{1,0:T(8,128)(2,1)}) custom-call(s32[10]{0:T(128)} %concatenate.9.places, bf16[768,1536]{1,0:T(8,128)(2,1)} %get-tuple-element.32.refs_0_.refs_2_, bf16[768,1536]{1,0:T(8,128)(2,1)} %copy-done.2, bf16[768,1536]{1,0:T(8,128)(2,1)} %get-tuple-element.32.refs_0_.refs_2_, ...), custom_call_target="tpu_custom_call" | custom-call | flops 1179648 | bytes 7077888 | tf_op jit(solution)/shard_map/pallas_call | solution.py:156
  92.9 3.6 %shard_map.116 = bf16[192,3072]{1,0:T(8,128)(2,1)} custom-call(s32[10]{0:T(128)} %concatenate.9.places, bf16[192,3072]{1,0:T(8,128)(2,1)} %copy-done.5, bf16[192,3072]{1,0:T(8,128)(2,1)} %copy-done.3, bf16[384,1536]{1,0:T(8,128)(2,1)} %get-tuple-element.35.refs_0_), custom_call_target="tpu_custom_call" | custom-call | bytes 3538944 | tf_op jit(solution)/shard_map/pallas_call | solution.py:129
  96.5 1.2 collective-permute-start.6
  98.0 1.9 collective-permute-start.9
  99.9 1.9 collective-permute-start.11
  101.9 3.8 %collective-permute-start.10 = (bf16[2,384,384]{2,1,0:T(8,128)(2,1)}, bf16[2,384,384]{2,1,0:T(8,128)(2,1)S(1)}, u32[]{:S(2)}, u32[]{:S(2)}) collective-permute-start(bf16[2,384,384]{2,1,0:T(8,128)(2,1)} %get-tuple-element.43), channel_id=1, source_target_pairs={{0,1},{1,2},{2,3},{3,4},{4,5},{5,6},{6,7},{8,9},{9,10},{10,11},{11... | collective-permute-start | bytes 1769480 | tf_op jit(solution)/shard_map/ppermute | solution.py:397
  105.7 16.7 %shard_map.117 = (bf16[768,1536]{1,0:T(8,128)(2,1)}, bf16[768,1536]{1,0:T(8,128)(2,1)}, bf16[768,1536]{1,0:T(8,128)(2,1)}, bf16[2,384,384]{2,1,0:T(8,128)(2,1)}, bf16[2,384,384]{2,1,0:T(8,128)(2,1)}) custom-call(s32[10]{0:T(128)} %concatenate.9.places, bf16[192,3072]{1,0:T(8,128)(2,1)} %copy-done.5, ...), custom_call_target="tpu_custom_call", output_to_operand_aliasing={{0}: (11, {}), {1}: (12, {}), {2}: (13, {})} | custom-call | flops 8606711808 | bytes 14155776 | tf_op jit(solution)/shard_map/pallas_call | solution.py:284
  122.4 1.0 copy-done.6
  123.4 3.5 %shard_map.118 = bf16[192,3072]{1,0:T(8,128)(2,1)} custom-call(s32[10]{0:T(128)} %concatenate.9.places, bf16[192,3072]{1,0:T(8,128)(2,1)} %copy-done.6, bf16[192,3072]{1,0:T(8,128)(2,1)} %copy-done.6, bf16[2,384,384]{2,1,0:T(8,128)(2,1)} %get-tuple-element.39.refs_0_.refs_4_), custom_call_target="tpu_custom_call" | custom-call | bytes 3538944 | tf_op jit(solution)/shard_map/pallas_call | solution.py:129
  127.0 2.4 %collective-permute-start.13 = (bf16[2,384,384]{2,1,0:T(8,128)(2,1)S(1)}, bf16[2,384,384]{2,1,0:T(8,128)(2,1)S(1)}, u32[]{:S(2)}, u32[]{:S(2)}) collective-permute-start(bf16[2,384,384]{2,1,0:T(8,128)(2,1)S(1)} %copy-done.8), channel_id=1, source_target_pairs={{1,0},{2,1},{3,2},{4,3},{5,4},{6,5},{7,6},{9,8},{10,9},{11,10},{12... | collective-permute-start | bytes 1769480 | tf_op jit(solution)/shard_map/ppermute | solution.py:397
  129.4 3.6 %shard_map.122 = (bf16[192,1536]{1,0:T(8,128)(2,1)}, bf16[192,1536]{1,0:T(8,128)(2,1)}) custom-call(s32[10]{0:T(128)} %concatenate.9.places, bf16[384,1536]{1,0:T(8,128)(2,1)} %get-tuple-element.57.refs_0_.refs_2_, bf16[384,1536]{1,0:T(8,128)(2,1)} %copy-done.7, bf16[384,1536]{1,0:T(8,128)(2,1)} %get-tuple-element.57.refs_0_.refs_2_, ...), custom_call_target="tpu_custom_call" | custom-call | flops 589824 | bytes 3538944 | tf_op jit(solution)/shard_map/pallas_call | solution.py:156
  133.0 3.2 %collective-permute-start.12 = (bf16[2,384,384]{2,1,0:T(8,128)(2,1)S(1)}, bf16[2,384,384]{2,1,0:T(8,128)(2,1)S(1)}, u32[]{:S(2)}, u32[]{:S(2)}) collective-permute-start(bf16[2,384,384]{2,1,0:T(8,128)(2,1)S(1)} %copy-done.26), channel_id=1, source_target_pairs={{0,1},{1,2},{2,3},{3,4},{4,5},{5,6},{6,7},{8,9},{9,10},{10,11},{11... | collective-permute-start | bytes 1769480 | tf_op jit(solution)/shard_map/ppermute | solution.py:397
  137.8 16.7 %shard_map.119 = (bf16[768,1536]{1,0:T(8,128)(2,1)}, bf16[768,1536]{1,0:T(8,128)(2,1)}, bf16[768,1536]{1,0:T(8,128)(2,1)}, bf16[2,384,384]{2,1,0:T(8,128)(2,1)}, bf16[2,384,384]{2,1,0:T(8,128)(2,1)}) custom-call(s32[10]{0:T(128)} %concatenate.9.places, bf16[192,3072]{1,0:T(8,128)(2,1)} %copy-done.3, ...), custom_call_target="tpu_custom_call", output_to_operand_aliasing={{0}: (11, {}), {1}: (12, {}), {2}: (13, {})} | custom-call | flops 8606711808 | bytes 14155776 | tf_op jit(solution)/shard_map/pallas_call | solution.py:284
  154.4 2.2 collective-permute-start.14
  156.6 2.4 %collective-permute-start.15 = (bf16[2,384,384]{2,1,0:T(8,128)(2,1)}, bf16[2,384,384]{2,1,0:T(8,128)(2,1)S(1)}, u32[]{:S(2)}, u32[]{:S(2)}) collective-permute-start(bf16[2,384,384]{2,1,0:T(8,128)(2,1)} %get-tuple-element.52.refs_0_), channel_id=1, source_target_pairs={{1,0},{2,1},{3,2},{4,3},{5,4},{6,5},{7,6},{9,8},{10,9},{11,10},{12... | collective-permute-start | bytes 1769480 | tf_op jit(solution)/shard_map/ppermute | solution.py:397
  159.1 2.9 %shard_map.123.a_ref = bf16[192,1536]{1,0:T(8,128)(2,1)} custom-call(s32[10]{0:T(128)} %concatenate.9.places, bf16[192,1536]{1,0:T(8,128)(2,1)} %get-tuple-element.58.a_ref, bf16[192,1536]{1,0:T(8,128)(2,1)} %copy-done.22, bf16[2,384,384]{2,1,0:T(8,128)(2,1)} %get-tuple-element.52.refs_0_), custom_call_target="tpu_custom_call" | custom-call | flops 294912 | bytes 1769472 | tf_op jit(solution)/shard_map/pallas_call | solution.py:75
  161.9 1.4 collective-permute-start.20
  163.4 0.8 copy-done.16
  164.6 16.7 %shard_map.120 = (bf16[768,1536]{1,0:T(8,128)(2,1)}, bf16[768,1536]{1,0:T(8,128)(2,1)}, bf16[768,1536]{1,0:T(8,128)(2,1)}, bf16[2,384,384]{2,1,0:T(8,128)(2,1)}, bf16[2,384,384]{2,1,0:T(8,128)(2,1)}) custom-call(s32[10]{0:T(128)} %concatenate.9.places, bf16[192,3072]{1,0:T(8,128)(2,1)} %copy-done.6, ...), custom_call_target="tpu_custom_call", output_to_operand_aliasing={{0}: (11, {}), {1}: (12, {}), {2}: (13, {})} | custom-call | flops 8606711808 | bytes 14155776 | tf_op jit(solution)/shard_map/pallas_call | solution.py:284
  181.3 3.9 %collective-permute-start.16 = (bf16[2,384,384]{2,1,0:T(8,128)(2,1)}, bf16[2,384,384]{2,1,0:T(8,128)(2,1)S(1)}, u32[]{:S(2)}, u32[]{:S(2)}) collective-permute-start(bf16[2,384,384]{2,1,0:T(8,128)(2,1)} %get-tuple-element.53), channel_id=1, source_target_pairs={{0,1},{1,2},{2,3},{3,4},{4,5},{5,6},{6,7},{8,9},{9,10},{10,11},{11... | collective-permute-start | bytes 1769480 | tf_op jit(solution)/shard_map/ppermute | solution.py:397
  185.2 1.9 collective-permute-start.17
  187.2 3.9 %collective-permute-done.20.b_ref = bf16[192,1536]{1,0:T(8,128)(2,1)S(1)} collective-permute-done((bf16[192,1536]{1,0:T(8,128)(2,1)}, bf16[192,1536]{1,0:T(8,128)(2,1)S(1)}, u32[]{:S(2)}, u32[]{:S(2)}) %collective-permute-start.20) | collective-permute-done | bytes 589856 | tf_op jit(solution)/shard_map/ppermute | solution.py:387
  191.1 0.8 copy-done.23
  191.9 2.9 %shard_map.124.mine_ref = bf16[192,1536]{1,0:T(8,128)(2,1)} custom-call(s32[10]{0:T(128)} %concatenate.9.places, bf16[192,1536]{1,0:T(8,128)(2,1)} %shard_map.123.a_ref, bf16[192,1536]{1,0:T(8,128)(2,1)} %copy-done.23, bf16[2,384,384]{2,1,0:T(8,128)(2,1)} %get-tuple-element.54.refs_0_, bf16[2,384,384]{2,1,0:T(8,128)(2,1)} %copy-done.9, ...), custom_call_target="tpu_custom_call" | custom-call | flops 294912 | bytes 1769472 | tf_op jit(solution)/shard_map/pallas_call | solution.py:75
  194.8 10.2 %collective-permute-done.17.refs_7_ = bf16[2,384,384]{2,1,0:T(8,128)(2,1)S(1)} collective-permute-done((bf16[2,384,384]{2,1,0:T(8,128)(2,1)}, bf16[2,384,384]{2,1,0:T(8,128)(2,1)S(1)}, u32[]{:S(2)}, u32[]{:S(2)}) %collective-permute-start.17) | collective-permute-done | bytes 589856 | tf_op jit(solution)/shard_map/ppermute | solution.py:397
  205.0 0.8 copy-done.20
  205.8 7.6 %shard_map.121 = (bf16[768,1536]{1,0:T(8,128)(2,1)}, bf16[768,1536]{1,0:T(8,128)(2,1)}) custom-call(s32[10]{0:T(128)} %concatenate.9.places, bf16[768,1536]{1,0:T(8,128)(2,1)} %get-tuple-element.49.dk_ref, bf16[768,1536]{1,0:T(8,128)(2,1)} %get-tuple-element.50.dv_ref, bf16[2,384,384]{2,1,0:T(8,128)(2,1)} %copy-done.15, bf16[2,384,384]{2,1,0:T(8,128)(2,1)} %copy-done.14, ...), custom_call_target="tpu_custom_call" | custom-call | flops 4718592 | bytes 14155776 | tf_op jit(solution)/shard_map/pallas_call | solution.py:345
  213.4 0.8 copy-done.21
  214.2 3.0 %shard_map.125 = bf16[384,1536]{1,0:T(8,128)(2,1)} custom-call(s32[10]{0:T(128)} %concatenate.9.places, bf16[192,1536]{1,0:T(8,128)(2,1)} %shard_map.124.mine_ref, bf16[192,1536]{1,0:T(8,128)(2,1)} %copy-done.21, bf16[768,1536]{1,0:T(8,128)(2,1)} %get-tuple-element.55.refs_0_), custom_call_target="tpu_custom_call" | custom-call | flops 294912 | bytes 2359296 | tf_op jit(solution)/shard_map/pallas_call | solution.py:101
  217.3 1.2 collective-permute-start.22
  218.4 2.7 %collective-permute-done.22 = bf16[384,1536]{1,0:T(8,128)(2,1)S(1)} collective-permute-done((bf16[384,1536]{1,0:T(8,128)(2,1)}, bf16[384,1536]{1,0:T(8,128)(2,1)S(1)}, u32[]{:S(2)}, u32[]{:S(2)}) %collective-permute-start.22) | collective-permute-done | bytes 1179680 | tf_op jit(solution)/shard_map/ppermute | solution.py:387
  221.1 4.7 %fusion = f32[384,3072]{1,0:T(8,128)} fusion(bf16[384,1536]{1,0:T(8,128)(2,1)S(1)} %collective-permute-done.22, bf16[384,1536]{1,0:T(8,128)(2,1)} %shard_map.125, pred[]{:T(512)S(6)} %eq.6), kind=kLoop, calls=%fused_computation.3 | loop fusion | flops 11796480 | bytes 7077889 | tf_op jit(solution)/shard_map/convert_element_type | solution.py:444
  (77 shorter events, 4.7 us)
Async XLA Ops:
  2.2 9.1 %copy-start.11 = (bf16[1,768,1536]{2,1,0:T(8,128)(2,1)S(1)}, bf16[1,768,1536]{2,1,0:T(8,128)(2,1)}, u32[]{:S(2)}) copy-start(bf16[1,768,1536]{2,1,0:T(8,128)(2,1)} %param.9) | copy-start | bytes 7077892
  2.2 9.1 %copy-start.12 = (bf16[1,768,1536]{2,1,0:T(8,128)(2,1)S(1)}, bf16[1,768,1536]{2,1,0:T(8,128)(2,1)}, u32[]{:S(2)}) copy-start(bf16[1,768,1536]{2,1,0:T(8,128)(2,1)} %param.10) | copy-start | bytes 7077892
  11.2 39.9 %collective-permute-start.2 = (bf16[4,384,1536]{2,1,0:T(8,128)(2,1)}, bf16[4,384,1536]{2,1,0:T(8,128)(2,1)}, u32[]{:S(2)}, u32[]{:S(2)}) collective-permute-start(bf16[4,384,1536]{2,1,0:T(8,128)(2,1)} %shard_map.112), channel_id=1, source_target_pairs={{0,1},{1,0},{2,3},{3,2},{4,5},{5,4},{6,7},{7,6},{8,9},{9,8},{10,11... | collective-permute-start | bytes 14155784 | tf_op jit(solution)/shard_map/ppermute | solution.py:387
  11.8 39.3 %collective-permute-start.3 = (bf16[2,384,1536]{2,1,0:T(8,128)(2,1)S(1)}, bf16[2,384,1536]{2,1,0:T(8,128)(2,1)}, u32[]{:S(2)}, u32[]{:S(2)}) collective-permute-start(bf16[2,384,1536]{2,1,0:T(8,128)(2,1)S(1)} %pad_maximum_fusion), channel_id=1, source_target_pairs={{0,1},{1,2},{2,3},{3,4},{4,5},{5,6},{6,7},{8,9},{9,10},{10,11},{11... | collective-permute-start | bytes 7077896 | tf_op jit(solution)/shard_map/ppermute | solution.py:397
  18.0 33.2 %collective-permute-start.4 = (bf16[2,384,1536]{2,1,0:T(8,128)(2,1)}, bf16[2,384,1536]{2,1,0:T(8,128)(2,1)}, u32[]{:S(2)}, u32[]{:S(2)}) collective-permute-start(bf16[2,384,1536]{2,1,0:T(8,128)(2,1)} %pad_maximum_fusion.1), channel_id=1, source_target_pairs={{1,0},{2,1},{3,2},{4,3},{5,4},{6,5},{7,6},{9,8},{10,9},{11,10},{12... | collective-permute-start | bytes 7077896 | tf_op jit(solution)/shard_map/ppermute | solution.py:397
  21.3 28.1 %collective-permute-start.1 = (bf16[192,3072]{1,0:T(8,128)(2,1)S(1)}, bf16[192,3072]{1,0:T(8,128)(2,1)S(1)}, u32[]{:S(2)}, u32[]{:S(2)}) collective-permute-start(bf16[192,3072]{1,0:T(8,128)(2,1)S(1)} %constant_dynamic-slice_fusion), channel_id=1, source_target_pairs={{0,16},{1,17},{2,18},{3,19},{4,20},{5,21},{6,22},{7,23},{8,24},{9,... | collective-permute-start | bytes 3538952 | tf_op jit(solution)/shard_map/ppermute | solution.py:387
  23.3 27.9 %collective-permute-start = (bf16[192,3072]{1,0:T(8,128)(2,1)S(1)}, bf16[192,3072]{1,0:T(8,128)(2,1)S(1)}, u32[]{:S(2)}, u32[]{:S(2)}) collective-permute-start(bf16[192,3072]{1,0:T(8,128)(2,1)S(1)} %constant_dynamic-slice_fusion), channel_id=1, source_target_pairs={{0,8},{1,9},{2,10},{3,11},{4,12},{5,13},{6,14},{7,15},{8,0},{9,1},... | collective-permute-start | bytes 3538952 | tf_op jit(solution)/shard_map/ppermute | solution.py:387
  49.4 1.8 copy-start.3
  51.2 1.0 copy-start.5
  59.1 28.2 %collective-permute-start.5 = (bf16[768,1536]{1,0:T(8,128)(2,1)}, bf16[768,1536]{1,0:T(8,128)(2,1)S(1)}, u32[]{:S(2)}, u32[]{:S(2)}) collective-permute-start(bf16[768,1536]{1,0:T(8,128)(2,1)} %get-tuple-element.33.refs_9_), channel_id=1, source_target_pairs={{0,8},{1,17},{2,10},{3,19},{4,12},{5,21},{6,14},{7,23},{8,0},{9,25... | collective-permute-start | bytes 7077896 | tf_op jit(solution)/shard_map/ppermute | solution.py:387
  59.4 42.5 %collective-permute-start.7 = (bf16[192,3072]{1,0:T(8,128)(2,1)}, bf16[192,3072]{1,0:T(8,128)(2,1)}, u32[]{:S(2)}, u32[]{:S(2)}) collective-permute-start(bf16[192,3072]{1,0:T(8,128)(2,1)} %copy-done.5), channel_id=1, source_target_pairs={{0,1},{1,0},{2,3},{3,2},{4,5},{5,4},{6,7},{7,6},{8,9},{9,8},{10,11... | collective-permute-start | bytes 3538952 | tf_op jit(solution)/shard_map/ppermute | solution.py:387
  87.3 1.4 copy-start.2
  92.9 4.8 %copy-start.13 = (bf16[384,1536]{1,0:T(8,128)(2,1)S(1)}, bf16[384,1536]{1,0:T(8,128)(2,1)}, u32[]{:S(2)}) copy-start(bf16[384,1536]{1,0:T(8,128)(2,1)} %get-tuple-element.35.refs_0_) | copy-start | bytes 3538948
  92.9 5.1 %copy-start.4 = (bf16[192,3072]{1,0:T(8,128)(2,1)S(1)}, bf16[192,3072]{1,0:T(8,128)(2,1)}, u32[]{:S(2)}) copy-start(bf16[192,3072]{1,0:T(8,128)(2,1)} %copy-done.3) | copy-start | bytes 3538948
  92.9 7.0 %copy-start.18 = (bf16[2,384,384]{2,1,0:T(8,128)(2,1)S(1)}, bf16[2,384,384]{2,1,0:T(8,128)(2,1)}, u32[]{:S(2)}) copy-start(bf16[2,384,384]{2,1,0:T(8,128)(2,1)} %get-tuple-element.34.refs_4_) | copy-start | bytes 1769476
  96.5 25.9 %collective-permute-start.6 = (bf16[192,3072]{1,0:T(8,128)(2,1)}, bf16[192,3072]{1,0:T(8,128)(2,1)S(1)}, u32[]{:S(2)}, u32[]{:S(2)}) collective-permute-start(bf16[192,3072]{1,0:T(8,128)(2,1)} %shard_map.116), channel_id=1, source_target_pairs={{0,16},{1,9},{2,18},{3,11},{4,20},{5,13},{6,22},{7,15},{8,24},{9,1... | collective-permute-start | bytes 3538952 | tf_op jit(solution)/shard_map/ppermute | solution.py:387
  97.7 29.2 %collective-permute-start.18 = (bf16[384,1536]{1,0:T(8,128)(2,1)S(1)}, bf16[384,1536]{1,0:T(8,128)(2,1)S(1)}, u32[]{:S(2)}, u32[]{:S(2)}) collective-permute-start(bf16[384,1536]{1,0:T(8,128)(2,1)S(1)} %copy-done.13), channel_id=1, source_target_pairs={{0,16},{1,9},{2,18},{3,11},{4,20},{5,13},{6,22},{7,15},{8,24},{9,1... | collective-permute-start | bytes 3538952 | tf_op jit(solution)/shard_map/ppermute | solution.py:387
  98.0 35.0 %collective-permute-start.9 = (bf16[192,3072]{1,0:T(8,128)(2,1)S(1)}, bf16[192,3072]{1,0:T(8,128)(2,1)S(1)}, u32[]{:S(2)}, u32[]{:S(2)}) collective-permute-start(bf16[192,3072]{1,0:T(8,128)(2,1)S(1)} %copy-done.4), channel_id=1, source_target_pairs={{0,1},{1,0},{2,3},{3,2},{4,5},{5,4},{6,7},{7,6},{8,9},{9,8},{10,11... | collective-permute-start | bytes 3538952 | tf_op jit(solution)/shard_map/ppermute | solution.py:387
  99.9 37.0 %collective-permute-start.11 = (bf16[2,384,384]{2,1,0:T(8,128)(2,1)S(1)}, bf16[2,384,384]{2,1,0:T(8,128)(2,1)S(1)}, u32[]{:S(2)}, u32[]{:S(2)}) collective-permute-start(bf16[2,384,384]{2,1,0:T(8,128)(2,1)S(1)} %copy-done.18), channel_id=1, source_target_pairs={{1,0},{2,1},{3,2},{4,3},{5,4},{6,5},{7,6},{9,8},{10,9},{11,10},{12... | collective-permute-start | bytes 1769480 | tf_op jit(solution)/shard_map/ppermute | solution.py:397
  101.9 34.3 %collective-permute-start.10 = (bf16[2,384,384]{2,1,0:T(8,128)(2,1)}, bf16[2,384,384]{2,1,0:T(8,128)(2,1)S(1)}, u32[]{:S(2)}, u32[]{:S(2)}) collective-permute-start(bf16[2,384,384]{2,1,0:T(8,128)(2,1)} %get-tuple-element.43), channel_id=1, source_target_pairs={{0,1},{1,2},{2,3},{3,4},{4,5},{5,6},{6,7},{8,9},{9,10},{10,11},{11... | collective-permute-start | bytes 1769480 | tf_op jit(solution)/shard_map/ppermute | solution.py:397
  122.4 4.6 %copy-start.8 = (bf16[2,384,384]{2,1,0:T(8,128)(2,1)S(1)}, bf16[2,384,384]{2,1,0:T(8,128)(2,1)}, u32[]{:S(2)}) copy-start(bf16[2,384,384]{2,1,0:T(8,128)(2,1)} %get-tuple-element.39.refs_0_.refs_4_) | copy-start | bytes 1769476
  122.4 1.0 copy-start.6
  126.9 36.4 %collective-permute-start.8 = (bf16[192,3072]{1,0:T(8,128)(2,1)}, bf16[192,3072]{1,0:T(8,128)(2,1)S(1)}, u32[]{:S(2)}, u32[]{:S(2)}) collective-permute-start(bf16[192,3072]{1,0:T(8,128)(2,1)} %shard_map.118), channel_id=1, source_target_pairs={{0,1},{1,0},{2,3},{3,2},{4,5},{5,4},{6,7},{7,6},{8,9},{9,8},{10,11... | collective-permute-start | bytes 3538952 | tf_op jit(solution)/shard_map/ppermute | solution.py:387
  127.0 2.4 %copy-start.7 = (bf16[384,1536]{1,0:T(8,128)(2,1)}, bf16[384,1536]{1,0:T(8,128)(2,1)S(1)}, u32[]{:S(2)}) copy-start(bf16[384,1536]{1,0:T(8,128)(2,1)S(1)} %collective-permute-done.18.refs_1_.refs_3_) | copy-start | bytes 3538948
  127.0 36.4 %collective-permute-start.13 = (bf16[2,384,384]{2,1,0:T(8,128)(2,1)S(1)}, bf16[2,384,384]{2,1,0:T(8,128)(2,1)S(1)}, u32[]{:S(2)}, u32[]{:S(2)}) collective-permute-start(bf16[2,384,384]{2,1,0:T(8,128)(2,1)S(1)} %copy-done.8), channel_id=1, source_target_pairs={{1,0},{2,1},{3,2},{4,3},{5,4},{6,5},{7,6},{9,8},{10,9},{11,10},{12... | collective-permute-start | bytes 1769480 | tf_op jit(solution)/shard_map/ppermute | solution.py:397
  129.4 3.6 %copy-start.26 = (bf16[2,384,384]{2,1,0:T(8,128)(2,1)S(1)}, bf16[2,384,384]{2,1,0:T(8,128)(2,1)}, u32[]{:S(2)}) copy-start(bf16[2,384,384]{2,1,0:T(8,128)(2,1)} %get-tuple-element.47) | copy-start | bytes 1769476
  133.0 3.9 %copy-start.25 = (bf16[192,3072]{1,0:T(8,128)(2,1)}, bf16[192,3072]{1,0:T(8,128)(2,1)S(1)}, u32[]{:S(2)}) copy-start(bf16[192,3072]{1,0:T(8,128)(2,1)S(1)} %collective-permute-done.9.refs_1_) | copy-start | bytes 3538948
  133.0 28.9 %collective-permute-start.12 = (bf16[2,384,384]{2,1,0:T(8,128)(2,1)S(1)}, bf16[2,384,384]{2,1,0:T(8,128)(2,1)S(1)}, u32[]{:S(2)}, u32[]{:S(2)}) collective-permute-start(bf16[2,384,384]{2,1,0:T(8,128)(2,1)S(1)} %copy-done.26), channel_id=1, source_target_pairs={{0,1},{1,2},{2,3},{3,4},{4,5},{5,6},{6,7},{8,9},{9,10},{10,11},{11... | collective-permute-start | bytes 1769480 | tf_op jit(solution)/shard_map/ppermute | solution.py:397
  136.2 0.8 copy-start.15
  136.2 20.4 %collective-permute-start.19 = (bf16[192,1536]{1,0:T(8,128)(2,1)}, bf16[192,1536]{1,0:T(8,128)(2,1)S(1)}, u32[]{:S(2)}, u32[]{:S(2)}) collective-permute-start(bf16[192,1536]{1,0:T(8,128)(2,1)} %get-tuple-element.59), channel_id=1, source_target_pairs={{0,2},{1,3},{2,0},{3,1},{4,6},{5,7},{6,4},{7,5},{8,10},{9,11},{10,... | collective-permute-start | bytes 1769480 | tf_op jit(solution)/shard_map/ppermute | solution.py:387
  136.9 0.8 copy-start.14
  154.4 32.7 %collective-permute-start.14 = (bf16[2,384,384]{2,1,0:T(8,128)(2,1)}, bf16[2,384,384]{2,1,0:T(8,128)(2,1)S(1)}, u32[]{:S(2)}, u32[]{:S(2)}) collective-permute-start(bf16[2,384,384]{2,1,0:T(8,128)(2,1)} %get-tuple-element.51), channel_id=1, source_target_pairs={{0,1},{1,2},{2,3},{3,4},{4,5},{5,6},{6,7},{8,9},{9,10},{10,11},{11... | collective-permute-start | bytes 1769480 | tf_op jit(solution)/shard_map/ppermute | solution.py:397
  156.6 2.4 %copy-start.22 = (bf16[192,1536]{1,0:T(8,128)(2,1)}, bf16[192,1536]{1,0:T(8,128)(2,1)S(1)}, u32[]{:S(2)}) copy-start(bf16[192,1536]{1,0:T(8,128)(2,1)S(1)} %collective-permute-done.19.b_ref) | copy-start | bytes 1769476
  156.6 30.5 %collective-permute-start.15 = (bf16[2,384,384]{2,1,0:T(8,128)(2,1)}, bf16[2,384,384]{2,1,0:T(8,128)(2,1)S(1)}, u32[]{:S(2)}, u32[]{:S(2)}) collective-permute-start(bf16[2,384,384]{2,1,0:T(8,128)(2,1)} %get-tuple-element.52.refs_0_), channel_id=1, source_target_pairs={{1,0},{2,1},{3,2},{4,3},{5,4},{6,5},{7,6},{9,8},{10,9},{11,10},{12... | collective-permute-start | bytes 1769480 | tf_op jit(solution)/shard_map/ppermute | solution.py:397
  161.9 1.5 copy-start.17
  161.9 29.2 %collective-permute-start.20 = (bf16[192,1536]{1,0:T(8,128)(2,1)}, bf16[192,1536]{1,0:T(8,128)(2,1)S(1)}, u32[]{:S(2)}, u32[]{:S(2)}) collective-permute-start(bf16[192,1536]{1,0:T(8,128)(2,1)} %shard_map.123.a_ref), channel_id=1, source_target_pairs={{0,4},{1,5},{2,6},{3,7},{4,0},{5,1},{6,2},{7,3},{8,12},{9,13},{10,... | collective-permute-start | bytes 1769480 | tf_op jit(solution)/shard_map/ppermute | solution.py:387
  163.4 0.8 copy-start.16
  163.4 1.2 copy-start.24
  181.3 13.5 %collective-permute-start.16 = (bf16[2,384,384]{2,1,0:T(8,128)(2,1)}, bf16[2,384,384]{2,1,0:T(8,128)(2,1)S(1)}, u32[]{:S(2)}, u32[]{:S(2)}) collective-permute-start(bf16[2,384,384]{2,1,0:T(8,128)(2,1)} %get-tuple-element.53), channel_id=1, source_target_pairs={{0,1},{1,2},{2,3},{3,4},{4,5},{5,6},{6,7},{8,9},{9,10},{10,11},{11... | collective-permute-start | bytes 1769480 | tf_op jit(solution)/shard_map/ppermute | solution.py:397
  185.2 19.8 %collective-permute-start.17 = (bf16[2,384,384]{2,1,0:T(8,128)(2,1)}, bf16[2,384,384]{2,1,0:T(8,128)(2,1)S(1)}, u32[]{:S(2)}, u32[]{:S(2)}) collective-permute-start(bf16[2,384,384]{2,1,0:T(8,128)(2,1)} %get-tuple-element.54.refs_0_), channel_id=1, source_target_pairs={{1,0},{2,1},{3,2},{4,3},{5,4},{6,5},{7,6},{9,8},{10,9},{11,10},{12... | collective-permute-start | bytes 1769480 | tf_op jit(solution)/shard_map/ppermute | solution.py:397
  187.1 4.0 %copy-start.9 = (bf16[2,384,384]{2,1,0:T(8,128)(2,1)}, bf16[2,384,384]{2,1,0:T(8,128)(2,1)S(1)}, u32[]{:S(2)}) copy-start(bf16[2,384,384]{2,1,0:T(8,128)(2,1)S(1)} %collective-permute-done.14.refs_4_.refs_1_) | copy-start | bytes 1769476
  187.1 4.0 %copy-start.10 = (bf16[2,384,384]{2,1,0:T(8,128)(2,1)}, bf16[2,384,384]{2,1,0:T(8,128)(2,1)S(1)}, u32[]{:S(2)}) copy-start(bf16[2,384,384]{2,1,0:T(8,128)(2,1)S(1)} %collective-permute-done.15.refs_5_.refs_2_) | copy-start | bytes 1769476
  194.8 18.6 %collective-permute-start.21 = (bf16[192,1536]{1,0:T(8,128)(2,1)}, bf16[192,1536]{1,0:T(8,128)(2,1)S(1)}, u32[]{:S(2)}, u32[]{:S(2)}) collective-permute-start(bf16[192,1536]{1,0:T(8,128)(2,1)} %shard_map.124.mine_ref), channel_id=1, source_target_pairs={{0,2},{1,3},{2,0},{3,1},{4,6},{5,7},{6,4},{7,5},{8,10},{9,11},{10,... | collective-permute-start | bytes 1769480 | tf_op jit(solution)/shard_map/ppermute | solution.py:387
  194.8 10.2 %copy-start.19 = (bf16[2,384,384]{2,1,0:T(8,128)(2,1)}, bf16[2,384,384]{2,1,0:T(8,128)(2,1)S(1)}, u32[]{:S(2)}) copy-start(bf16[2,384,384]{2,1,0:T(8,128)(2,1)S(1)} %collective-permute-done.16.refs_6_) | copy-start | bytes 1769476
  205.0 0.8 copy-start.20
  213.4 0.8 copy-start.21
  217.3 3.9 %collective-permute-start.22 = (bf16[384,1536]{1,0:T(8,128)(2,1)}, bf16[384,1536]{1,0:T(8,128)(2,1)S(1)}, u32[]{:S(2)}, u32[]{:S(2)}) collective-permute-start(bf16[384,1536]{1,0:T(8,128)(2,1)} %shard_map.125), channel_id=1, source_target_pairs={{0,1},{1,0},{2,3},{3,2},{4,5},{5,4},{6,7},{7,6},{8,9},{9,8},{10,11... | collective-permute-start | bytes 3538952 | tf_op jit(solution)/shard_map/ppermute | solution.py:387
  218.4 7.4 %copy-start.1 = (s32[1,16,3]{1,0,2:T(1,128)S(1)}, s32[1,16,3]{1,0,2:T(1,128)}, u32[]{:S(2)}) copy-start(s32[1,16,3]{1,0,2:T(1,128)} %param.15) | copy-start | bytes 580
  (2 other events, 1.5 us)
